TPU v7x, 512 devices: a whole 4x4x16 slice. The times are simulated.
512 devices in a mesh: group: 16 (over y, x), pos: 32 (over z, core).
Axes of the slice: x: 4, y: 4, z: 16, core: 2. Of those that a mesh axis runs over, the one named last changes fastest.
Arguments:
- queries: bfloat16 [65536, 256], P(('group', 'pos')), parts along dimension 0, may hold values from -24 to 24
- hist_keys: bfloat16 [524288, 256], P(('group', 'pos')), parts along dimension 0, may hold values from -24 to 24
- hist_values: bfloat16 [524288, 256], P(('group', 'pos')), parts along dimension 0, may hold values from -6 to 6
- block_dev: int32 [65536, 8], P(('group', 'pos')), parts along dimension 0, may hold values from 0 to 31, all different within a row; in each aligned block of 128 rows (0 to 127, 128 to 255, ...) at most 64 rows name the same one
- block_local: int32 [65536, 8], P(('group', 'pos')), parts along dimension 0, may hold values from 0 to 7
Outputs:
- attended: bfloat16 [65536, 256], P(('group', 'pos')), parts along dimension 0
There are 16 independent parts, one for each index of `group`. A program takes and returns all parts, laid end to end along the dimension named above; each array names one. Nothing has to cross between parts.
Inputs may be any that keep to these rules, and one draw needn't show every extreme that they name: `block_dev`: each candidate names 8 different devices. Among the candidates of one device at most 64 name the same device, and in every draw some device is named by exactly 64 of them.
All inputs are finite; a program needn't handle non-finite values.
Results may differ from a plain program's by a relative error of at most 0.0055.
Values may be sent and summed in bfloat16 or wider, within the bound.
No kernel may reach another device: no remote copies, remote signals or barrier semaphores. Data moves between devices by JAX's collectives and lax.ppermute only.
A program may use at most 64 MiB of HBM per device.

v0:
```python
import jax
import jax.numpy as jnp
from jax import lax
from jax.sharding import PartitionSpec as P

BLK = 128


def attend(rows, local, keys, values):
    count = rows.shape[0]
    width = rows.shape[1]
    positions = keys.shape[0]
    nblocks = positions // BLK
    size = 128
    scale = 1.0 / width**0.5
    block_ids = jnp.arange(nblocks, dtype=jnp.int32)

    def one(args):
        query, index = args
        scores = (
            lax.dot_general(
                query, keys, (((1,), (1,)), ((), ())), preferred_element_type=jnp.float32
            )
            * scale
        )
        scores = scores.reshape(size, nblocks, BLK)
        chosen = index[:, None] == block_ids[None, :]
        block_peak = jnp.max(scores, axis=2)
        peak = jnp.sum(jnp.where(chosen, block_peak, 0.0), axis=1)
        shifted = jnp.where(chosen[:, :, None], scores - peak[:, None, None], -1e30)
        expo = jnp.exp(shifted)
        total = jnp.sum(expo, axis=(1, 2))
        weights = expo.astype(jnp.bfloat16).reshape(size, positions)
        summed = jnp.dot(weights, values, preferred_element_type=jnp.float32)
        return ((summed / total[:, None]).astype(jnp.bfloat16), peak + jnp.log(total))

    outs, lses = lax.map(
        one, (rows.reshape(count // size, size, width), local.reshape(count // size, size))
    )
    return (outs.reshape(count, width), lses.reshape(count))


def combine(partial_value, lse, axis):
    top = jnp.max(lse, axis=axis, keepdims=True)
    mix = jnp.exp(lse - top)
    mix = mix / jnp.sum(mix, axis=axis, keepdims=True)
    return jnp.sum(jnp.expand_dims(mix, -1) * partial_value, axis=axis).astype(jnp.bfloat16)


def body(queries, hist_keys, hist_values, block_dev, block_local):
    devices = lax.axis_size("pos")
    cand_dev, width = queries.shape
    every_query, every_dev, every_local = (
        lax.all_gather(queries, "pos", axis=0, tiled=True),
        lax.all_gather(block_dev, "pos", axis=0, tiled=True),
        lax.all_gather(block_local, "pos", axis=0, tiled=True),
    )
    here = lax.axis_index("pos")
    hit = every_dev == here
    targeted = jnp.any(hit, axis=1)
    local = jnp.sum(jnp.where(hit, every_local, 0), axis=1).astype(jnp.int32)
    outs, lses = attend(every_query, local, hist_keys, hist_values)
    lses = jnp.where(targeted, lses, -1e30)
    send_out = outs.reshape(devices, cand_dev, width)
    send_lse = lses.reshape(devices, cand_dev)
    back_out, back_lse = (
        lax.all_to_all(
            send_out.astype(jnp.float32), "pos", split_axis=0, concat_axis=0, tiled=True
        ),
        lax.all_to_all(send_lse, "pos", split_axis=0, concat_axis=0, tiled=True),
    )
    return combine(back_out, back_lse, 0)


def solution(mesh):
    return jax.shard_map(
        body,
        mesh=mesh,
        in_specs=(
            P(("group", "pos"), None),
            P(("group", "pos"), None),
            P(("group", "pos"), None),
            P(("group", "pos"), None),
            P(("group", "pos"), None),
        ),
        out_specs=P(("group", "pos"), None),
        check_vma=False,
    )
```

profile of v0, /device:TPU:6, one launch (start us, length us, event | category | flops | bytes accessed | tf_op | source)
XLA Modules:
  0.0 438.4 jit_solution(15924864219858615508)
XLA Ops:
  7.3 36.8 %all_gather.9 = s32[4096,8]{0,1:T(8,128)S(1)} all-gather(s32[128,8]{0,1:T(8,128)} %param.10), channel_id=1, replica_groups=mesh['group'=16,'pos'=32] {'pos'}, dimensions={0}, use_global_device_ids=true | all-gather | bytes 135168 | tf_op jit(solution)/shard_map/all_gather | solution.py:55
  44.1 27.7 %all_gather.10 = s32[4096,8]{0,1:T(8,128)S(1)} all-gather(s32[128,8]{0,1:T(8,128)} %param.11), channel_id=1, replica_groups=mesh['group'=16,'pos'=32] {'pos'}, dimensions={0}, use_global_device_ids=true | all-gather | bytes 135168 | tf_op jit(solution)/shard_map/all_gather | solution.py:56
  71.9 13.9 %all-gather.2.cloned.1.call-done = bf16[4096,256]{1,0:T(8,128)(2,1)} async-done(((bf16[128,256]{1,0:T(8,128)(2,1)}), bf16[4096,256]{1,0:T(8,128)(2,1)}) %all-gather.2.cloned.1.call-update) | async-done | bytes 2097168 | tf_op jit(solution)/shard_map/all_gather | solution.py:54
  85.8 125.0 %while.13 = (s32[]{:T(128)}, bf16[32,128,256]{2,1,0:T(8,128)(2,1)S(1)}, f32[32,128]{1,0:T(8,128)S(1)}, s32[32,128]{1,0:T(8,128)S(1)}, bf16[32,128,256]{2,1,0:T(8...) while((s32[]{:T(128)}, ...), condition=%wide.region_6.7_spmd.clone, body=%wide.region_2.6_spmd.clone.sunk | while | flops 135334784 | bytes 4736129 | solution.py:37
  86.1 1.4 convolution_multiply_fusion.2
  97.9 1.4 convolution_multiply_fusion.2
  105.7 1.4 convolution_multiply_fusion.2
  113.5 1.4 convolution_multiply_fusion.2
  121.3 1.4 convolution_multiply_fusion.2
  129.1 1.4 convolution_multiply_fusion.2
  136.9 1.4 convolution_multiply_fusion.2
  144.7 1.4 convolution_multiply_fusion.2
  152.6 1.4 convolution_multiply_fusion.2
  160.4 1.4 convolution_multiply_fusion.2
  168.2 1.4 convolution_multiply_fusion.2
  176.0 1.4 convolution_multiply_fusion.2
  183.8 1.4 convolution_multiply_fusion.2
  191.6 1.4 convolution_multiply_fusion.2
  211.5 8.3 %all-to-all-start = ((f32[32,1,128]{2,1,0:T(1,128)}), f32[32,1,128]{2,1,0:T(1,128)S(1)}, u32[]{:S(2)}, u32[]{:S(2)}) async-start(f32[32,1,128]{2,1,0:T(1,128)} %bitcast.3), calls=%async_computation | async-start | bytes 32768 | tf_op jit(solution)/shard_map/all_to_all | solution.py:70
  219.7 2.5 convert_element_type.13
  222.2 9.9 %all-to-all-done = f32[32,1,128]{2,1,0:T(1,128)S(1)} async-done(((f32[32,1,128]{2,1,0:T(1,128)}), f32[32,1,128]{2,1,0:T(1,128)S(1)}, u32[]{:S(2)}, u32[]{:S(2)}) %all-to-all-start) | async-done | bytes 16416 | tf_op jit(solution)/shard_map/all_to_all | solution.py:70
  232.1 4.9 %all-to-all-start.1 = ((f32[32,128,256]{2,1,0:T(8,128)}), f32[32,128,256]{2,1,0:T(8,128)}, u32[]{:S(2)}, u32[]{:S(2)}) async-start(f32[32,128,256]{2,1,0:T(8,128)} %convert_element_type.13), calls=%async_computation.1 | async-start | bytes 8388608 | tf_op jit(solution)/shard_map/all_to_all | solution.py:67
  237.1 191.2 %all-to-all-done.1 = f32[32,128,256]{2,1,0:T(8,128)} async-done(((f32[32,128,256]{2,1,0:T(8,128)}), f32[32,128,256]{2,1,0:T(8,128)}, u32[]{:S(2)}, u32[]{:S(2)}) %all-to-all-start.1) | async-done | bytes 4194336 | tf_op jit(solution)/shard_map/all_to_all | solution.py:67
  428.3 3.2 multiply_reduce_fusion
  (348 shorter events, 104.8 us)
Async XLA Ops:
  6.5 79.3 %all-gather.2.cloned.1.call-start = ((), (), s32[]{:S(2)}) async-start(), calls=%async_computation.2 | async-start | bytes 2162688 | tf_op jit(solution)/shard_map/all_gather | solution.py:54
  211.5 20.7 %all-to-all-start = ((f32[32,1,128]{2,1,0:T(1,128)}), f32[32,1,128]{2,1,0:T(1,128)S(1)}, u32[]{:S(2)}, u32[]{:S(2)}) async-start(f32[32,1,128]{2,1,0:T(1,128)} %bitcast.3), calls=%async_computation | async-start | bytes 32768 | tf_op jit(solution)/shard_map/all_to_all | solution.py:70
  232.1 196.2 %all-to-all-start.1 = ((f32[32,128,256]{2,1,0:T(8,128)}), f32[32,128,256]{2,1,0:T(8,128)}, u32[]{:S(2)}, u32[]{:S(2)}) async-start(f32[32,128,256]{2,1,0:T(8,128)} %convert_element_type.13), calls=%async_computation.1 | async-start | bytes 8388608 | tf_op jit(solution)/shard_map/all_to_all | solution.py:67
Sparse Core Ops, SparseCore 0:
  9.5 76.3 all-gather.1
where the time goes:
time: 441 us; the launch traced here: 438 us
  waiting for transfers between devices  216 us (49%)
  matrix products  88 us (20%)
  blocking collectives  64.5 us (15%)
  other arithmetic  30.2 us (7%)
  between operations  13.4 us (3%)
  starting transfers between devices  13.1 us (3%)
  local copies, waits for them, and re-layouts  11 us (2%)
    all_to_all x1, waiting for transfers between devices, body(): lax.all_to_all(send_out.astype(jnp.float32), 'pos', split_axis=0, concat_...  191 us
    dot_general x32, matrix products, one(): lax.dot_general(query, keys, (((1,), (1,)), ((), ())), preferred_element_...  44.4 us
    dot_general x32, matrix products, one(): summed = jnp.dot(weights, values, preferred_element_type=jnp.float32)  43.6 us
    all_gather x1, blocking collectives, body(): lax.all_gather(block_dev, 'pos', axis=0, tiled=True)  36.8 us
    all_gather x1, blocking collectives, body(): lax.all_gather(block_local, 'pos', axis=0, tiled=True)  27.7 us
    all_gather x1, waiting for transfers between devices, body(): lax.all_gather(queries, 'pos', axis=0, tiled=True)  13.9 us
    all_to_all x1, waiting for transfers between devices, body(): lax.all_to_all(send_lse, 'pos', split_axis=0, concat_axis=0, tiled=True)  9.9 us
  transfers between devices with their start and end apart: 3, of which 3 were waited for; matrix products, arithmetic and copies ran while one was open for 1% of the time, Pallas kernels for 0%

commit v1 on v0

v1 whole, which is shorter than its diff:
```python
import functools

import jax
import jax.numpy as jnp
from jax import lax
from jax.experimental import pallas as pl
from jax.experimental.pallas import tpu as pltpu
from jax.sharding import Mesh, PartitionSpec as P

BLK = 128
NONE = -1e30


def attend_kernel(nloc, chip_ref, x_ref, k_ref, vt_ref, out_ref):
    cand = out_ref.shape[2]
    width = k_ref.shape[2]
    first = (chip_ref[0] * (2 * nloc)).astype(jnp.float32)
    query = jnp.concatenate([x_ref[0, :cand, :], x_ref[1, :cand, :]], axis=0)
    ids = jnp.concatenate(
        [x_ref[0, cand:, :cand].astype(jnp.float32), x_ref[1, cand:, :cand].astype(jnp.float32)],
        axis=1,
    )
    scale = 1.0 / width**0.5
    parts, lses = [], []
    for half in range(2):
        near = ids - (first + half * nloc)
        inside = jnp.logical_and(near >= 0.0, near < nloc)
        sel = jnp.max(jnp.where(inside, near, -1.0), axis=0, keepdims=True)
        scores = lax.dot_general(
            k_ref[half], query, (((1,), (1,)), ((), ())), preferred_element_type=jnp.float32
        )
        picked = scores[0:BLK]
        for b in range(1, nloc):
            picked = jnp.where(sel == b, scores[b * BLK : (b + 1) * BLK], picked)
        peak = jnp.max(picked, axis=0, keepdims=True)
        expo = jnp.exp((picked - peak) * scale)
        total = jnp.sum(expo, axis=0, keepdims=True)
        spread = jnp.concatenate(
            [jnp.where(sel == b, expo, 0.0).astype(jnp.bfloat16) for b in range(nloc)], axis=0
        )
        summed = jnp.dot(vt_ref[half], spread, preferred_element_type=jnp.float32)
        parts.append((summed / total).astype(jnp.bfloat16).astype(jnp.float32))
        lses.append(jnp.where(sel >= 0.0, peak * scale + jnp.log(total), NONE))
    top = jnp.maximum(lses[0], lses[1])
    mix0, mix1 = jnp.exp(lses[0] - top), jnp.exp(lses[1] - top)
    mixed = mix0 + mix1
    merged = ((mix0 / mixed) * parts[0] + (mix1 / mixed) * parts[1]).astype(jnp.bfloat16)
    lse = top + jnp.log(mixed)
    big = lse.astype(jnp.bfloat16)
    rest = lse - big.astype(jnp.float32)
    mid = rest.astype(jnp.bfloat16)
    low = (rest - mid.astype(jnp.float32)).astype(jnp.bfloat16)
    row = lax.broadcasted_iota(jnp.int32, (16, 2 * cand), 0)
    tail = jnp.where(
        row == 0,
        big.astype(jnp.float32),
        jnp.where(row == 1, mid.astype(jnp.float32), low.astype(jnp.float32)),
    ).astype(jnp.bfloat16)
    for s in range(2):
        out_ref[s, :width, :] = merged[:, s * cand : (s + 1) * cand]
        out_ref[s, width:, :] = tail[:, s * cand : (s + 1) * cand]


def attend(chip, x, keys, vt, cand):
    sources, rows, width = x.shape
    halves, positions, _ = keys.shape
    return pl.pallas_call(
        functools.partial(attend_kernel, positions // BLK),
        grid=(sources // 2,),
        in_specs=[
            pl.BlockSpec(memory_space=pltpu.SMEM),
            pl.BlockSpec((2, rows, width), lambda i: (i, 0, 0)),
            pl.BlockSpec((halves, positions, width), lambda i: (0, 0, 0)),
            pl.BlockSpec((halves, width, positions), lambda i: (0, 0, 0)),
        ],
        out_specs=pl.BlockSpec((2, width + 16, cand), lambda i: (i, 0, 0)),
        out_shape=jax.ShapeDtypeStruct((sources, width + 16, cand), jnp.bfloat16),
        compiler_params=pltpu.CompilerParams(vmem_limit_bytes=40 * 1024 * 1024),
    )(chip, x, keys, vt)


def merge_kernel(x_ref, out_ref):
    sources, rows, cand = x_ref.shape
    width = rows - 16
    lses = []
    for s in range(sources):
        tail = x_ref[s, width:, :].astype(jnp.float32)
        lses.append(tail[0:1] + tail[1:2] + tail[2:3])
    top = functools.reduce(jnp.maximum, lses)
    mixes = [jnp.exp(one - top) for one in lses]
    inverse = 1.0 / functools.reduce(jnp.add, mixes)
    total = jnp.zeros((width, cand), jnp.float32)
    for s in range(sources):
        total = total + (mixes[s] * inverse) * x_ref[s, :width, :].astype(jnp.float32)
    out_ref[...] = total.T.astype(jnp.bfloat16)


def merge(x):
    _, rows, cand = x.shape
    return pl.pallas_call(
        merge_kernel,
        out_shape=jax.ShapeDtypeStruct((cand, rows - 16), jnp.bfloat16),
        compiler_params=pltpu.CompilerParams(vmem_limit_bytes=40 * 1024 * 1024),
    )(x)


def body(queries, hist_keys, hist_values, block_dev, block_local):
    chips = lax.axis_size("z")
    cand, width = queries.shape
    nloc = hist_keys.shape[0] // BLK
    topk = block_dev.shape[1]
    ids = (block_dev * nloc + block_local).astype(jnp.bfloat16).T
    mine = jnp.concatenate([queries, jnp.pad(ids, ((0, 0), (0, width - cand)))], axis=0)
    x = lax.all_to_all(
        jnp.broadcast_to(mine[None], (chips, cand + topk, width)), "z", 0, 0, tiled=True
    )
    core = lax.axis_index("core")
    other_keys = lax.ppermute(hist_keys, "core", [(0, 1), (1, 0)])
    vt = hist_values.T
    other_vt = lax.ppermute(vt, "core", [(0, 1), (1, 0)])
    keys = jnp.where(core == 0, jnp.stack([hist_keys, other_keys]), jnp.stack([other_keys, hist_keys]))
    vts = jnp.where(core == 0, jnp.stack([vt, other_vt]), jnp.stack([other_vt, vt]))
    chip = lax.axis_index("z").astype(jnp.int32).reshape(1)
    sent = attend(chip, x, keys, vts, cand)
    back = lax.all_to_all(sent, "z", 0, 0, tiled=True)
    return merge(back)


def solution(mesh):
    groups, pos = mesh.devices.shape
    chips = Mesh(mesh.devices.reshape(groups, pos // 2, 2), ("group", "z", "core"))
    spec = P(("group", "z", "core"), None)
    return jax.shard_map(
        body, mesh=chips, in_specs=(spec,) * 5, out_specs=spec, check_vma=False
    )
```

time: 441 us -> 150 us (0.34)
  waiting for transfers between devices: 216 us -> 44 us
  matrix products: 88 us -> 0 us
  other arithmetic: 30.2 us -> 4.69 us
  Pallas kernels: 0 us -> 13.9 us
  between operations: 13.4 us -> 0.11 us
  local copies, waits for them, and re-layouts: 11 us -> 2.06 us
  starting transfers between devices: 13.1 us -> 19.7 us
    all_to_all x2 -> x1, waiting for transfers between devices: 201 us -> 44 us  [body(): lax.all_to_all(jnp.broadcast_to(mine[None], (chips, cand + topk, width)),...]
    dot_general x64 -> x0, matrix products: 88 us -> none  [the longest x32 44.4 us: one(): lax.dot_general(query, keys, (((1,), (1,)), ((), ())), preferred_element_...]
    all_to_all x0 -> x1, blocking collectives: none -> 65.4 us  [body(): back = lax.all_to_all(sent, 'z', 0, 0, tiled=True)]
    all_gather x2 -> x0, blocking collectives: 64.5 us -> none  [the longest x1 36.8 us: body(): lax.all_gather(block_dev, 'pos', axis=0, tiled=True)]
    reduce_sum x67 -> x0, other arithmetic: 17.5 us -> none  [the longest x32 8.76 us: one(): total = jnp.sum(expo, axis=(1, 2))]
    pallas_call x0 -> x2, Pallas kernels: none -> 13.9 us  [the longest x1 13 us: attend(): pl.pallas_call(functools.partial(attend_kernel, positions // BLK), grid=(...]
    all_gather x1 -> x0, waiting for transfers between devices: 13.9 us -> none  [body(): lax.all_gather(queries, 'pos', axis=0, tiled=True)]
    reduce_max x33 -> x0, other arithmetic: 6.59 us -> none  [the longest x32 6.53 us: one(): block_peak = jnp.max(scores, axis=2)]
  transfers between devices with their start and end apart: 3 -> 3, of which waited for: 3 -> 1; matrix products, arithmetic and copies ran while one was open for 1% -> 2% of each run, Pallas kernels for 0% -> 0%
where the time goes in v1:
time: 150 us
  blocking collectives  65.4 us (44%)
  waiting for transfers between devices  44 us (29%)
  starting transfers between devices  19.7 us (13%)
  Pallas kernels  13.9 us (9%)
  other arithmetic  4.69 us (3%)
  local copies, waits for them, and re-layouts  2.06 us (1%)
    all_to_all x1, blocking collectives, body(): back = lax.all_to_all(sent, 'z', 0, 0, tiled=True)  65.4 us
    all_to_all x1, waiting for transfers between devices, body(): lax.all_to_all(jnp.broadcast_to(mine[None], (chips, cand + topk, width)),...  44 us
    all_to_all x1, starting transfers between devices, body(): lax.all_to_all(jnp.broadcast_to(mine[None], (chips, cand + topk, width)),...  15.3 us
    pallas_call x1, Pallas kernels, attend(): pl.pallas_call(functools.partial(attend_kernel, positions // BLK), grid=(...  13 us
  transfers between devices with their start and end apart: 3, of which 1 were waited for; matrix products, arithmetic and copies ran while one was open for 2% of the time, Pallas kernels for 0%

profile of v1, /device:TPU:6, one launch (start us, length us, event | category | flops | bytes accessed | tf_op | source)
XLA Modules:
  0.0 149.9 jit_solution(7523248243967451338)
XLA Ops:
  0.0 0.7 fusion.2
  0.7 0.8 fusion.1
  1.6 1.1 broadcast_in_dim.2
  2.6 0.0 copy-start.1
  2.6 0.0 copy-start.3
  2.6 15.3 %all-to-all-start = ((bf16[16,136,256]{2,1,0:T(8,128)(2,1)}), bf16[16,136,256]{2,1,0:T(8,128)(2,1)S(1)}, u32[]{:S(2)}, u32[]{:S(2)}) async-start(bf16[16,136,256]{2,1,0:T(8,128)(2,1)} %broadcast_in_dim.2), calls=%async_computation | async-start | bytes 2228224 | tf_op jit(solution)/shard_map/all_to_all | solution.py:114
  18.0 0.0 copy-done.1
  18.0 1.9 %collective-permute-start = (bf16[1024,256]{1,0:T(8,128)(2,1)S(1)}, bf16[1024,256]{1,0:T(8,128)(2,1)S(1)}, u32[]{:S(2)}, u32[]{:S(2)}) collective-permute-start(bf16[1024,256]{1,0:T(8,128)(2,1)S(1)} %copy-done.1), channel_id=1, source_target_pairs={{0,1},{1,0},{2,3},{3,2},{4,5},{5,4},{6,7},{7,6},{8,9},{9,8},{10,11... | collective-permute-start | bytes 1572872 | tf_op jit(solution)/shard_map/ppermute | solution.py:118
  19.9 0.0 copy-done.3
  19.9 0.2 copy.6
  20.1 0.0 copy-start
  20.1 2.4 %collective-permute-start.1 = (bf16[256,1024]{1,0:T(8,128)(2,1)S(1)}, bf16[256,1024]{1,0:T(8,128)(2,1)}, u32[]{:S(2)}, u32[]{:S(2)}) collective-permute-start(bf16[256,1024]{1,0:T(8,128)(2,1)S(1)} %bitcast.9), channel_id=1, source_target_pairs={{0,1},{1,0},{2,3},{3,2},{4,5},{5,4},{6,7},{7,6},{8,9},{9,8},{10,11... | collective-permute-start | bytes 1572872 | tf_op jit(solution)/shard_map/ppermute | solution.py:120
  22.5 0.0 collective-permute-done
  22.6 0.0 copy-start.2
  22.6 0.8 copy-done.2
  23.4 1.4 maximum_select_fusion.k_ref
  24.8 0.0 collective-permute-done.1
  24.8 0.0 copy-done
  24.8 1.7 %maximum_select_fusion.1.vt_ref = bf16[2,256,1024]{2,1,0:T(8,128)(2,1)S(1)} fusion(bf16[1,256,1024]{2,1,0:T(8,128)(2,1)} %bitcast.6, bf16[1,256,1024]{2,1,0:T(8,128)(2,1)} %bitcast.10, pred[]{:T(512)S(6)} %eq.4), kind=kLoop, calls=%fused_computation.1 | loop fusion | flops 1572864 | bytes 2097153 | tf_op jit(solution)/shard_map/jit(_where)/select_n | solution.py:122
  26.5 44.0 %all-to-all-done.x_ref = bf16[16,136,256]{2,1,0:T(8,128)(2,1)S(1)} async-done(((bf16[16,136,256]{2,1,0:T(8,128)(2,1)}), bf16[16,136,256]{2,1,0:T(8,128)(2,1)S(1)}, u32[]{:S(2)}, u32[]{:S(2)}) %all-to-all-start) | async-done | bytes 1114144 | tf_op jit(solution)/shard_map/all_to_all | solution.py:114
  70.5 13.0 %shard_map.55 = bf16[16,272,128]{2,1,0:T(8,128)(2,1)S(1)} custom-call(s32[1]{0:T(128)} %bitcast.chip_ref, bf16[16,136,256]{2,1,0:T(8,128)(2,1)S(1)} %all-to-all-done.x_ref, bf16[2,1024,256]{2,1,0:T(8,128)(2,1)S(1)} %maximum_select_fusion.k_ref, bf16[2,256,1024]{2,1,0:T(8,128)(2,1)S(1)} %maximum_select_fusion.1.vt_ref), custom_call_target="tpu_custom_call" | custom-call | tf_op jit(solution)/shard_map/pallas_call | solution.py:67
  83.5 65.4 %all_to_all.10.x_ref = bf16[16,272,128]{2,1,0:T(8,128)(2,1)S(1)} all-to-all(bf16[16,272,128]{2,1,0:T(8,128)(2,1)S(1)} %shard_map.55), channel_id=1, replica_groups=mesh['group'=16,'z'=16,'core'=2] {'z'}, dimensions={0} | all-to-all | bytes 2228224 | tf_op jit(solution)/shard_map/all_to_all | solution.py:125
  148.9 1.0 shard_map.56
Async XLA Ops:
  2.6 15.3 %copy-start.1 = (bf16[1024,256]{1,0:T(8,128)(2,1)S(1)}, bf16[1024,256]{1,0:T(8,128)(2,1)}, u32[]{:S(2)}) copy-start(bf16[1024,256]{1,0:T(8,128)(2,1)} %param.6) | copy-start | bytes 1572868
  2.6 17.3 %copy-start.3 = (bf16[1024,256]{1,0:T(8,128)(2,1)S(1)}, bf16[1024,256]{1,0:T(8,128)(2,1)}, u32[]{:S(2)}) copy-start(bf16[1024,256]{1,0:T(8,128)(2,1)} %param.7) | copy-start | bytes 1572868
  2.6 67.9 %all-to-all-start = ((bf16[16,136,256]{2,1,0:T(8,128)(2,1)}), bf16[16,136,256]{2,1,0:T(8,128)(2,1)S(1)}, u32[]{:S(2)}, u32[]{:S(2)}) async-start(bf16[16,136,256]{2,1,0:T(8,128)(2,1)} %broadcast_in_dim.2), calls=%async_computation | async-start | bytes 2228224 | tf_op jit(solution)/shard_map/all_to_all | solution.py:114
  18.0 4.6 %collective-permute-start = (bf16[1024,256]{1,0:T(8,128)(2,1)S(1)}, bf16[1024,256]{1,0:T(8,128)(2,1)S(1)}, u32[]{:S(2)}, u32[]{:S(2)}) collective-permute-start(bf16[1024,256]{1,0:T(8,128)(2,1)S(1)} %copy-done.1), channel_id=1, source_target_pairs={{0,1},{1,0},{2,3},{3,2},{4,5},{5,4},{6,7},{7,6},{8,9},{9,8},{10,11... | collective-permute-start | bytes 1572872 | tf_op jit(solution)/shard_map/ppermute | solution.py:118
  20.1 4.7 %copy-start = (bf16[1024,256]{0,1:T(8,128)(2,1)}, bf16[1024,256]{0,1:T(8,128)(2,1)S(1)}, u32[]{:S(2)}) copy-start(bf16[1024,256]{0,1:T(8,128)(2,1)S(1)} %copy.6) | copy-start | bytes 1572868
  20.1 4.6 %collective-permute-start.1 = (bf16[256,1024]{1,0:T(8,128)(2,1)S(1)}, bf16[256,1024]{1,0:T(8,128)(2,1)}, u32[]{:S(2)}, u32[]{:S(2)}) collective-permute-start(bf16[256,1024]{1,0:T(8,128)(2,1)S(1)} %bitcast.9), channel_id=1, source_target_pairs={{0,1},{1,0},{2,3},{3,2},{4,5},{5,4},{6,7},{7,6},{8,9},{9,8},{10,11... | collective-permute-start | bytes 1572872 | tf_op jit(solution)/shard_map/ppermute | solution.py:120
  22.6 0.8 copy-start.2

commit v2 on v0

v2 whole, which is shorter than its diff:
```python
import functools

import jax
import jax.numpy as jnp
from jax import lax
from jax.experimental import pallas as pl
from jax.experimental.pallas import tpu as pltpu
from jax.sharding import Mesh, PartitionSpec as P

BLK = 128
NONE = -1e30
TAIL = 16
VMEM = pl.BlockSpec(memory_space=pltpu.VMEM)
SMEM = pl.BlockSpec(memory_space=pltpu.SMEM)
PARAMS = pltpu.CompilerParams(vmem_limit_bytes=40 * 1024 * 1024)


def tail_rows(lse):
    big = lse.astype(jnp.bfloat16).astype(jnp.float32)
    rest = lse - big
    mid = rest.astype(jnp.bfloat16).astype(jnp.float32)
    row = lax.broadcasted_iota(jnp.int32, (TAIL, lse.shape[1]), 0)
    return jnp.where(row == 0, big, jnp.where(row == 1, mid, rest - mid)).astype(jnp.bfloat16)


def lse_row(tail):
    tail = tail.astype(jnp.float32)
    return tail[0:1] + tail[1:2] + tail[2:3]


def attend_kernel(first_ref, x_ref, k0_ref, k1_ref, v0_ref, v1_ref, out_ref):
    sources, _, cand = out_ref.shape
    positions, width = k0_ref.shape
    nloc = positions // BLK
    scale = 1.0 / width**0.5
    for s in range(0, sources, 2):
        query = jnp.concatenate([x_ref[s, :cand, :], x_ref[s + 1, :cand, :]], axis=0)
        ids = jnp.concatenate(
            [
                x_ref[s, cand:, :cand].astype(jnp.float32),
                x_ref[s + 1, cand:, :cand].astype(jnp.float32),
            ],
            axis=1,
        )
        parts, lses = [], []
        for half, (k_ref, v_ref) in enumerate(((k0_ref, v0_ref), (k1_ref, v1_ref))):
            near = ids - first_ref[half].astype(jnp.float32)
            inside = jnp.logical_and(near >= 0.0, near < nloc)
            sel = jnp.max(jnp.where(inside, near, -1.0), axis=0, keepdims=True)
            scores = lax.dot_general(
                k_ref[...], query, (((1,), (1,)), ((), ())), preferred_element_type=jnp.float32
            )
            picked = scores[0:BLK]
            for b in range(1, nloc):
                picked = jnp.where(sel == b, scores[b * BLK : (b + 1) * BLK], picked)
            peak = jnp.max(picked, axis=0, keepdims=True)
            expo = jnp.exp((picked - peak) * scale)
            total = jnp.sum(expo, axis=0, keepdims=True)
            spread = jnp.concatenate(
                [jnp.where(sel == b, expo, 0.0).astype(jnp.bfloat16) for b in range(nloc)], axis=0
            )
            summed = jnp.dot(v_ref[...], spread, preferred_element_type=jnp.float32)
            parts.append((summed / total).astype(jnp.bfloat16).astype(jnp.float32))
            lses.append(jnp.where(sel >= 0.0, peak * scale + jnp.log(total), NONE))
        top = jnp.maximum(lses[0], lses[1])
        mix0, mix1 = jnp.exp(lses[0] - top), jnp.exp(lses[1] - top)
        mixed = mix0 + mix1
        merged = ((mix0 / mixed) * parts[0] + (mix1 / mixed) * parts[1]).astype(jnp.bfloat16)
        tail = tail_rows(top + jnp.log(mixed))
        for j in range(2):
            out_ref[s + j, :width, :] = merged[:, j * cand : (j + 1) * cand]
            out_ref[s + j, width:, :] = tail[:, j * cand : (j + 1) * cand]


def attend(first, x, keys, vts, cand):
    sources, _, width = x.shape
    return pl.pallas_call(
        attend_kernel,
        in_specs=[SMEM] + [VMEM] * 5,
        out_specs=VMEM,
        out_shape=jax.ShapeDtypeStruct((sources, width + TAIL, cand), jnp.bfloat16),
        compiler_params=PARAMS,
    )(first, x, *keys, *vts)


def mix(blocks):
    width = blocks[0].shape[0] - TAIL
    lses = [lse_row(one[width:, :]) for one in blocks]
    top = functools.reduce(jnp.maximum, lses)
    mixes = [jnp.exp(one - top) for one in lses]
    mixed = functools.reduce(jnp.add, mixes)
    inverse = 1.0 / mixed
    total = (mixes[0] * inverse) * blocks[0][:width, :].astype(jnp.float32)
    for one, block in zip(mixes[1:], blocks[1:]):
        total = total + (one * inverse) * block[:width, :].astype(jnp.float32)
    return total, top + jnp.log(mixed)


def near_kernel(*refs):
    out_ref = refs[-1]
    sources, rows, _ = out_ref.shape
    for s in range(sources):
        total, lse = mix([ref[s] for ref in refs[:-1]])
        out_ref[s, : rows - TAIL, :] = total.astype(jnp.bfloat16)
        out_ref[s, rows - TAIL :, :] = tail_rows(lse)


def near_merge(*parts):
    return pl.pallas_call(
        near_kernel,
        in_specs=[VMEM] * len(parts),
        out_specs=VMEM,
        out_shape=jax.ShapeDtypeStruct(parts[0].shape, parts[0].dtype),
        compiler_params=PARAMS,
    )(*parts)


def far_kernel(x_ref, out_ref):
    total, _ = mix([x_ref[s] for s in range(x_ref.shape[0])])
    out_ref[...] = total.T.astype(jnp.bfloat16)


def far_merge(x):
    _, rows, cand = x.shape
    return pl.pallas_call(
        far_kernel,
        in_specs=[VMEM],
        out_specs=VMEM,
        out_shape=jax.ShapeDtypeStruct((cand, rows - TAIL), jnp.bfloat16),
        compiler_params=PARAMS,
    )(x)


def body(chips, queries, hist_keys, hist_values, block_dev, block_local):
    cand, width = queries.shape
    nloc = hist_keys.shape[0] // BLK
    topk = block_dev.shape[1]
    stride = 4
    members = chips // stride

    def shift(x, by):
        pairs = [
            (2 * z + c, 2 * ((z + by(c)) % chips) + c) for z in range(chips) for c in range(2)
        ]
        return lax.ppermute(x, ("z", "core"), pairs)

    far = [[2 * (r + stride * j) + c for j in range(members)] for c in range(2) for r in range(stride)]

    def exchange(x):
        return lax.all_to_all(x, ("z", "core"), 0, 0, tiled=True, axis_index_groups=far)

    swap = [(0, 1), (1, 0)]
    ids = (block_dev * nloc + block_local).astype(jnp.bfloat16).T
    mine = jnp.concatenate([queries, jnp.pad(ids, ((0, 0), (0, width - cand)))], axis=0)
    own = exchange(jnp.broadcast_to(mine[None], (members, cand + topk, width)))
    vt = hist_values.T
    keys = (hist_keys, lax.ppermute(hist_keys, "core", swap))
    vts = (vt, lax.ppermute(vt, "core", swap))
    here = 2 * lax.axis_index("z").astype(jnp.int32)
    core = lax.axis_index("core").astype(jnp.int32)
    first = jnp.stack([here + core, here + 1 - core]) * nloc

    steps = (lambda c: 2 - 4 * c, lambda c: 1, lambda c: -1)
    others = [shift(own, by) for by in steps]
    mine_part = attend(first, own, keys, vts, cand)
    back = [
        shift(attend(first, x, keys, vts, cand), lambda c, by=by: -by(c))
        for x, by in zip(others, steps)
    ]
    merged = near_merge(mine_part, *back)
    return far_merge(exchange(merged))


def solution(mesh):
    groups, pos = mesh.devices.shape
    chips = Mesh(mesh.devices.reshape(groups, pos // 2, 2), ("group", "z", "core"))
    spec = P(("group", "z", "core"), None)
    return jax.shard_map(
        functools.partial(body, pos // 2),
        mesh=chips,
        in_specs=(spec,) * 5,
        out_specs=spec,
        check_vma=False,
    )
```

time: 441 us -> 104 us (0.24)
  waiting for transfers between devices: 216 us -> 25.6 us
  matrix products: 88 us -> 0 us
  blocking collectives: 64.5 us -> 23 us
  other arithmetic: 30.2 us -> 1.69 us
  starting transfers between devices: 13.1 us -> 40.4 us
  between operations: 13.4 us -> 0.15 us
  Pallas kernels: 0 us -> 12 us
  local copies, waits for them, and re-layouts: 11 us -> 0.94 us
    all_to_all x2 -> x1, waiting for transfers between devices: 201 us -> 14.2 us  [exchange(): lax.all_to_all(x, ('z', 'core'), 0, 0, tiled=True, axis_index_groups=far)]
    dot_general x64 -> x0, matrix products: 88 us -> none  [the longest x32 44.4 us: one(): lax.dot_general(query, keys, (((1,), (1,)), ((), ())), preferred_element_...]
    all_gather x2 -> x0, blocking collectives: 64.5 us -> none  [the longest x1 36.8 us: body(): lax.all_gather(block_dev, 'pos', axis=0, tiled=True)]
    ppermute x0 -> x8, starting transfers between devices: none -> 25.3 us  [the longest x6 21 us: shift(): return lax.ppermute(x, ('z', 'core'), pairs)]
    all_to_all x0 -> x1, blocking collectives: none -> 23 us  [exchange(): lax.all_to_all(x, ('z', 'core'), 0, 0, tiled=True, axis_index_groups=far)]
    reduce_sum x67 -> x0, other arithmetic: 17.5 us -> none  [the longest x32 8.76 us: one(): total = jnp.sum(expo, axis=(1, 2))]
    all_gather x1 -> x0, waiting for transfers between devices: 13.9 us -> none  [body(): lax.all_gather(queries, 'pos', axis=0, tiled=True)]
    pallas_call x0 -> x6, Pallas kernels: none -> 12 us  [the longest x4 10.9 us: attend(): pl.pallas_call(attend_kernel, in_specs=[SMEM] + [VMEM] * 5, out_specs=VME...]
  transfers between devices with their start and end apart: 3 -> 9, of which waited for: 3 -> 4; matrix products, arithmetic and copies ran while one was open for 1% -> 0% of each run, Pallas kernels for 0% -> 10%
where the time goes in v2:
time: 104 us
  starting transfers between devices  40.4 us (39%)
  waiting for transfers between devices  25.6 us (25%)
  blocking collectives  23 us (22%)
  Pallas kernels  12 us (12%)
  other arithmetic  1.69 us (2%)
    all_to_all x1, blocking collectives, exchange(): lax.all_to_all(x, ('z', 'core'), 0, 0, tiled=True, axis_index_groups=far)  23 us
    ppermute x6, starting transfers between devices, shift(): return lax.ppermute(x, ('z', 'core'), pairs)  21 us
    all_to_all x1, starting transfers between devices, exchange(): lax.all_to_all(x, ('z', 'core'), 0, 0, tiled=True, axis_index_groups=far)  15.1 us
    all_to_all x1, waiting for transfers between devices, exchange(): lax.all_to_all(x, ('z', 'core'), 0, 0, tiled=True, axis_index_groups=far)  14.2 us
    ppermute x6, waiting for transfers between devices, shift(): return lax.ppermute(x, ('z', 'core'), pairs)  11.3 us
    pallas_call x4, Pallas kernels, attend(): pl.pallas_call(attend_kernel, in_specs=[SMEM] + [VMEM] * 5, out_specs=VME...  10.9 us
    ppermute x1, starting transfers between devices, body(): keys = (hist_keys, lax.ppermute(hist_keys, 'core', swap))  2.41 us
  transfers between devices with their start and end apart: 9, of which 4 were waited for; matrix products, arithmetic and copies ran while one was open for 0% of the time, Pallas kernels for 10%

profile of v2, /device:TPU:6, one launch (start us, length us, event | category | flops | bytes accessed | tf_op | source)
XLA Modules:
  0.0 103.7 jit_solution(13790194186783929226)
XLA Ops:
  0.0 0.8 fusion.2
  0.8 0.8 fusion.1
  1.6 0.7 broadcast_in_dim.2
  2.3 15.1 %all-to-all-start = ((bf16[4,136,256]{2,1,0:T(8,128)(2,1)}), bf16[4,136,256]{2,1,0:T(8,128)(2,1)S(1)}, u32[]{:S(2)}, u32[]{:S(2)}) async-start(bf16[4,136,256]{2,1,0:T(8,128)(2,1)} %broadcast_in_dim.2), calls=%async_computation | async-start | bytes 557056 | tf_op jit(solution)/shard_map/all_to_all | solution.py:150
  17.4 0.2 copy.6
  17.6 1.9 %collective-permute-start.1 = (bf16[256,1024]{1,0:T(8,128)(2,1)S(1)}, bf16[256,1024]{1,0:T(8,128)(2,1)S(1)}, u32[]{:S(2)}, u32[]{:S(2)}) collective-permute-start(bf16[256,1024]{1,0:T(8,128)(2,1)S(1)} %bitcast.5), channel_id=1, source_target_pairs={{0,1},{1,0},{2,3},{3,2},{4,5},{5,4},{6,7},{7,6},{8,9},{9,8},{10,11... | collective-permute-start | bytes 1572872 | tf_op jit(solution)/shard_map/ppermute | solution.py:158
  19.6 2.4 %collective-permute-start = (bf16[1024,256]{1,0:T(8,128)(2,1)S(1)}, bf16[1024,256]{1,0:T(8,128)(2,1)S(1)}, u32[]{:S(2)}, u32[]{:S(2)}) collective-permute-start(bf16[1024,256]{1,0:T(8,128)(2,1)S(1)} %copy-done), channel_id=1, source_target_pairs={{0,1},{1,0},{2,3},{3,2},{4,5},{5,4},{6,7},{7,6},{8,9},{9,8},{10,11... | collective-permute-start | bytes 1572872 | tf_op jit(solution)/shard_map/ppermute | solution.py:157
  22.0 14.2 %all-to-all-done.x_ref = bf16[4,136,256]{2,1,0:T(8,128)(2,1)S(1)} async-done(((bf16[4,136,256]{2,1,0:T(8,128)(2,1)}), bf16[4,136,256]{2,1,0:T(8,128)(2,1)S(1)}, u32[]{:S(2)}, u32[]{:S(2)}) %all-to-all-start) | async-done | bytes 278560 | tf_op jit(solution)/shard_map/all_to_all | solution.py:150
  36.2 6.2 %collective-permute-start.2 = (bf16[4,136,256]{2,1,0:T(8,128)(2,1)S(1)}, bf16[4,136,256]{2,1,0:T(8,128)(2,1)S(1)}, u32[]{:S(2)}, u32[]{:S(2)}) collective-permute-start(bf16[4,136,256]{2,1,0:T(8,128)(2,1)S(1)} %all-to-all-done.x_ref), channel_id=1, source_target_pairs={{0,4},{1,29},{2,6},{3,31},{4,8},{5,1},{6,10},{7,3},{8,12},{9,5},{1... | collective-permute-start | bytes 835592 | tf_op jit(solution)/shard_map/ppermute | solution.py:145
  42.4 1.9 %collective-permute-start.4 = (bf16[4,136,256]{2,1,0:T(8,128)(2,1)S(1)}, bf16[4,136,256]{2,1,0:T(8,128)(2,1)S(1)}, u32[]{:S(2)}, u32[]{:S(2)}) collective-permute-start(bf16[4,136,256]{2,1,0:T(8,128)(2,1)S(1)} %all-to-all-done.x_ref), channel_id=1, source_target_pairs={{0,2},{1,3},{2,4},{3,5},{4,6},{5,7},{6,8},{7,9},{8,10},{9,11},{10,... | collective-permute-start | bytes 835592 | tf_op jit(solution)/shard_map/ppermute | solution.py:145
  44.3 5.1 %collective-permute-start.6 = (bf16[4,136,256]{2,1,0:T(8,128)(2,1)S(1)}, bf16[4,136,256]{2,1,0:T(8,128)(2,1)S(1)}, u32[]{:S(2)}, u32[]{:S(2)}) collective-permute-start(bf16[4,136,256]{2,1,0:T(8,128)(2,1)S(1)} %all-to-all-done.x_ref), channel_id=1, source_target_pairs={{0,30},{1,31},{2,0},{3,1},{4,2},{5,3},{6,4},{7,5},{8,6},{9,7},{10,... | collective-permute-start | bytes 835592 | tf_op jit(solution)/shard_map/ppermute | solution.py:145
  49.6 1.6 %collective-permute-done.2.x_ref = bf16[4,136,256]{2,1,0:T(8,128)(2,1)S(1)} collective-permute-done((bf16[4,136,256]{2,1,0:T(8,128)(2,1)S(1)}, bf16[4,136,256]{2,1,0:T(8,128)(2,1)S(1)}, u32[]{:S(2)}, u32[]{:S(2)}) %collective-permute-start.2) | collective-permute-done | bytes 278560 | tf_op jit(solution)/shard_map/ppermute | solution.py:145
  51.1 2.7 %shard_map.56 = bf16[4,272,128]{2,1,0:T(8,128)(2,1)S(1)} custom-call(s32[2]{0:T(128)S(1)} %add_multiply_fusion.first_ref, bf16[4,136,256]{2,1,0:T(8,128)(2,1)S(1)} %collective-permute-done.2.x_ref, bf16[1024,256]{1,0:T(8,128)(2,1)S(1)} %copy-done, bf16[1024,256]{1,0:T(8,128)(2,1)S(1)} %collective-permute-done.k1_ref, bf16[256,1024]{1,0:T(8,128)(2,1)S(1)} %bitcast.6, ...), custom_call_target="tpu_custom_call" | custom-call | tf_op jit(solution)/shard_map/pallas_call | solution.py:77
  53.8 1.9 %collective-permute-start.3 = (bf16[4,272,128]{2,1,0:T(8,128)(2,1)S(1)}, bf16[4,272,128]{2,1,0:T(8,128)(2,1)S(1)}, u32[]{:S(2)}, u32[]{:S(2)}) collective-permute-start(bf16[4,272,128]{2,1,0:T(8,128)(2,1)S(1)} %shard_map.56), channel_id=1, source_target_pairs={{0,28},{1,5},{2,30},{3,7},{4,0},{5,9},{6,2},{7,11},{8,4},{9,13},{1... | collective-permute-start | bytes 835592 | tf_op jit(solution)/shard_map/ppermute | solution.py:145
  55.8 6.8 %collective-permute-done.4.x_ref = bf16[4,136,256]{2,1,0:T(8,128)(2,1)S(1)} collective-permute-done((bf16[4,136,256]{2,1,0:T(8,128)(2,1)S(1)}, bf16[4,136,256]{2,1,0:T(8,128)(2,1)S(1)}, u32[]{:S(2)}, u32[]{:S(2)}) %collective-permute-start.4) | collective-permute-done | bytes 278560 | tf_op jit(solution)/shard_map/ppermute | solution.py:145
  62.6 2.7 %shard_map.57 = bf16[4,272,128]{2,1,0:T(8,128)(2,1)S(1)} custom-call(s32[2]{0:T(128)S(1)} %add_multiply_fusion.first_ref, bf16[4,136,256]{2,1,0:T(8,128)(2,1)S(1)} %collective-permute-done.4.x_ref, bf16[1024,256]{1,0:T(8,128)(2,1)S(1)} %copy-done, bf16[1024,256]{1,0:T(8,128)(2,1)S(1)} %collective-permute-done.k1_ref, bf16[256,1024]{1,0:T(8,128)(2,1)S(1)} %bitcast.7, ...), custom_call_target="tpu_custom_call" | custom-call | tf_op jit(solution)/shard_map/pallas_call | solution.py:77
  65.3 1.9 %collective-permute-start.5 = (bf16[4,272,128]{2,1,0:T(8,128)(2,1)S(1)}, bf16[4,272,128]{2,1,0:T(8,128)(2,1)S(1)}, u32[]{:S(2)}, u32[]{:S(2)}) collective-permute-start(bf16[4,272,128]{2,1,0:T(8,128)(2,1)S(1)} %shard_map.57), channel_id=1, source_target_pairs={{0,30},{1,31},{2,0},{3,1},{4,2},{5,3},{6,4},{7,5},{8,6},{9,7},{10,... | collective-permute-start | bytes 835592 | tf_op jit(solution)/shard_map/ppermute | solution.py:145
  67.2 2.7 %shard_map.58 = bf16[4,272,128]{2,1,0:T(8,128)(2,1)S(1)} custom-call(s32[2]{0:T(128)S(1)} %add_multiply_fusion.first_ref, bf16[4,136,256]{2,1,0:T(8,128)(2,1)S(1)} %collective-permute-done.6.x_ref, bf16[1024,256]{1,0:T(8,128)(2,1)S(1)} %copy-done, bf16[1024,256]{1,0:T(8,128)(2,1)S(1)} %collective-permute-done.k1_ref, bf16[256,1024]{1,0:T(8,128)(2,1)S(1)} %bitcast.8, ...), custom_call_target="tpu_custom_call" | custom-call | tf_op jit(solution)/shard_map/pallas_call | solution.py:77
  70.0 3.9 %collective-permute-start.7 = (bf16[4,272,128]{2,1,0:T(8,128)(2,1)S(1)}, bf16[4,272,128]{2,1,0:T(8,128)(2,1)S(1)}, u32[]{:S(2)}, u32[]{:S(2)}) collective-permute-start(bf16[4,272,128]{2,1,0:T(8,128)(2,1)S(1)} %shard_map.58), channel_id=1, source_target_pairs={{0,2},{1,3},{2,4},{3,5},{4,6},{5,7},{6,8},{7,9},{8,10},{9,11},{10,... | collective-permute-start | bytes 835592 | tf_op jit(solution)/shard_map/ppermute | solution.py:145
  73.9 2.7 %shard_map.55.refs_0_ = bf16[4,272,128]{2,1,0:T(8,128)(2,1)S(1)} custom-call(s32[2]{0:T(128)S(1)} %add_multiply_fusion.first_ref, bf16[4,136,256]{2,1,0:T(8,128)(2,1)S(1)} %all-to-all-done.x_ref, bf16[1024,256]{1,0:T(8,128)(2,1)S(1)} %copy-done, bf16[1024,256]{1,0:T(8,128)(2,1)S(1)} %collective-permute-done.k1_ref, bf16[256,1024]{1,0:T(8,128)(2,1)S(1)} %bitcast.9, ...), custom_call_target="tpu_custom_call" | custom-call | tf_op jit(solution)/shard_map/pallas_call | solution.py:77
  76.6 3.0 %collective-permute-done.7.refs_3_ = bf16[4,272,128]{2,1,0:T(8,128)(2,1)S(1)} collective-permute-done((bf16[4,272,128]{2,1,0:T(8,128)(2,1)S(1)}, bf16[4,272,128]{2,1,0:T(8,128)(2,1)S(1)}, u32[]{:S(2)}, u32[]{:S(2)}) %collective-permute-start.7) | collective-permute-done | bytes 278560 | tf_op jit(solution)/shard_map/ppermute | solution.py:145
  79.6 0.3 shard_map.59
  79.9 23.0 %all_to_all.10.x_ref = bf16[4,272,128]{2,1,0:T(8,128)(2,1)S(1)} all-to-all(bf16[4,272,128]{2,1,0:T(8,128)(2,1)S(1)} %shard_map.59), channel_id=1, replica_groups={{0,8,16,24},{2,10,18,26},{4,12,20,28},{6,14,22,30},{1,9,17,25},{3,11,19..., dimensions={0} | all-to-all | bytes 557056 | tf_op jit(solution)/shard_map/all_to_all | solution.py:150
  102.9 0.8 shard_map.60
  (10 shorter events, 0.1 us)
Async XLA Ops:
  0.0 17.4 %copy-start.1 = (bf16[1024,256]{1,0:T(8,128)(2,1)S(1)}, bf16[1024,256]{1,0:T(8,128)(2,1)}, u32[]{:S(2)}) copy-start(bf16[1024,256]{1,0:T(8,128)(2,1)} %param.7) | copy-start | bytes 1572868
  2.3 33.9 %all-to-all-start = ((bf16[4,136,256]{2,1,0:T(8,128)(2,1)}), bf16[4,136,256]{2,1,0:T(8,128)(2,1)S(1)}, u32[]{:S(2)}, u32[]{:S(2)}) async-start(bf16[4,136,256]{2,1,0:T(8,128)(2,1)} %broadcast_in_dim.2), calls=%async_computation | async-start | bytes 557056 | tf_op jit(solution)/shard_map/all_to_all | solution.py:150
  17.4 2.1 %copy-start = (bf16[1024,256]{1,0:T(8,128)(2,1)S(1)}, bf16[1024,256]{1,0:T(8,128)(2,1)}, u32[]{:S(2)}) copy-start(bf16[1024,256]{1,0:T(8,128)(2,1)} %k0_ref.7) | copy-start | bytes 1572868
  17.6 31.9 %collective-permute-start.1 = (bf16[256,1024]{1,0:T(8,128)(2,1)S(1)}, bf16[256,1024]{1,0:T(8,128)(2,1)S(1)}, u32[]{:S(2)}, u32[]{:S(2)}) collective-permute-start(bf16[256,1024]{1,0:T(8,128)(2,1)S(1)} %bitcast.5), channel_id=1, source_target_pairs={{0,1},{1,0},{2,3},{3,2},{4,5},{5,4},{6,7},{7,6},{8,9},{9,8},{10,11... | collective-permute-start | bytes 1572872 | tf_op jit(solution)/shard_map/ppermute | solution.py:158
  19.6 30.0 %collective-permute-start = (bf16[1024,256]{1,0:T(8,128)(2,1)S(1)}, bf16[1024,256]{1,0:T(8,128)(2,1)S(1)}, u32[]{:S(2)}, u32[]{:S(2)}) collective-permute-start(bf16[1024,256]{1,0:T(8,128)(2,1)S(1)} %copy-done), channel_id=1, source_target_pairs={{0,1},{1,0},{2,3},{3,2},{4,5},{5,4},{6,7},{7,6},{8,9},{9,8},{10,11... | collective-permute-start | bytes 1572872 | tf_op jit(solution)/shard_map/ppermute | solution.py:157
  36.2 14.9 %collective-permute-start.2 = (bf16[4,136,256]{2,1,0:T(8,128)(2,1)S(1)}, bf16[4,136,256]{2,1,0:T(8,128)(2,1)S(1)}, u32[]{:S(2)}, u32[]{:S(2)}) collective-permute-start(bf16[4,136,256]{2,1,0:T(8,128)(2,1)S(1)} %all-to-all-done.x_ref), channel_id=1, source_target_pairs={{0,4},{1,29},{2,6},{3,31},{4,8},{5,1},{6,10},{7,3},{8,12},{9,5},{1... | collective-permute-start | bytes 835592 | tf_op jit(solution)/shard_map/ppermute | solution.py:145
  42.4 20.2 %collective-permute-start.4 = (bf16[4,136,256]{2,1,0:T(8,128)(2,1)S(1)}, bf16[4,136,256]{2,1,0:T(8,128)(2,1)S(1)}, u32[]{:S(2)}, u32[]{:S(2)}) collective-permute-start(bf16[4,136,256]{2,1,0:T(8,128)(2,1)S(1)} %all-to-all-done.x_ref), channel_id=1, source_target_pairs={{0,2},{1,3},{2,4},{3,5},{4,6},{5,7},{6,8},{7,9},{8,10},{9,11},{10,... | collective-permute-start | bytes 835592 | tf_op jit(solution)/shard_map/ppermute | solution.py:145
  44.3 22.9 %collective-permute-start.6 = (bf16[4,136,256]{2,1,0:T(8,128)(2,1)S(1)}, bf16[4,136,256]{2,1,0:T(8,128)(2,1)S(1)}, u32[]{:S(2)}, u32[]{:S(2)}) collective-permute-start(bf16[4,136,256]{2,1,0:T(8,128)(2,1)S(1)} %all-to-all-done.x_ref), channel_id=1, source_target_pairs={{0,30},{1,31},{2,0},{3,1},{4,2},{5,3},{6,4},{7,5},{8,6},{9,7},{10,... | collective-permute-start | bytes 835592 | tf_op jit(solution)/shard_map/ppermute | solution.py:145
  53.8 22.8 %collective-permute-start.3 = (bf16[4,272,128]{2,1,0:T(8,128)(2,1)S(1)}, bf16[4,272,128]{2,1,0:T(8,128)(2,1)S(1)}, u32[]{:S(2)}, u32[]{:S(2)}) collective-permute-start(bf16[4,272,128]{2,1,0:T(8,128)(2,1)S(1)} %shard_map.56), channel_id=1, source_target_pairs={{0,28},{1,5},{2,30},{3,7},{4,0},{5,9},{6,2},{7,11},{8,4},{9,13},{1... | collective-permute-start | bytes 835592 | tf_op jit(solution)/shard_map/ppermute | solution.py:145
  65.3 11.3 %collective-permute-start.5 = (bf16[4,272,128]{2,1,0:T(8,128)(2,1)S(1)}, bf16[4,272,128]{2,1,0:T(8,128)(2,1)S(1)}, u32[]{:S(2)}, u32[]{:S(2)}) collective-permute-start(bf16[4,272,128]{2,1,0:T(8,128)(2,1)S(1)} %shard_map.57), channel_id=1, source_target_pairs={{0,30},{1,31},{2,0},{3,1},{4,2},{5,3},{6,4},{7,5},{8,6},{9,7},{10,... | collective-permute-start | bytes 835592 | tf_op jit(solution)/shard_map/ppermute | solution.py:145
  70.0 9.7 %collective-permute-start.7 = (bf16[4,272,128]{2,1,0:T(8,128)(2,1)S(1)}, bf16[4,272,128]{2,1,0:T(8,128)(2,1)S(1)}, u32[]{:S(2)}, u32[]{:S(2)}) collective-permute-start(bf16[4,272,128]{2,1,0:T(8,128)(2,1)S(1)} %shard_map.58), channel_id=1, source_target_pairs={{0,2},{1,3},{2,4},{3,5},{4,6},{5,7},{6,8},{7,9},{8,10},{9,11},{10,... | collective-permute-start | bytes 835592 | tf_op jit(solution)/shard_map/ppermute | solution.py:145

commit v3 on v2

--- a/solution.py
+++ b/solution.py
@@ -28,23 +28,24 @@
     return tail[0:1] + tail[1:2] + tail[2:3]
 
 
-def attend_kernel(first_ref, x_ref, k0_ref, k1_ref, v0_ref, v1_ref, out_ref):
-    sources, _, cand = out_ref.shape
+def attend_kernel(stride, place_ref, xa_ref, xb_ref, k0_ref, k1_ref, v0_ref, v1_ref, out_ref):
+    members, _, cand = out_ref.shape
+    rest = cand - xa_ref.shape[1]
     positions, width = k0_ref.shape
     nloc = positions // BLK
     scale = 1.0 / width**0.5
-    for s in range(0, sources, 2):
-        query = jnp.concatenate([x_ref[s, :cand, :], x_ref[s + 1, :cand, :]], axis=0)
-        ids = jnp.concatenate(
-            [
-                x_ref[s, cand:, :cand].astype(jnp.float32),
-                x_ref[s + 1, cand:, :cand].astype(jnp.float32),
-            ],
-            axis=1,
-        )
+    for s in range(0, members, 2):
+        rows, ids = [], []
+        for j in range(2):
+            source = place_ref[0] + stride * (s + j)
+            small = xb_ref[source]
+            rows += [xa_ref[source], small[:rest]]
+            ids.append(small[rest:, :cand].astype(jnp.float32))
+        query = jnp.concatenate(rows, axis=0)
+        ids = jnp.concatenate(ids, axis=1)
         parts, lses = [], []
         for half, (k_ref, v_ref) in enumerate(((k0_ref, v0_ref), (k1_ref, v1_ref))):
-            near = ids - first_ref[half].astype(jnp.float32)
+            near = ids - place_ref[1 + half].astype(jnp.float32)
             inside = jnp.logical_and(near >= 0.0, near < nloc)
             sel = jnp.max(jnp.where(inside, near, -1.0), axis=0, keepdims=True)
             scores = lax.dot_general(
@@ -72,15 +73,15 @@
             out_ref[s + j, width:, :] = tail[:, j * cand : (j + 1) * cand]
 
 
-def attend(first, x, keys, vts, cand):
-    sources, _, width = x.shape
+def attend(place, xa, xb, keys, vts, cand, stride):
+    chips, _, width = xa.shape
     return pl.pallas_call(
-        attend_kernel,
-        in_specs=[SMEM] + [VMEM] * 5,
+        functools.partial(attend_kernel, stride),
+        in_specs=[SMEM] + [VMEM] * 6,
         out_specs=VMEM,
-        out_shape=jax.ShapeDtypeStruct((sources, width + TAIL, cand), jnp.bfloat16),
+        out_shape=jax.ShapeDtypeStruct((chips // stride, width + TAIL, cand), jnp.bfloat16),
         compiler_params=PARAMS,
-    )(first, x, *keys, *vts)
+    )(place, xa, xb, *keys, *vts)
 
 
 def mix(blocks):
@@ -151,23 +152,25 @@
 
     swap = [(0, 1), (1, 0)]
     ids = (block_dev * nloc + block_local).astype(jnp.bfloat16).T
-    mine = jnp.concatenate([queries, jnp.pad(ids, ((0, 0), (0, width - cand)))], axis=0)
-    own = exchange(jnp.broadcast_to(mine[None], (members, cand + topk, width)))
+    rest = 8
+    small = jnp.concatenate([queries[cand - rest :], jnp.pad(ids, ((0, 0), (0, width - cand)))], axis=0)
+    xb = lax.all_to_all(
+        jnp.broadcast_to(small[None], (chips, rest + topk, width)), "z", 0, 0, tiled=True
+    )
     vt = hist_values.T
     keys = (hist_keys, lax.ppermute(hist_keys, "core", swap))
     vts = (vt, lax.ppermute(vt, "core", swap))
-    here = 2 * lax.axis_index("z").astype(jnp.int32)
+    xa = lax.all_gather(queries[: cand - rest], "z")
+    z = lax.axis_index("z").astype(jnp.int32)
     core = lax.axis_index("core").astype(jnp.int32)
-    first = jnp.stack([here + core, here + 1 - core]) * nloc
+
+    def part(by):
+        place = [(z + by + chips) % stride, (2 * z + core) * nloc, (2 * z + 1 - core) * nloc]
+        return attend(jnp.stack(place), xa, xb, keys, vts, cand, stride)
 
     steps = (lambda c: 2 - 4 * c, lambda c: 1, lambda c: -1)
-    others = [shift(own, by) for by in steps]
-    mine_part = attend(first, own, keys, vts, cand)
-    back = [
-        shift(attend(first, x, keys, vts, cand), lambda c, by=by: -by(c))
-        for x, by in zip(others, steps)
-    ]
-    merged = near_merge(mine_part, *back)
+    back = [shift(part(by(core)), by) for by in steps]
+    merged = near_merge(part(0), *back)
     return far_merge(exchange(merged))
 
 

time: 104 us -> 112 us (1.077)
  blocking collectives: 23 us -> 60.1 us
  waiting for transfers between devices: 25.6 us -> 3.13 us
  starting transfers between devices: 40.4 us -> 28.8 us
  local copies, waits for them, and re-layouts: 0.94 us -> 4.19 us
  Pallas kernels: 12 us -> 14.5 us
  other arithmetic: 1.69 us -> 0.31 us
    all_gather x0 -> x1, blocking collectives: none -> 35.5 us  [body(): xa = lax.all_gather(queries[:cand - rest], 'z')]
    all_to_all x1, waiting for transfers between devices: 14.2 us -> 0.01 us  [body(): lax.all_to_all(jnp.broadcast_to(small[None], (chips, rest + topk, width))...]
    ppermute x6 -> x3, starting transfers between devices: 21 us -> 9.24 us  [shift(): return lax.ppermute(x, ('z', 'core'), pairs)]
    ppermute x6 -> x3, waiting for transfers between devices: 11.3 us -> 3.12 us  [shift(): return lax.ppermute(x, ('z', 'core'), pairs)]
    unnamed x5 -> x7, local copies, waits for them, and re-layouts: 0.21 us -> 2.01 us
    all_to_all x1, blocking collectives: 23 us -> 24.6 us  [exchange(): lax.all_to_all(x, ('z', 'core'), 0, 0, tiled=True, axis_index_groups=far)]
    slice x0 -> x4, local copies, waits for them, and re-layouts: none -> 1.51 us  [the longest x2 0.83 us: body(): xa = lax.all_gather(queries[:cand - rest], 'z')]
    pallas_call x4, Pallas kernels: 10.9 us -> 12.3 us  [attend(): pl.pallas_call(functools.partial(attend_kernel, stride), in_specs=[SMEM]...]
  transfers between devices with their start and end apart: 9 -> 6, of which waited for: 4 -> 1; matrix products, arithmetic and copies ran while one was open for 0% -> 1% of each run, Pallas kernels for 10% -> 9%
where the time goes in v3:
time: 112 us; the launch traced here: 111 us
  blocking collectives  60.1 us (54%)
  starting transfers between devices  28.8 us (26%)
  Pallas kernels  14.5 us (13%)
  local copies, waits for them, and re-layouts  4.19 us (4%)
  waiting for transfers between devices  3.13 us (3%)
    all_gather x1, blocking collectives, body(): xa = lax.all_gather(queries[:cand - rest], 'z')  35.5 us
    all_to_all x1, blocking collectives, exchange(): lax.all_to_all(x, ('z', 'core'), 0, 0, tiled=True, axis_index_groups=far)  24.6 us
    all_to_all x1, starting transfers between devices, body(): lax.all_to_all(jnp.broadcast_to(small[None], (chips, rest + topk, width))...  15.2 us
    pallas_call x4, Pallas kernels, attend(): pl.pallas_call(functools.partial(attend_kernel, stride), in_specs=[SMEM]...  12.3 us
    ppermute x3, starting transfers between devices, shift(): return lax.ppermute(x, ('z', 'core'), pairs)  9.24 us
    ppermute x3, waiting for transfers between devices, shift(): return lax.ppermute(x, ('z', 'core'), pairs)  3.12 us
    ppermute x1, starting transfers between devices, body(): keys = (hist_keys, lax.ppermute(hist_keys, 'core', swap))  2.41 us
  transfers between devices with their start and end apart: 6, of which 1 were waited for; matrix products, arithmetic and copies ran while one was open for 1% of the time, Pallas kernels for 9%

profile of v3, /device:TPU:6, one launch (start us, length us, event | category | flops | bytes accessed | tf_op | source)
XLA Modules:
  0.0 111.1 jit_solution(13607069382438327053)
XLA Ops:
  0.0 0.7 copy-done.1
  0.7 0.7 slice-done
  1.4 0.7 broadcast_in_dim.2
  2.1 15.2 %all-to-all-start = ((bf16[16,16,256]{2,1,0:T(8,128)(2,1)}), bf16[16,16,256]{2,1,0:T(8,128)(2,1)S(1)}, u32[]{:S(2)}, u32[]{:S(2)}) async-start(bf16[16,16,256]{2,1,0:T(8,128)(2,1)} %broadcast_in_dim.2), calls=%async_computation | async-start | bytes 262144 | tf_op jit(solution)/shard_map/all_to_all | solution.py:157
  17.3 1.3 %copy.6 = bf16[1024,256]{0,1:T(8,128)(2,1)S(1)} copy(bf16[1024,256]{1,0:T(8,128)(2,1)} %param.7) | data formatting | bytes 1048576 | tf_op args[2]
  18.6 1.9 %collective-permute-start.1 = (bf16[256,1024]{1,0:T(8,128)(2,1)S(1)}, bf16[256,1024]{1,0:T(8,128)(2,1)S(1)}, u32[]{:S(2)}, u32[]{:S(2)}) collective-permute-start(bf16[256,1024]{1,0:T(8,128)(2,1)S(1)} %bitcast.14), channel_id=1, source_target_pairs={{0,1},{1,0},{2,3},{3,2},{4,5},{5,4},{6,7},{7,6},{8,9},{9,8},{10,11... | collective-permute-start | bytes 1572872 | tf_op jit(solution)/shard_map/ppermute | solution.py:162
  20.5 2.4 %collective-permute-start = (bf16[1024,256]{1,0:T(8,128)(2,1)S(1)}, bf16[1024,256]{1,0:T(8,128)(2,1)S(1)}, u32[]{:S(2)}, u32[]{:S(2)}) collective-permute-start(bf16[1024,256]{1,0:T(8,128)(2,1)S(1)} %copy-done), channel_id=1, source_target_pairs={{0,1},{1,0},{2,3},{3,2},{4,5},{5,4},{6,7},{7,6},{8,9},{9,8},{10,11... | collective-permute-start | bytes 1572872 | tf_op jit(solution)/shard_map/ppermute | solution.py:161
  23.0 0.1 add_add_fusion.1.place_ref
  23.0 0.1 add_add_fusion.2.place_ref
  23.1 0.1 add_add_fusion.3.place_ref
  23.2 0.8 slice-done.1
  24.0 35.5 %all-gather = bf16[1920,256]{1,0:T(8,128)(2,1)S(1)} all-gather(bf16[120,256]{1,0:T(8,128)(2,1)S(1)} %slice-done.1), channel_id=2, replica_groups=mesh['group'=16,'z'=16,'core'=2] {'z'}, dimensions={0}, use_global_device_ids=true | all-gather | bytes 1044480 | tf_op jit(solution)/shard_map/all_gather | solution.py:163
  59.6 2.7 %shard_map.56 = bf16[4,272,128]{2,1,0:T(8,128)(2,1)S(1)} custom-call(s32[3]{0:T(128)S(1)} %add_add_fusion.1.place_ref, bf16[16,120,256]{2,1,0:T(8,128)(2,1)S(1)} %bitcast.10, bf16[16,16,256]{2,1,0:T(8,128)(2,1)S(1)} %all-to-all-done.xb_ref, bf16[1024,256]{1,0:T(8,128)(2,1)S(1)} %copy-done, bf16[1024,256]{1,0:T(8,128)(2,1)S(1)} %collective-permute-done.k1_ref, ...), custom_call_target="tpu_custom_call" | custom-call | tf_op jit(solution)/shard_map/pallas_call | solution.py:78
  62.3 2.2 %collective-permute-start.2 = (bf16[4,272,128]{2,1,0:T(8,128)(2,1)S(1)}, bf16[4,272,128]{2,1,0:T(8,128)(2,1)}, u32[]{:S(2)}, u32[]{:S(2)}) collective-permute-start(bf16[4,272,128]{2,1,0:T(8,128)(2,1)S(1)} %shard_map.56), channel_id=1, source_target_pairs={{0,4},{1,29},{2,6},{3,31},{4,8},{5,1},{6,10},{7,3},{8,12},{9,5},{1... | collective-permute-start | bytes 835592 | tf_op jit(solution)/shard_map/ppermute | solution.py:146
  64.5 3.4 %shard_map.57 = bf16[4,272,128]{2,1,0:T(8,128)(2,1)} custom-call(s32[3]{0:T(128)S(1)} %add_add_fusion.2.place_ref, bf16[16,120,256]{2,1,0:T(8,128)(2,1)S(1)} %bitcast.11, bf16[16,16,256]{2,1,0:T(8,128)(2,1)S(1)} %all-to-all-done.xb_ref, bf16[1024,256]{1,0:T(8,128)(2,1)S(1)} %copy-done, bf16[1024,256]{1,0:T(8,128)(2,1)S(1)} %collective-permute-done.k1_ref, ...), custom_call_target="tpu_custom_call" | custom-call | tf_op jit(solution)/shard_map/pallas_call | solution.py:78
  67.9 4.3 %collective-permute-start.3 = (bf16[4,272,128]{2,1,0:T(8,128)(2,1)}, bf16[4,272,128]{2,1,0:T(8,128)(2,1)}, u32[]{:S(2)}, u32[]{:S(2)}) collective-permute-start(bf16[4,272,128]{2,1,0:T(8,128)(2,1)} %shard_map.57), channel_id=1, source_target_pairs={{0,2},{1,3},{2,4},{3,5},{4,6},{5,7},{6,8},{7,9},{8,10},{9,11},{10,... | collective-permute-start | bytes 835592 | tf_op jit(solution)/shard_map/ppermute | solution.py:146
  72.2 3.4 %shard_map.58 = bf16[4,272,128]{2,1,0:T(8,128)(2,1)} custom-call(s32[3]{0:T(128)S(1)} %add_add_fusion.3.place_ref, bf16[16,120,256]{2,1,0:T(8,128)(2,1)S(1)} %bitcast.12, bf16[16,16,256]{2,1,0:T(8,128)(2,1)S(1)} %all-to-all-done.xb_ref, bf16[1024,256]{1,0:T(8,128)(2,1)S(1)} %copy-done, bf16[1024,256]{1,0:T(8,128)(2,1)S(1)} %collective-permute-done.k1_ref, ...), custom_call_target="tpu_custom_call" | custom-call | tf_op jit(solution)/shard_map/pallas_call | solution.py:78
  75.6 2.8 %collective-permute-start.4 = (bf16[4,272,128]{2,1,0:T(8,128)(2,1)}, bf16[4,272,128]{2,1,0:T(8,128)(2,1)}, u32[]{:S(2)}, u32[]{:S(2)}) collective-permute-start(bf16[4,272,128]{2,1,0:T(8,128)(2,1)} %shard_map.58), channel_id=1, source_target_pairs={{0,30},{1,31},{2,0},{3,1},{4,2},{5,3},{6,4},{7,5},{8,6},{9,7},{10,... | collective-permute-start | bytes 835592 | tf_op jit(solution)/shard_map/ppermute | solution.py:146
  78.4 0.1 add_add_fusion.place_ref
  78.5 2.7 %shard_map.55.refs_0_ = bf16[4,272,128]{2,1,0:T(8,128)(2,1)S(1)} custom-call(s32[3]{0:T(128)S(1)} %add_add_fusion.place_ref, bf16[16,120,256]{2,1,0:T(8,128)(2,1)S(1)} %bitcast.13, bf16[16,16,256]{2,1,0:T(8,128)(2,1)S(1)} %all-to-all-done.xb_ref, bf16[1024,256]{1,0:T(8,128)(2,1)S(1)} %copy-done, bf16[1024,256]{1,0:T(8,128)(2,1)S(1)} %collective-permute-done.k1_ref, ...), custom_call_target="tpu_custom_call" | custom-call | tf_op jit(solution)/shard_map/pallas_call | solution.py:78
  81.3 3.1 %collective-permute-done.4.refs_3_ = bf16[4,272,128]{2,1,0:T(8,128)(2,1)} collective-permute-done((bf16[4,272,128]{2,1,0:T(8,128)(2,1)}, bf16[4,272,128]{2,1,0:T(8,128)(2,1)}, u32[]{:S(2)}, u32[]{:S(2)}) %collective-permute-start.4) | collective-permute-done | bytes 278560 | tf_op jit(solution)/shard_map/ppermute | solution.py:146
  84.4 1.4 %shard_map.59 = bf16[4,272,128]{2,1,0:T(8,128)(2,1)S(1)} custom-call(bf16[4,272,128]{2,1,0:T(8,128)(2,1)S(1)} %shard_map.55.refs_0_, bf16[4,272,128]{2,1,0:T(8,128)(2,1)} %collective-permute-done.2.refs_1_, bf16[4,272,128]{2,1,0:T(8,128)(2,1)} %collective-permute-done.3.refs_2_, bf16[4,272,128]{2,1,0:T(8,128)(2,1)} %collective-permute-done.4.refs_3_), custom_call_target="tpu_custom_call" | custom-call | tf_op jit(solution)/shard_map/pallas_call | solution.py:110
  85.8 24.6 %all_to_all.10.x_ref = bf16[4,272,128]{2,1,0:T(8,128)(2,1)S(1)} all-to-all(bf16[4,272,128]{2,1,0:T(8,128)(2,1)S(1)} %shard_map.59), channel_id=1, replica_groups={{0,8,16,24},{2,10,18,26},{4,12,20,28},{6,14,22,30},{1,9,17,25},{3,11,19..., dimensions={0} | all-to-all | bytes 557056 | tf_op jit(solution)/shard_map/all_to_all | solution.py:151
  110.4 0.8 shard_map.60
  (14 shorter events, 0.0 us)
Async XLA Ops:
  0.0 0.7 copy-start.1
  0.0 0.7 copy-start.2
  0.7 0.7 slice-start
  2.1 57.5 %all-to-all-start = ((bf16[16,16,256]{2,1,0:T(8,128)(2,1)}), bf16[16,16,256]{2,1,0:T(8,128)(2,1)S(1)}, u32[]{:S(2)}, u32[]{:S(2)}) async-start(bf16[16,16,256]{2,1,0:T(8,128)(2,1)} %broadcast_in_dim.2), calls=%async_computation | async-start | bytes 262144 | tf_op jit(solution)/shard_map/all_to_all | solution.py:157
  17.3 3.3 %copy-start = (bf16[1024,256]{1,0:T(8,128)(2,1)S(1)}, bf16[1024,256]{1,0:T(8,128)(2,1)}, u32[]{:S(2)}) copy-start(bf16[1024,256]{1,0:T(8,128)(2,1)} %k0_ref.7) | copy-start | bytes 1572868
  18.6 41.0 %collective-permute-start.1 = (bf16[256,1024]{1,0:T(8,128)(2,1)S(1)}, bf16[256,1024]{1,0:T(8,128)(2,1)S(1)}, u32[]{:S(2)}, u32[]{:S(2)}) collective-permute-start(bf16[256,1024]{1,0:T(8,128)(2,1)S(1)} %bitcast.14), channel_id=1, source_target_pairs={{0,1},{1,0},{2,3},{3,2},{4,5},{5,4},{6,7},{7,6},{8,9},{9,8},{10,11... | collective-permute-start | bytes 1572872 | tf_op jit(solution)/shard_map/ppermute | solution.py:162
  20.5 39.0 %collective-permute-start = (bf16[1024,256]{1,0:T(8,128)(2,1)S(1)}, bf16[1024,256]{1,0:T(8,128)(2,1)S(1)}, u32[]{:S(2)}, u32[]{:S(2)}) collective-permute-start(bf16[1024,256]{1,0:T(8,128)(2,1)S(1)} %copy-done), channel_id=1, source_target_pairs={{0,1},{1,0},{2,3},{3,2},{4,5},{5,4},{6,7},{7,6},{8,9},{9,8},{10,11... | collective-permute-start | bytes 1572872 | tf_op jit(solution)/shard_map/ppermute | solution.py:161
  23.2 0.8 slice-start.1
  62.3 18.9 %collective-permute-start.2 = (bf16[4,272,128]{2,1,0:T(8,128)(2,1)S(1)}, bf16[4,272,128]{2,1,0:T(8,128)(2,1)}, u32[]{:S(2)}, u32[]{:S(2)}) collective-permute-start(bf16[4,272,128]{2,1,0:T(8,128)(2,1)S(1)} %shard_map.56), channel_id=1, source_target_pairs={{0,4},{1,29},{2,6},{3,31},{4,8},{5,1},{6,10},{7,3},{8,12},{9,5},{1... | collective-permute-start | bytes 835592 | tf_op jit(solution)/shard_map/ppermute | solution.py:146
  67.9 13.3 %collective-permute-start.3 = (bf16[4,272,128]{2,1,0:T(8,128)(2,1)}, bf16[4,272,128]{2,1,0:T(8,128)(2,1)}, u32[]{:S(2)}, u32[]{:S(2)}) collective-permute-start(bf16[4,272,128]{2,1,0:T(8,128)(2,1)} %shard_map.57), channel_id=1, source_target_pairs={{0,2},{1,3},{2,4},{3,5},{4,6},{5,7},{6,8},{7,9},{8,10},{9,11},{10,... | collective-permute-start | bytes 835592 | tf_op jit(solution)/shard_map/ppermute | solution.py:146
  75.6 8.7 %collective-permute-start.4 = (bf16[4,272,128]{2,1,0:T(8,128)(2,1)}, bf16[4,272,128]{2,1,0:T(8,128)(2,1)}, u32[]{:S(2)}, u32[]{:S(2)}) collective-permute-start(bf16[4,272,128]{2,1,0:T(8,128)(2,1)} %shard_map.58), channel_id=1, source_target_pairs={{0,30},{1,31},{2,0},{3,1},{4,2},{5,3},{6,4},{7,5},{8,6},{9,7},{10,... | collective-permute-start | bytes 835592 | tf_op jit(solution)/shard_map/ppermute | solution.py:146

commit v4 on v2

v4 whole, which is shorter than its diff:
```python
import functools

import jax
import jax.numpy as jnp
from jax import lax
from jax.experimental import pallas as pl
from jax.experimental.pallas import tpu as pltpu
from jax.sharding import Mesh, PartitionSpec as P

BLK = 128
NONE = -1e30
TAIL = 16
VMEM = pl.BlockSpec(memory_space=pltpu.VMEM)
SMEM = pl.BlockSpec(memory_space=pltpu.SMEM)
ANY = pl.BlockSpec(memory_space=pl.ANY)
PARAMS = pltpu.CompilerParams(vmem_limit_bytes=40 * 1024 * 1024)


def tail_rows(lse):
    big = lse.astype(jnp.bfloat16).astype(jnp.float32)
    rest = lse - big
    mid = rest.astype(jnp.bfloat16).astype(jnp.float32)
    row = lax.broadcasted_iota(jnp.int32, (TAIL, lse.shape[1]), 0)
    return jnp.where(row == 0, big, jnp.where(row == 1, mid, rest - mid)).astype(jnp.bfloat16)


def lse_row(tail):
    tail = tail.astype(jnp.float32)
    return tail[0:1] + tail[1:2] + tail[2:3]


def attend_kernel(counts, first_ref, k0_ref, k1_ref, v0_ref, v1_ref, *refs):
    cand = refs[-1].shape[2]
    positions, width = k0_ref.shape
    nloc = positions // BLK
    scale = 1.0 / width**0.5
    slots = [
        (x_ref, out_ref, s)
        for x_ref, out_ref, count in zip(refs, refs[-len(counts) :], counts)
        for s in range(count)
    ]
    for p in range(0, len(slots), 2):
        pair = slots[p : p + 2]
        query = jnp.concatenate([x_ref[s, :cand, :] for x_ref, _, s in pair], axis=0)
        ids = jnp.concatenate(
            [x_ref[s, cand:, :cand].astype(jnp.float32) for x_ref, _, s in pair], axis=1
        )
        parts, lses = [], []
        for half, (k_ref, v_ref) in enumerate(((k0_ref, v0_ref), (k1_ref, v1_ref))):
            near = ids - first_ref[half].astype(jnp.float32)
            inside = jnp.logical_and(near >= 0.0, near < nloc)
            sel = jnp.max(jnp.where(inside, near, -1.0), axis=0, keepdims=True)
            scores = lax.dot_general(
                k_ref[...], query, (((1,), (1,)), ((), ())), preferred_element_type=jnp.float32
            )
            picked = scores[0:BLK]
            for b in range(1, nloc):
                picked = jnp.where(sel == b, scores[b * BLK : (b + 1) * BLK], picked)
            peak = jnp.max(picked, axis=0, keepdims=True)
            expo = jnp.exp((picked - peak) * scale)
            total = jnp.sum(expo, axis=0, keepdims=True)
            spread = jnp.concatenate(
                [jnp.where(sel == b, expo, 0.0).astype(jnp.bfloat16) for b in range(nloc)], axis=0
            )
            summed = jnp.dot(v_ref[...], spread, preferred_element_type=jnp.float32)
            parts.append((summed / total).astype(jnp.bfloat16).astype(jnp.float32))
            lses.append(jnp.where(sel >= 0.0, peak * scale + jnp.log(total), NONE))
        top = jnp.maximum(lses[0], lses[1])
        mix0, mix1 = jnp.exp(lses[0] - top), jnp.exp(lses[1] - top)
        mixed = mix0 + mix1
        merged = ((mix0 / mixed) * parts[0] + (mix1 / mixed) * parts[1]).astype(jnp.bfloat16)
        tail = tail_rows(top + jnp.log(mixed))
        for j, (_, out_ref, s) in enumerate(pair):
            out_ref[s, :width, :] = merged[:, j * cand : (j + 1) * cand]
            out_ref[s, width:, :] = tail[:, j * cand : (j + 1) * cand]


def attend(first, xs, keys, vts, cand, after=()):
    counts = [x.shape[0] for x in xs]
    width = xs[0].shape[2]
    return pl.pallas_call(
        functools.partial(attend_kernel, counts),
        in_specs=[SMEM] + [VMEM] * (4 + len(xs)) + [ANY] * len(after),
        out_specs=[VMEM] * len(xs),
        out_shape=[jax.ShapeDtypeStruct((n, width + TAIL, cand), jnp.bfloat16) for n in counts],
        compiler_params=PARAMS,
    )(first, *keys, *vts, *xs, *after)


def mix(blocks):
    width = blocks[0].shape[0] - TAIL
    lses = [lse_row(one[width:, :]) for one in blocks]
    top = functools.reduce(jnp.maximum, lses)
    mixes = [jnp.exp(one - top) for one in lses]
    mixed = functools.reduce(jnp.add, mixes)
    inverse = 1.0 / mixed
    total = (mixes[0] * inverse) * blocks[0][:width, :].astype(jnp.float32)
    for one, block in zip(mixes[1:], blocks[1:]):
        total = total + (one * inverse) * block[:width, :].astype(jnp.float32)
    return total, top + jnp.log(mixed)


def stack_kernel(*refs):
    out_ref = refs[-1]
    for s in range(out_ref.shape[0]):
        out_ref[s] = refs[s][...]


def stack(blocks, after):
    return pl.pallas_call(
        stack_kernel,
        in_specs=[VMEM] * len(blocks) + [ANY] * len(after),
        out_specs=VMEM,
        out_shape=jax.ShapeDtypeStruct((len(blocks),) + blocks[0].shape, blocks[0].dtype),
        compiler_params=PARAMS,
    )(*blocks, *after)


def near_kernel(*refs):
    *parts, extra, out1_ref, out2_ref = refs
    width = out1_ref.shape[0] - TAIL
    for slot, out_ref in ((1, out1_ref), (2, out2_ref)):
        blocks = [ref[slot] for ref in parts] + ([extra[0]] if slot == 1 else [])
        total, lse = mix(blocks)
        out_ref[:width, :] = total.astype(jnp.bfloat16)
        out_ref[width:, :] = tail_rows(lse)


def near_merge(parts, extra):
    shape = jax.ShapeDtypeStruct(extra.shape[1:], extra.dtype)
    return pl.pallas_call(
        near_kernel,
        in_specs=[VMEM] * (len(parts) + 1),
        out_specs=[VMEM] * 2,
        out_shape=[shape] * 2,
        compiler_params=PARAMS,
    )(*parts, extra)


def far_kernel(*refs):
    *parts, one, two, out_ref = refs
    total, _ = mix([ref[0] for ref in parts] + [one[...], two[...]])
    out_ref[...] = total.T.astype(jnp.bfloat16)


def far_merge(parts, one, two):
    rows, cand = one.shape
    return pl.pallas_call(
        far_kernel,
        in_specs=[VMEM] * (len(parts) + 2),
        out_specs=VMEM,
        out_shape=jax.ShapeDtypeStruct((cand, rows - TAIL), jnp.bfloat16),
        compiler_params=PARAMS,
    )(*parts, one, two)


def body(chips, queries, hist_keys, hist_values, block_dev, block_local):
    cand, width = queries.shape
    nloc = hist_keys.shape[0] // BLK

    def shift(x, by):
        pairs = [
            (2 * z + c, 2 * ((z + by * (1 - 2 * c)) % chips) + c)
            for z in range(chips)
            for c in range(2)
        ]
        return lax.ppermute(x, ("z", "core"), pairs)

    ids = (block_dev * nloc + block_local).astype(jnp.bfloat16).T
    mine = jnp.concatenate([queries, jnp.pad(ids, ((0, 0), (0, width - cand)))], axis=0)
    up5, down5 = shift(mine, -5), shift(mine, 5)

    swap = [(0, 1), (1, 0)]
    vt = hist_values.T
    keys = (hist_keys, lax.ppermute(hist_keys, "core", swap))
    vts = (vt, lax.ppermute(vt, "core", swap))
    here = 2 * lax.axis_index("z").astype(jnp.int32)
    core = lax.axis_index("core").astype(jnp.int32)
    first = jnp.stack([here + core, here + 1 - core]) * nloc

    own = stack([mine, up5, down5], (keys[1], vts[1]))
    up2, down2 = shift(own, -2), shift(own, 2)
    eight = shift(up5[None], -3)
    up1, down1 = shift(own, -1), shift(own, 1)

    part_up2, part_down2 = attend(first, (up2, down2), keys, vts, cand)
    back = [shift(part_up2, 2), shift(part_down2, -2)]
    part_own, part_eight = attend(first, (own, eight), keys, vts, cand, (part_up2,))
    extra = shift(part_eight, 3)
    part_up1, part_down1 = attend(first, (up1, down1), keys, vts, cand, (part_eight,))
    back += [shift(part_up1, 1), shift(part_down1, -1)]
    parts = [part_own] + back
    slot1, slot2 = near_merge(parts, extra)
    return far_merge(parts, shift(slot1, 5), shift(slot2, -5))


def solution(mesh):
    groups, pos = mesh.devices.shape
    chips = Mesh(mesh.devices.reshape(groups, pos // 2, 2), ("group", "z", "core"))
    spec = P(("group", "z", "core"), None)
    return jax.shard_map(
        functools.partial(body, pos // 2),
        mesh=chips,
        in_specs=(spec,) * 5,
        out_specs=spec,
        check_vma=False,
    )
```

time: 104 us -> 103 us (level)
  the two profiles are of different devices: /device:TPU:6 before, /device:TPU:1 now
where the time goes in v4:
time: 103 us; the launch traced here: 102 us
  starting transfers between devices  69.9 us (68%)
  waiting for transfers between devices  20.2 us (20%)
  Pallas kernels  10.3 us (10%)
  local copies, waits for them, and re-layouts  1.28 us (1%)
    ppermute x14, starting transfers between devices, shift(): return lax.ppermute(x, ('z', 'core'), pairs)  59 us
    ppermute x14, waiting for transfers between devices, shift(): return lax.ppermute(x, ('z', 'core'), pairs)  20.2 us
    pallas_call x3, Pallas kernels, attend(): pl.pallas_call(functools.partial(attend_kernel, counts), in_specs=[SMEM]...  9.25 us
    ppermute x1, starting transfers between devices, body(): keys = (hist_keys, lax.ppermute(hist_keys, 'core', swap))  8.91 us
  transfers between devices with their start and end apart: 16, of which 4 were waited for; matrix products, arithmetic and copies ran while one was open for 1% of the time, Pallas kernels for 9%

profile of v4, /device:TPU:1, one launch (start us, length us, event | category | flops | bytes accessed | tf_op | source)
XLA Modules:
  0.0 102.0 jit_solution(15394858277249281436)
XLA Ops:
  0.0 8.9 %collective-permute-start = (bf16[1024,256]{1,0:T(8,128)(2,1)}, bf16[1024,256]{1,0:T(8,128)(2,1)S(1)}, u32[]{:S(2)}, u32[]{:S(2)}) collective-permute-start(bf16[1024,256]{1,0:T(8,128)(2,1)} %k0_ref.5), channel_id=1, source_target_pairs={{0,1},{1,0},{2,3},{3,2},{4,5},{5,4},{6,7},{7,6},{8,9},{9,8},{10,11... | collective-permute-start | bytes 1572872 | tf_op jit(solution)/shard_map/ppermute | solution.py:175
  8.9 1.3 %copy.6 = bf16[1024,256]{0,1:T(8,128)(2,1)S(1)} copy(bf16[1024,256]{1,0:T(8,128)(2,1)} %param.7) | data formatting | bytes 1048576 | tf_op args[2]
  10.2 1.9 %collective-permute-start.1 = (bf16[256,1024]{1,0:T(8,128)(2,1)S(1)}, bf16[256,1024]{1,0:T(8,128)(2,1)S(1)}, u32[]{:S(2)}, u32[]{:S(2)}) collective-permute-start(bf16[256,1024]{1,0:T(8,128)(2,1)S(1)} %bitcast.6), channel_id=1, source_target_pairs={{0,1},{1,0},{2,3},{3,2},{4,5},{5,4},{6,7},{7,6},{8,9},{9,8},{10,11... | collective-permute-start | bytes 1572872 | tf_op jit(solution)/shard_map/ppermute | solution.py:176
  12.2 4.9 %collective-permute-start.2 = (bf16[136,256]{1,0:T(8,128)(2,1)S(1)}, bf16[136,256]{1,0:T(8,128)(2,1)S(1)}, u32[]{:S(2)}, u32[]{:S(2)}) collective-permute-start(bf16[136,256]{1,0:T(8,128)(2,1)S(1)} %fusion.1.refs_0_), channel_id=1, source_target_pairs={{0,22},{1,11},{2,24},{3,13},{4,26},{5,15},{6,28},{7,17},{8,30},{9,... | collective-permute-start | bytes 208904 | tf_op jit(solution)/shard_map/ppermute | solution.py:167
  17.1 6.5 %collective-permute-start.3 = (bf16[136,256]{1,0:T(8,128)(2,1)S(1)}, bf16[136,256]{1,0:T(8,128)(2,1)S(1)}, u32[]{:S(2)}, u32[]{:S(2)}) collective-permute-start(bf16[136,256]{1,0:T(8,128)(2,1)S(1)} %fusion.1.refs_0_), channel_id=1, source_target_pairs={{0,10},{1,23},{2,12},{3,25},{4,14},{5,27},{6,16},{7,29},{8,18},{9,... | collective-permute-start | bytes 208904 | tf_op jit(solution)/shard_map/ppermute | solution.py:167
  23.7 6.3 %collective-permute-done.3.refs_2_ = bf16[136,256]{1,0:T(8,128)(2,1)S(1)} collective-permute-done((bf16[136,256]{1,0:T(8,128)(2,1)S(1)}, bf16[136,256]{1,0:T(8,128)(2,1)S(1)}, u32[]{:S(2)}, u32[]{:S(2)}) %collective-permute-start.3) | collective-permute-done | bytes 69664 | tf_op jit(solution)/shard_map/ppermute | solution.py:167
  29.9 2.0 %collective-permute-start.5 = (bf16[3,136,256]{2,1,0:T(8,128)(2,1)S(1)}, bf16[3,136,256]{2,1,0:T(8,128)(2,1)S(1)}, u32[]{:S(2)}, u32[]{:S(2)}) collective-permute-start(bf16[3,136,256]{2,1,0:T(8,128)(2,1)S(1)} %shard_map.55.refs_0_), channel_id=1, source_target_pairs={{0,28},{1,5},{2,30},{3,7},{4,0},{5,9},{6,2},{7,11},{8,4},{9,13},{1... | collective-permute-start | bytes 626696 | tf_op jit(solution)/shard_map/ppermute | solution.py:167
  31.9 5.4 %collective-permute-start.6 = (bf16[3,136,256]{2,1,0:T(8,128)(2,1)S(1)}, bf16[3,136,256]{2,1,0:T(8,128)(2,1)S(1)}, u32[]{:S(2)}, u32[]{:S(2)}) collective-permute-start(bf16[3,136,256]{2,1,0:T(8,128)(2,1)S(1)} %shard_map.55.refs_0_), channel_id=1, source_target_pairs={{0,4},{1,29},{2,6},{3,31},{4,8},{5,1},{6,10},{7,3},{8,12},{9,5},{1... | collective-permute-start | bytes 626696 | tf_op jit(solution)/shard_map/ppermute | solution.py:167
  37.4 3.6 %collective-permute-start.9 = (bf16[3,136,256]{2,1,0:T(8,128)(2,1)S(1)}, bf16[3,136,256]{2,1,0:T(8,128)(2,1)S(1)}, u32[]{:S(2)}, u32[]{:S(2)}) collective-permute-start(bf16[3,136,256]{2,1,0:T(8,128)(2,1)S(1)} %shard_map.55.refs_0_), channel_id=1, source_target_pairs={{0,30},{1,3},{2,0},{3,5},{4,2},{5,7},{6,4},{7,9},{8,6},{9,11},{10,... | collective-permute-start | bytes 626696 | tf_op jit(solution)/shard_map/ppermute | solution.py:167
  41.0 2.9 %collective-permute-start.10 = (bf16[3,136,256]{2,1,0:T(8,128)(2,1)S(1)}, bf16[3,136,256]{2,1,0:T(8,128)(2,1)S(1)}, u32[]{:S(2)}, u32[]{:S(2)}) collective-permute-start(bf16[3,136,256]{2,1,0:T(8,128)(2,1)S(1)} %shard_map.55.refs_0_), channel_id=1, source_target_pairs={{0,2},{1,31},{2,4},{3,1},{4,6},{5,3},{6,8},{7,5},{8,10},{9,7},{10,... | collective-permute-start | bytes 626696 | tf_op jit(solution)/shard_map/ppermute | solution.py:167
  43.9 5.8 %collective-permute-start.4 = (bf16[1,136,256]{2,1,0:T(8,128)(2,1)S(1)}, bf16[1,136,256]{2,1,0:T(8,128)(2,1)S(1)}, u32[]{:S(2)}, u32[]{:S(2)}) collective-permute-start(bf16[1,136,256]{2,1,0:T(8,128)(2,1)S(1)} %bitcast.10), channel_id=1, source_target_pairs={{0,26},{1,7},{2,28},{3,9},{4,30},{5,11},{6,0},{7,13},{8,2},{9,15},... | collective-permute-start | bytes 208904 | tf_op jit(solution)/shard_map/ppermute | solution.py:167
  49.8 3.3 %shard_map.56 = (bf16[3,272,128]{2,1,0:T(8,128)(2,1)S(1)}, bf16[3,272,128]{2,1,0:T(8,128)(2,1)S(1)}) custom-call(s32[2]{0:T(128)S(1)} %add_multiply_fusion.first_ref, bf16[1024,256]{1,0:T(8,128)(2,1)S(1)} %copy-done, bf16[1024,256]{1,0:T(8,128)(2,1)S(1)} %collective-permute-done.refs_3_.k1_ref, bf16[256,1024]{1,0:T(8,128)(2,1)S(1)} %bitcast.7, ...), custom_call_target="tpu_custom_call" | custom-call | tf_op jit(solution)/shard_map/pallas_call | solution.py:81
  53.1 1.9 %collective-permute-start.7 = (bf16[3,272,128]{2,1,0:T(8,128)(2,1)S(1)}, bf16[3,272,128]{2,1,0:T(8,128)(2,1)S(1)}, u32[]{:S(2)}, u32[]{:S(2)}) collective-permute-start(bf16[3,272,128]{2,1,0:T(8,128)(2,1)S(1)} %get-tuple-element.13.refs_2_), channel_id=1, source_target_pairs={{0,4},{1,29},{2,6},{3,31},{4,8},{5,1},{6,10},{7,3},{8,12},{9,5},{1... | collective-permute-start | bytes 626696 | tf_op jit(solution)/shard_map/ppermute | solution.py:167
  55.0 4.3 %collective-permute-start.8 = (bf16[3,272,128]{2,1,0:T(8,128)(2,1)S(1)}, bf16[3,272,128]{2,1,0:T(8,128)(2,1)S(1)}, u32[]{:S(2)}, u32[]{:S(2)}) collective-permute-start(bf16[3,272,128]{2,1,0:T(8,128)(2,1)S(1)} %get-tuple-element.15), channel_id=1, source_target_pairs={{0,28},{1,5},{2,30},{3,7},{4,0},{5,9},{6,2},{7,11},{8,4},{9,13},{1... | collective-permute-start | bytes 626696 | tf_op jit(solution)/shard_map/ppermute | solution.py:167
  59.3 2.7 %shard_map.57 = (bf16[3,272,128]{2,1,0:T(8,128)(2,1)S(1)}, bf16[1,272,128]{2,1,0:T(8,128)(2,1)S(1)}) custom-call(s32[2]{0:T(128)S(1)} %add_multiply_fusion.first_ref, bf16[1024,256]{1,0:T(8,128)(2,1)S(1)} %copy-done, bf16[1024,256]{1,0:T(8,128)(2,1)S(1)} %collective-permute-done.refs_3_.k1_ref, bf16[256,1024]{1,0:T(8,128)(2,1)S(1)} %bitcast.8, ...), custom_call_target="tpu_custom_call" | custom-call | tf_op jit(solution)/shard_map/pallas_call | solution.py:81
  62.0 3.3 %shard_map.58 = (bf16[3,272,128]{2,1,0:T(8,128)(2,1)S(1)}, bf16[3,272,128]{2,1,0:T(8,128)(2,1)S(1)}) custom-call(s32[2]{0:T(128)S(1)} %add_multiply_fusion.first_ref, bf16[1024,256]{1,0:T(8,128)(2,1)S(1)} %copy-done, bf16[1024,256]{1,0:T(8,128)(2,1)S(1)} %collective-permute-done.refs_3_.k1_ref, bf16[256,1024]{1,0:T(8,128)(2,1)S(1)} %bitcast.9, ...), custom_call_target="tpu_custom_call" | custom-call | tf_op jit(solution)/shard_map/pallas_call | solution.py:81
  65.3 4.6 %collective-permute-start.11 = (bf16[3,272,128]{2,1,0:T(8,128)(2,1)S(1)}, bf16[3,272,128]{2,1,0:T(8,128)(2,1)S(1)}, u32[]{:S(2)}, u32[]{:S(2)}) collective-permute-start(bf16[3,272,128]{2,1,0:T(8,128)(2,1)S(1)} %get-tuple-element.17), channel_id=1, source_target_pairs={{0,2},{1,31},{2,4},{3,1},{4,6},{5,3},{6,8},{7,5},{8,10},{9,7},{10,... | collective-permute-start | bytes 626696 | tf_op jit(solution)/shard_map/ppermute | solution.py:167
  69.9 1.9 %collective-permute-start.12 = (bf16[3,272,128]{2,1,0:T(8,128)(2,1)S(1)}, bf16[3,272,128]{2,1,0:T(8,128)(2,1)S(1)}, u32[]{:S(2)}, u32[]{:S(2)}) collective-permute-start(bf16[3,272,128]{2,1,0:T(8,128)(2,1)S(1)} %get-tuple-element.18), channel_id=1, source_target_pairs={{0,30},{1,3},{2,0},{3,5},{4,2},{5,7},{6,4},{7,9},{8,6},{9,11},{10,... | collective-permute-start | bytes 626696 | tf_op jit(solution)/shard_map/ppermute | solution.py:167
  71.9 3.7 %collective-permute-start.13 = (bf16[1,272,128]{2,1,0:T(8,128)(2,1)S(1)}, bf16[1,272,128]{2,1,0:T(8,128)(2,1)S(1)}, u32[]{:S(2)}, u32[]{:S(2)}) collective-permute-start(bf16[1,272,128]{2,1,0:T(8,128)(2,1)S(1)} %get-tuple-element.16.refs_2_), channel_id=1, source_target_pairs={{0,6},{1,27},{2,8},{3,29},{4,10},{5,31},{6,12},{7,1},{8,14},{9,3},... | collective-permute-start | bytes 208904 | tf_op jit(solution)/shard_map/ppermute | solution.py:167
  75.6 3.8 %collective-permute-done.13.refs_5_ = bf16[1,272,128]{2,1,0:T(8,128)(2,1)S(1)} collective-permute-done((bf16[1,272,128]{2,1,0:T(8,128)(2,1)S(1)}, bf16[1,272,128]{2,1,0:T(8,128)(2,1)S(1)}, u32[]{:S(2)}, u32[]{:S(2)}) %collective-permute-start.13) | collective-permute-done | bytes 69664 | tf_op jit(solution)/shard_map/ppermute | solution.py:167
  80.4 9.5 %collective-permute-start.14 = (bf16[272,128]{1,0:T(8,128)(2,1)S(1)}, bf16[272,128]{1,0:T(8,128)(2,1)S(1)}, u32[]{:S(2)}, u32[]{:S(2)}) collective-permute-start(bf16[272,128]{1,0:T(8,128)(2,1)S(1)} %get-tuple-element.19), channel_id=1, source_target_pairs={{0,10},{1,23},{2,12},{3,25},{4,14},{5,27},{6,16},{7,29},{8,18},{9,... | collective-permute-start | bytes 208904 | tf_op jit(solution)/shard_map/ppermute | solution.py:167
  89.9 1.9 %collective-permute-start.15 = (bf16[272,128]{1,0:T(8,128)(2,1)S(1)}, bf16[272,128]{1,0:T(8,128)(2,1)S(1)}, u32[]{:S(2)}, u32[]{:S(2)}) collective-permute-start(bf16[272,128]{1,0:T(8,128)(2,1)S(1)} %get-tuple-element.20), channel_id=1, source_target_pairs={{0,22},{1,11},{2,24},{3,13},{4,26},{5,15},{6,28},{7,17},{8,30},{9,... | collective-permute-start | bytes 208904 | tf_op jit(solution)/shard_map/ppermute | solution.py:167
  91.9 9.3 %collective-permute-done.15.refs_6_ = bf16[272,128]{1,0:T(8,128)(2,1)S(1)} collective-permute-done((bf16[272,128]{1,0:T(8,128)(2,1)S(1)}, bf16[272,128]{1,0:T(8,128)(2,1)S(1)}, u32[]{:S(2)}, u32[]{:S(2)}) %collective-permute-start.15) | collective-permute-done | bytes 69664 | tf_op jit(solution)/shard_map/ppermute | solution.py:167
  101.2 0.8 shard_map.60
  (26 shorter events, 1.1 us)
Async XLA Ops:
  0.0 12.2 %copy-start.1 = (bf16[128,256]{1,0:T(8,128)(2,1)S(1)}, bf16[128,256]{1,0:T(8,128)(2,1)}, u32[]{:S(2)}) copy-start(bf16[128,256]{1,0:T(8,128)(2,1)} %param.5) | copy-start | bytes 196612
  0.0 29.9 %collective-permute-start = (bf16[1024,256]{1,0:T(8,128)(2,1)}, bf16[1024,256]{1,0:T(8,128)(2,1)S(1)}, u32[]{:S(2)}, u32[]{:S(2)}) collective-permute-start(bf16[1024,256]{1,0:T(8,128)(2,1)} %k0_ref.5), channel_id=1, source_target_pairs={{0,1},{1,0},{2,3},{3,2},{4,5},{5,4},{6,7},{7,6},{8,9},{9,8},{10,11... | collective-permute-start | bytes 1572872 | tf_op jit(solution)/shard_map/ppermute | solution.py:175
  8.9 3.2 %copy-start.2 = (s32[128,8]{0,1:T(8,128)S(1)}, s32[128,8]{0,1:T(8,128)}, u32[]{:S(2)}) copy-start(s32[128,8]{0,1:T(8,128)} %param.9) | copy-start | bytes 12292
  8.9 3.2 %copy-start.3 = (s32[128,8]{0,1:T(8,128)S(1)}, s32[128,8]{0,1:T(8,128)}, u32[]{:S(2)}) copy-start(s32[128,8]{0,1:T(8,128)} %param.8) | copy-start | bytes 12292
  10.2 19.7 %collective-permute-start.1 = (bf16[256,1024]{1,0:T(8,128)(2,1)S(1)}, bf16[256,1024]{1,0:T(8,128)(2,1)S(1)}, u32[]{:S(2)}, u32[]{:S(2)}) collective-permute-start(bf16[256,1024]{1,0:T(8,128)(2,1)S(1)} %bitcast.6), channel_id=1, source_target_pairs={{0,1},{1,0},{2,3},{3,2},{4,5},{5,4},{6,7},{7,6},{8,9},{9,8},{10,11... | collective-permute-start | bytes 1572872 | tf_op jit(solution)/shard_map/ppermute | solution.py:176
  12.2 37.6 %copy-start = (bf16[1024,256]{1,0:T(8,128)(2,1)S(1)}, bf16[1024,256]{1,0:T(8,128)(2,1)}, u32[]{:S(2)}) copy-start(bf16[1024,256]{1,0:T(8,128)(2,1)} %k0_ref.5) | copy-start | bytes 1572868
  12.2 11.4 %collective-permute-start.2 = (bf16[136,256]{1,0:T(8,128)(2,1)S(1)}, bf16[136,256]{1,0:T(8,128)(2,1)S(1)}, u32[]{:S(2)}, u32[]{:S(2)}) collective-permute-start(bf16[136,256]{1,0:T(8,128)(2,1)S(1)} %fusion.1.refs_0_), channel_id=1, source_target_pairs={{0,22},{1,11},{2,24},{3,13},{4,26},{5,15},{6,28},{7,17},{8,30},{9,... | collective-permute-start | bytes 208904 | tf_op jit(solution)/shard_map/ppermute | solution.py:167
  17.1 12.8 %collective-permute-start.3 = (bf16[136,256]{1,0:T(8,128)(2,1)S(1)}, bf16[136,256]{1,0:T(8,128)(2,1)S(1)}, u32[]{:S(2)}, u32[]{:S(2)}) collective-permute-start(bf16[136,256]{1,0:T(8,128)(2,1)S(1)} %fusion.1.refs_0_), channel_id=1, source_target_pairs={{0,10},{1,23},{2,12},{3,25},{4,14},{5,27},{6,16},{7,29},{8,18},{9,... | collective-permute-start | bytes 208904 | tf_op jit(solution)/shard_map/ppermute | solution.py:167
  29.9 19.8 %collective-permute-start.5 = (bf16[3,136,256]{2,1,0:T(8,128)(2,1)S(1)}, bf16[3,136,256]{2,1,0:T(8,128)(2,1)S(1)}, u32[]{:S(2)}, u32[]{:S(2)}) collective-permute-start(bf16[3,136,256]{2,1,0:T(8,128)(2,1)S(1)} %shard_map.55.refs_0_), channel_id=1, source_target_pairs={{0,28},{1,5},{2,30},{3,7},{4,0},{5,9},{6,2},{7,11},{8,4},{9,13},{1... | collective-permute-start | bytes 626696 | tf_op jit(solution)/shard_map/ppermute | solution.py:167
  31.9 17.8 %collective-permute-start.6 = (bf16[3,136,256]{2,1,0:T(8,128)(2,1)S(1)}, bf16[3,136,256]{2,1,0:T(8,128)(2,1)S(1)}, u32[]{:S(2)}, u32[]{:S(2)}) collective-permute-start(bf16[3,136,256]{2,1,0:T(8,128)(2,1)S(1)} %shard_map.55.refs_0_), channel_id=1, source_target_pairs={{0,4},{1,29},{2,6},{3,31},{4,8},{5,1},{6,10},{7,3},{8,12},{9,5},{1... | collective-permute-start | bytes 626696 | tf_op jit(solution)/shard_map/ppermute | solution.py:167
  37.4 24.6 %collective-permute-start.9 = (bf16[3,136,256]{2,1,0:T(8,128)(2,1)S(1)}, bf16[3,136,256]{2,1,0:T(8,128)(2,1)S(1)}, u32[]{:S(2)}, u32[]{:S(2)}) collective-permute-start(bf16[3,136,256]{2,1,0:T(8,128)(2,1)S(1)} %shard_map.55.refs_0_), channel_id=1, source_target_pairs={{0,30},{1,3},{2,0},{3,5},{4,2},{5,7},{6,4},{7,9},{8,6},{9,11},{10,... | collective-permute-start | bytes 626696 | tf_op jit(solution)/shard_map/ppermute | solution.py:167
  41.0 21.0 %collective-permute-start.10 = (bf16[3,136,256]{2,1,0:T(8,128)(2,1)S(1)}, bf16[3,136,256]{2,1,0:T(8,128)(2,1)S(1)}, u32[]{:S(2)}, u32[]{:S(2)}) collective-permute-start(bf16[3,136,256]{2,1,0:T(8,128)(2,1)S(1)} %shard_map.55.refs_0_), channel_id=1, source_target_pairs={{0,2},{1,31},{2,4},{3,1},{4,6},{5,3},{6,8},{7,5},{8,10},{9,7},{10,... | collective-permute-start | bytes 626696 | tf_op jit(solution)/shard_map/ppermute | solution.py:167
  43.9 15.4 %collective-permute-start.4 = (bf16[1,136,256]{2,1,0:T(8,128)(2,1)S(1)}, bf16[1,136,256]{2,1,0:T(8,128)(2,1)S(1)}, u32[]{:S(2)}, u32[]{:S(2)}) collective-permute-start(bf16[1,136,256]{2,1,0:T(8,128)(2,1)S(1)} %bitcast.10), channel_id=1, source_target_pairs={{0,26},{1,7},{2,28},{3,9},{4,30},{5,11},{6,0},{7,13},{8,2},{9,15},... | collective-permute-start | bytes 208904 | tf_op jit(solution)/shard_map/ppermute | solution.py:167
  53.1 26.4 %collective-permute-start.7 = (bf16[3,272,128]{2,1,0:T(8,128)(2,1)S(1)}, bf16[3,272,128]{2,1,0:T(8,128)(2,1)S(1)}, u32[]{:S(2)}, u32[]{:S(2)}) collective-permute-start(bf16[3,272,128]{2,1,0:T(8,128)(2,1)S(1)} %get-tuple-element.13.refs_2_), channel_id=1, source_target_pairs={{0,4},{1,29},{2,6},{3,31},{4,8},{5,1},{6,10},{7,3},{8,12},{9,5},{1... | collective-permute-start | bytes 626696 | tf_op jit(solution)/shard_map/ppermute | solution.py:167
  55.0 24.5 %collective-permute-start.8 = (bf16[3,272,128]{2,1,0:T(8,128)(2,1)S(1)}, bf16[3,272,128]{2,1,0:T(8,128)(2,1)S(1)}, u32[]{:S(2)}, u32[]{:S(2)}) collective-permute-start(bf16[3,272,128]{2,1,0:T(8,128)(2,1)S(1)} %get-tuple-element.15), channel_id=1, source_target_pairs={{0,28},{1,5},{2,30},{3,7},{4,0},{5,9},{6,2},{7,11},{8,4},{9,13},{1... | collective-permute-start | bytes 626696 | tf_op jit(solution)/shard_map/ppermute | solution.py:167
  65.3 14.2 %collective-permute-start.11 = (bf16[3,272,128]{2,1,0:T(8,128)(2,1)S(1)}, bf16[3,272,128]{2,1,0:T(8,128)(2,1)S(1)}, u32[]{:S(2)}, u32[]{:S(2)}) collective-permute-start(bf16[3,272,128]{2,1,0:T(8,128)(2,1)S(1)} %get-tuple-element.17), channel_id=1, source_target_pairs={{0,2},{1,31},{2,4},{3,1},{4,6},{5,3},{6,8},{7,5},{8,10},{9,7},{10,... | collective-permute-start | bytes 626696 | tf_op jit(solution)/shard_map/ppermute | solution.py:167
  69.9 10.3 %collective-permute-start.12 = (bf16[3,272,128]{2,1,0:T(8,128)(2,1)S(1)}, bf16[3,272,128]{2,1,0:T(8,128)(2,1)S(1)}, u32[]{:S(2)}, u32[]{:S(2)}) collective-permute-start(bf16[3,272,128]{2,1,0:T(8,128)(2,1)S(1)} %get-tuple-element.18), channel_id=1, source_target_pairs={{0,30},{1,3},{2,0},{3,5},{4,2},{5,7},{6,4},{7,9},{8,6},{9,11},{10,... | collective-permute-start | bytes 626696 | tf_op jit(solution)/shard_map/ppermute | solution.py:167
  71.9 7.6 %collective-permute-start.13 = (bf16[1,272,128]{2,1,0:T(8,128)(2,1)S(1)}, bf16[1,272,128]{2,1,0:T(8,128)(2,1)S(1)}, u32[]{:S(2)}, u32[]{:S(2)}) collective-permute-start(bf16[1,272,128]{2,1,0:T(8,128)(2,1)S(1)} %get-tuple-element.16.refs_2_), channel_id=1, source_target_pairs={{0,6},{1,27},{2,8},{3,29},{4,10},{5,31},{6,12},{7,1},{8,14},{9,3},... | collective-permute-start | bytes 208904 | tf_op jit(solution)/shard_map/ppermute | solution.py:167
  80.4 11.4 %collective-permute-start.14 = (bf16[272,128]{1,0:T(8,128)(2,1)S(1)}, bf16[272,128]{1,0:T(8,128)(2,1)S(1)}, u32[]{:S(2)}, u32[]{:S(2)}) collective-permute-start(bf16[272,128]{1,0:T(8,128)(2,1)S(1)} %get-tuple-element.19), channel_id=1, source_target_pairs={{0,10},{1,23},{2,12},{3,25},{4,14},{5,27},{6,16},{7,29},{8,18},{9,... | collective-permute-start | bytes 208904 | tf_op jit(solution)/shard_map/ppermute | solution.py:167
  89.9 11.2 %collective-permute-start.15 = (bf16[272,128]{1,0:T(8,128)(2,1)S(1)}, bf16[272,128]{1,0:T(8,128)(2,1)S(1)}, u32[]{:S(2)}, u32[]{:S(2)}) collective-permute-start(bf16[272,128]{1,0:T(8,128)(2,1)S(1)} %get-tuple-element.20), channel_id=1, source_target_pairs={{0,22},{1,11},{2,24},{3,13},{4,26},{5,15},{6,28},{7,17},{8,30},{9,... | collective-permute-start | bytes 208904 | tf_op jit(solution)/shard_map/ppermute | solution.py:167

commit v5 on v2

--- a/solution.py
+++ b/solution.py
@@ -12,6 +12,7 @@
 TAIL = 16
 VMEM = pl.BlockSpec(memory_space=pltpu.VMEM)
 SMEM = pl.BlockSpec(memory_space=pltpu.SMEM)
+ANY = pl.BlockSpec(memory_space=pl.ANY)
 PARAMS = pltpu.CompilerParams(vmem_limit_bytes=40 * 1024 * 1024)
 
 
@@ -28,7 +29,8 @@
     return tail[0:1] + tail[1:2] + tail[2:3]
 
 
-def attend_kernel(first_ref, x_ref, k0_ref, k1_ref, v0_ref, v1_ref, out_ref):
+def attend_kernel(first_ref, x_ref, k0_ref, k1_ref, v0_ref, v1_ref, *refs):
+    out_ref = refs[-1]
     sources, _, cand = out_ref.shape
     positions, width = k0_ref.shape
     nloc = positions // BLK
@@ -72,15 +74,29 @@
             out_ref[s + j, width:, :] = tail[:, j * cand : (j + 1) * cand]
 
 
-def attend(first, x, keys, vts, cand):
+def attend(first, x, keys, vts, cand, after=()):
     sources, _, width = x.shape
     return pl.pallas_call(
         attend_kernel,
-        in_specs=[SMEM] + [VMEM] * 5,
+        in_specs=[SMEM] + [VMEM] * 5 + [ANY] * len(after),
         out_specs=VMEM,
         out_shape=jax.ShapeDtypeStruct((sources, width + TAIL, cand), jnp.bfloat16),
         compiler_params=PARAMS,
-    )(first, x, *keys, *vts)
+    )(first, x, *keys, *vts, *after)
+
+
+def behind_kernel(x_ref, *refs):
+    refs[-1][...] = x_ref[...]
+
+
+def behind(x, others):
+    return pl.pallas_call(
+        behind_kernel,
+        in_specs=[VMEM] + [ANY] * len(others),
+        out_specs=VMEM,
+        out_shape=jax.ShapeDtypeStruct(x.shape, x.dtype),
+        compiler_params=PARAMS,
+    )(x, *others)
 
 
 def mix(blocks):
@@ -135,7 +151,7 @@
     cand, width = queries.shape
     nloc = hist_keys.shape[0] // BLK
     topk = block_dev.shape[1]
-    stride = 4
+    stride = 2
     members = chips // stride
 
     def shift(x, by):
@@ -160,14 +176,11 @@
     core = lax.axis_index("core").astype(jnp.int32)
     first = jnp.stack([here + core, here + 1 - core]) * nloc
 
-    steps = (lambda c: 2 - 4 * c, lambda c: 1, lambda c: -1)
-    others = [shift(own, by) for by in steps]
-    mine_part = attend(first, own, keys, vts, cand)
-    back = [
-        shift(attend(first, x, keys, vts, cand), lambda c, by=by: -by(c))
-        for x, by in zip(others, steps)
-    ]
-    merged = near_merge(mine_part, *back)
+    own = behind(own, (keys[1], vts[1]))
+    other = shift(own, lambda c: 1 - 2 * c)
+    own_part = attend(first, own, keys, vts, cand)
+    other_part = attend(first, other, keys, vts, cand, (own_part,))
+    merged = near_merge(own_part, shift(other_part, lambda c: 2 * c - 1))
     return far_merge(exchange(merged))
 
 

time: 104 us -> 116 us (1.12)
  blocking collectives: 23 us -> 38.6 us
  starting transfers between devices: 40.4 us -> 29 us
  waiting for transfers between devices: 25.6 us -> 36.5 us
  Pallas kernels: 12 us -> 8.8 us
    all_to_all x1, blocking collectives: 23 us -> 38.6 us  [exchange(): lax.all_to_all(x, ('z', 'core'), 0, 0, tiled=True, axis_index_groups=far)]
    ppermute x6 -> x2, starting transfers between devices: 21 us -> 9.45 us  [shift(): return lax.ppermute(x, ('z', 'core'), pairs)]
    all_to_all x1, waiting for transfers between devices: 14.2 us -> 21.5 us  [exchange(): lax.all_to_all(x, ('z', 'core'), 0, 0, tiled=True, axis_index_groups=far)]
    pallas_call x4 -> x3, Pallas kernels: 10.9 us -> 7.66 us  [the longest x2 7.63 us: attend(): pl.pallas_call(attend_kernel, in_specs=[SMEM] + [VMEM] * 5 + [ANY] * len(...]
    ppermute x6 -> x2, waiting for transfers between devices: 11.3 us -> 13.5 us  [shift(): return lax.ppermute(x, ('z', 'core'), pairs)]
    ppermute x1, waiting for transfers between devices: 0.01 us -> 1.5 us  [body(): keys = (hist_keys, lax.ppermute(hist_keys, 'core', swap))]
  transfers between devices with their start and end apart: 9 -> 5, of which waited for: 4 -> 4; matrix products, arithmetic and copies ran while one was open for 0% -> 0% of each run, Pallas kernels for 10% -> 3%
where the time goes in v5:
time: 116 us
  blocking collectives  38.6 us (33%)
  waiting for transfers between devices  36.5 us (31%)
  starting transfers between devices  29 us (25%)
  Pallas kernels  8.8 us (8%)
  other arithmetic  1.63 us (1%)
    all_to_all x1, blocking collectives, exchange(): lax.all_to_all(x, ('z', 'core'), 0, 0, tiled=True, axis_index_groups=far)  38.6 us
    all_to_all x1, waiting for transfers between devices, exchange(): lax.all_to_all(x, ('z', 'core'), 0, 0, tiled=True, axis_index_groups=far)  21.5 us
    all_to_all x1, starting transfers between devices, exchange(): lax.all_to_all(x, ('z', 'core'), 0, 0, tiled=True, axis_index_groups=far)  15.2 us
    ppermute x2, waiting for transfers between devices, shift(): return lax.ppermute(x, ('z', 'core'), pairs)  13.5 us
    ppermute x2, starting transfers between devices, shift(): return lax.ppermute(x, ('z', 'core'), pairs)  9.45 us
    pallas_call x2, Pallas kernels, attend(): pl.pallas_call(attend_kernel, in_specs=[SMEM] + [VMEM] * 5 + [ANY] * len(...  7.63 us
    ppermute x1, starting transfers between devices, body(): keys = (hist_keys, lax.ppermute(hist_keys, 'core', swap))  2.41 us
  transfers between devices with their start and end apart: 5, of which 4 were waited for; matrix products, arithmetic and copies ran while one was open for 0% of the time, Pallas kernels for 3%

profile of v5, /device:TPU:6, one launch (start us, length us, event | category | flops | bytes accessed | tf_op | source)
XLA Modules:
  0.0 115.7 jit_solution(7023699815302402030)
XLA Ops:
  0.0 0.7 fusion.2
  0.7 0.8 fusion.1
  1.6 0.8 broadcast_in_dim.2
  2.4 0.0 copy-start.1
  2.4 15.2 %all-to-all-start = ((bf16[8,136,256]{2,1,0:T(8,128)(2,1)}), bf16[8,136,256]{2,1,0:T(8,128)(2,1)S(1)}, u32[]{:S(2)}, u32[]{:S(2)}) async-start(bf16[8,136,256]{2,1,0:T(8,128)(2,1)} %broadcast_in_dim.2), calls=%async_computation | async-start | bytes 1114112 | tf_op jit(solution)/shard_map/all_to_all | solution.py:166
  17.6 0.0 copy-done.1
  17.6 0.0 copy-start
  17.6 0.2 copy.6
  17.9 1.9 %collective-permute-start.1 = (bf16[256,1024]{1,0:T(8,128)(2,1)S(1)}, bf16[256,1024]{1,0:T(8,128)(2,1)S(1)}, u32[]{:S(2)}, u32[]{:S(2)}) collective-permute-start(bf16[256,1024]{1,0:T(8,128)(2,1)S(1)} %bitcast.5), channel_id=1, source_target_pairs={{0,1},{1,0},{2,3},{3,2},{4,5},{5,4},{6,7},{7,6},{8,9},{9,8},{10,11... | collective-permute-start | bytes 1572872 | tf_op jit(solution)/shard_map/ppermute | solution.py:174
  19.8 0.0 copy-done
  19.8 2.4 %collective-permute-start = (bf16[1024,256]{1,0:T(8,128)(2,1)S(1)}, bf16[1024,256]{1,0:T(8,128)(2,1)S(1)}, u32[]{:S(2)}, u32[]{:S(2)}) collective-permute-start(bf16[1024,256]{1,0:T(8,128)(2,1)S(1)} %copy-done), channel_id=1, source_target_pairs={{0,1},{1,0},{2,3},{3,2},{4,5},{5,4},{6,7},{7,6},{8,9},{9,8},{10,11... | collective-permute-start | bytes 1572872 | tf_op jit(solution)/shard_map/ppermute | solution.py:173
  22.2 0.0 collective-permute-done.1.refs_1_.v1_ref
  22.2 1.5 %collective-permute-done.refs_0_.k1_ref = bf16[1024,256]{1,0:T(8,128)(2,1)S(1)} collective-permute-done((bf16[1024,256]{1,0:T(8,128)(2,1)S(1)}, bf16[1024,256]{1,0:T(8,128)(2,1)S(1)}, u32[]{:S(2)}, u32[]{:S(2)}) %collective-permute-start) | collective-permute-done | bytes 524320 | tf_op jit(solution)/shard_map/ppermute | solution.py:173
  23.7 21.5 %all-to-all-done.x_ref = bf16[8,136,256]{2,1,0:T(8,128)(2,1)S(1)} async-done(((bf16[8,136,256]{2,1,0:T(8,128)(2,1)}), bf16[8,136,256]{2,1,0:T(8,128)(2,1)S(1)}, u32[]{:S(2)}, u32[]{:S(2)}) %all-to-all-start) | async-done | bytes 557088 | tf_op jit(solution)/shard_map/all_to_all | solution.py:166
  45.2 3.8 %collective-permute-start.2 = (bf16[8,136,256]{2,1,0:T(8,128)(2,1)S(1)}, bf16[8,136,256]{2,1,0:T(8,128)(2,1)S(1)}, u32[]{:S(2)}, u32[]{:S(2)}) collective-permute-start(bf16[8,136,256]{2,1,0:T(8,128)(2,1)S(1)} %shard_map.55.x_ref), channel_id=1, source_target_pairs={{0,2},{1,31},{2,4},{3,1},{4,6},{5,3},{6,8},{7,5},{8,10},{9,7},{10,... | collective-permute-start | bytes 1671176 | tf_op jit(solution)/shard_map/ppermute | solution.py:161
  49.1 0.1 add_multiply_fusion.first_ref
  49.2 3.8 %shard_map.56.refs_0_ = bf16[8,272,128]{2,1,0:T(8,128)(2,1)S(1)} custom-call(s32[2]{0:T(128)S(1)} %add_multiply_fusion.first_ref, bf16[8,136,256]{2,1,0:T(8,128)(2,1)S(1)} %shard_map.55.x_ref, bf16[1024,256]{1,0:T(8,128)(2,1)S(1)} %copy-done, bf16[1024,256]{1,0:T(8,128)(2,1)S(1)} %collective-permute-done.refs_0_.k1_ref, bf16[256,1024]{1,0:T(8,128)(2,1)S(1)} %bitcast.6, ...), custom_call_target="tpu_custom_call" | custom-call | tf_op jit(solution)/shard_map/pallas_call | solution.py:79
  53.0 5.9 %collective-permute-done.2.x_ref = bf16[8,136,256]{2,1,0:T(8,128)(2,1)S(1)} collective-permute-done((bf16[8,136,256]{2,1,0:T(8,128)(2,1)S(1)}, bf16[8,136,256]{2,1,0:T(8,128)(2,1)S(1)}, u32[]{:S(2)}, u32[]{:S(2)}) %collective-permute-start.2) | collective-permute-done | bytes 557088 | tf_op jit(solution)/shard_map/ppermute | solution.py:161
  58.9 3.8 %shard_map.57 = bf16[8,272,128]{2,1,0:T(8,128)(2,1)S(1)} custom-call(s32[2]{0:T(128)S(1)} %add_multiply_fusion.first_ref, bf16[8,136,256]{2,1,0:T(8,128)(2,1)S(1)} %collective-permute-done.2.x_ref, bf16[1024,256]{1,0:T(8,128)(2,1)S(1)} %copy-done, bf16[1024,256]{1,0:T(8,128)(2,1)S(1)} %collective-permute-done.refs_0_.k1_ref, bf16[256,1024]{1,0:T(8,128)(2,1)S(1)} %bitcast.7, ...), custom_call_target="tpu_custom_call" | custom-call | tf_op jit(solution)/shard_map/pallas_call | solution.py:79
  62.7 5.6 %collective-permute-start.3 = (bf16[8,272,128]{2,1,0:T(8,128)(2,1)S(1)}, bf16[8,272,128]{2,1,0:T(8,128)(2,1)S(1)}, u32[]{:S(2)}, u32[]{:S(2)}) collective-permute-start(bf16[8,272,128]{2,1,0:T(8,128)(2,1)S(1)} %shard_map.57), channel_id=1, source_target_pairs={{0,30},{1,3},{2,0},{3,5},{4,2},{5,7},{6,4},{7,9},{8,6},{9,11},{10,... | collective-permute-start | bytes 1671176 | tf_op jit(solution)/shard_map/ppermute | solution.py:161
  68.4 7.6 %collective-permute-done.3.refs_1_ = bf16[8,272,128]{2,1,0:T(8,128)(2,1)S(1)} collective-permute-done((bf16[8,272,128]{2,1,0:T(8,128)(2,1)S(1)}, bf16[8,272,128]{2,1,0:T(8,128)(2,1)S(1)}, u32[]{:S(2)}, u32[]{:S(2)}) %collective-permute-start.3) | collective-permute-done | bytes 557088 | tf_op jit(solution)/shard_map/ppermute | solution.py:161
  75.9 0.3 shard_map.58
  76.2 38.6 %all_to_all.10.x_ref = bf16[8,272,128]{2,1,0:T(8,128)(2,1)S(1)} all-to-all(bf16[8,272,128]{2,1,0:T(8,128)(2,1)S(1)} %shard_map.58), channel_id=1, replica_groups={{0,4,8,12,16,20,24,28},{2,6,10,14,18,22,26,30},{1,5,9,13,17,21,25,29},{..., dimensions={0} | all-to-all | bytes 1114112 | tf_op jit(solution)/shard_map/all_to_all | solution.py:166
  114.9 0.8 shard_map.59
  (1 shorter events, 0.0 us)
Async XLA Ops:
  2.4 15.2 %copy-start.1 = (bf16[1024,256]{1,0:T(8,128)(2,1)S(1)}, bf16[1024,256]{1,0:T(8,128)(2,1)}, u32[]{:S(2)}) copy-start(bf16[1024,256]{1,0:T(8,128)(2,1)} %param.7) | copy-start | bytes 1572868
  2.4 42.8 %all-to-all-start = ((bf16[8,136,256]{2,1,0:T(8,128)(2,1)}), bf16[8,136,256]{2,1,0:T(8,128)(2,1)S(1)}, u32[]{:S(2)}, u32[]{:S(2)}) async-start(bf16[8,136,256]{2,1,0:T(8,128)(2,1)} %broadcast_in_dim.2), calls=%async_computation | async-start | bytes 1114112 | tf_op jit(solution)/shard_map/all_to_all | solution.py:166
  17.6 2.2 %copy-start = (bf16[1024,256]{1,0:T(8,128)(2,1)S(1)}, bf16[1024,256]{1,0:T(8,128)(2,1)}, u32[]{:S(2)}) copy-start(bf16[1024,256]{1,0:T(8,128)(2,1)} %k0_ref.3) | copy-start | bytes 1572868
  17.9 4.4 %collective-permute-start.1 = (bf16[256,1024]{1,0:T(8,128)(2,1)S(1)}, bf16[256,1024]{1,0:T(8,128)(2,1)S(1)}, u32[]{:S(2)}, u32[]{:S(2)}) collective-permute-start(bf16[256,1024]{1,0:T(8,128)(2,1)S(1)} %bitcast.5), channel_id=1, source_target_pairs={{0,1},{1,0},{2,3},{3,2},{4,5},{5,4},{6,7},{7,6},{8,9},{9,8},{10,11... | collective-permute-start | bytes 1572872 | tf_op jit(solution)/shard_map/ppermute | solution.py:174
  19.8 3.9 %collective-permute-start = (bf16[1024,256]{1,0:T(8,128)(2,1)S(1)}, bf16[1024,256]{1,0:T(8,128)(2,1)S(1)}, u32[]{:S(2)}, u32[]{:S(2)}) collective-permute-start(bf16[1024,256]{1,0:T(8,128)(2,1)S(1)} %copy-done), channel_id=1, source_target_pairs={{0,1},{1,0},{2,3},{3,2},{4,5},{5,4},{6,7},{7,6},{8,9},{9,8},{10,11... | collective-permute-start | bytes 1572872 | tf_op jit(solution)/shard_map/ppermute | solution.py:173
  45.2 13.7 %collective-permute-start.2 = (bf16[8,136,256]{2,1,0:T(8,128)(2,1)S(1)}, bf16[8,136,256]{2,1,0:T(8,128)(2,1)S(1)}, u32[]{:S(2)}, u32[]{:S(2)}) collective-permute-start(bf16[8,136,256]{2,1,0:T(8,128)(2,1)S(1)} %shard_map.55.x_ref), channel_id=1, source_target_pairs={{0,2},{1,31},{2,4},{3,1},{4,6},{5,3},{6,8},{7,5},{8,10},{9,7},{10,... | collective-permute-start | bytes 1671176 | tf_op jit(solution)/shard_map/ppermute | solution.py:161
  62.7 13.2 %collective-permute-start.3 = (bf16[8,272,128]{2,1,0:T(8,128)(2,1)S(1)}, bf16[8,272,128]{2,1,0:T(8,128)(2,1)S(1)}, u32[]{:S(2)}, u32[]{:S(2)}) collective-permute-start(bf16[8,272,128]{2,1,0:T(8,128)(2,1)S(1)} %shard_map.57), channel_id=1, source_target_pairs={{0,30},{1,3},{2,0},{3,5},{4,2},{5,7},{6,4},{7,9},{8,6},{9,11},{10,... | collective-permute-start | bytes 1671176 | tf_op jit(solution)/shard_map/ppermute | solution.py:161

commit v6 on v3

--- a/solution.py
+++ b/solution.py
@@ -12,7 +12,7 @@
 TAIL = 16
 VMEM = pl.BlockSpec(memory_space=pltpu.VMEM)
 SMEM = pl.BlockSpec(memory_space=pltpu.SMEM)
-PARAMS = pltpu.CompilerParams(vmem_limit_bytes=40 * 1024 * 1024)
+PARAMS = pltpu.CompilerParams(vmem_limit_bytes=20 * 1024 * 1024)
 
 
 def tail_rows(lse):
@@ -28,13 +28,14 @@
     return tail[0:1] + tail[1:2] + tail[2:3]
 
 
-def attend_kernel(stride, place_ref, xa_ref, xb_ref, k0_ref, k1_ref, v0_ref, v1_ref, out_ref):
+def attend_kernel(stride, place_ref, xa_ref, xb_ref, k_ref, v_ref, out_ref):
     members, _, cand = out_ref.shape
     rest = cand - xa_ref.shape[1]
-    positions, width = k0_ref.shape
+    _, positions, width = k_ref.shape
     nloc = positions // BLK
     scale = 1.0 / width**0.5
-    for s in range(0, members, 2):
+    def pair(p, carry):
+        s = 2 * p
         rows, ids = [], []
         for j in range(2):
             source = place_ref[0] + stride * (s + j)
@@ -44,12 +45,12 @@
         query = jnp.concatenate(rows, axis=0)
         ids = jnp.concatenate(ids, axis=1)
         parts, lses = [], []
-        for half, (k_ref, v_ref) in enumerate(((k0_ref, v0_ref), (k1_ref, v1_ref))):
-            near = ids - place_ref[1 + half].astype(jnp.float32)
+        for half in range(2):
+            near = ids - (place_ref[1] + half * nloc).astype(jnp.float32)
             inside = jnp.logical_and(near >= 0.0, near < nloc)
             sel = jnp.max(jnp.where(inside, near, -1.0), axis=0, keepdims=True)
             scores = lax.dot_general(
-                k_ref[...], query, (((1,), (1,)), ((), ())), preferred_element_type=jnp.float32
+                k_ref[half], query, (((1,), (1,)), ((), ())), preferred_element_type=jnp.float32
             )
             picked = scores[0:BLK]
             for b in range(1, nloc):
@@ -60,7 +61,7 @@
             spread = jnp.concatenate(
                 [jnp.where(sel == b, expo, 0.0).astype(jnp.bfloat16) for b in range(nloc)], axis=0
             )
-            summed = jnp.dot(v_ref[...], spread, preferred_element_type=jnp.float32)
+            summed = jnp.dot(v_ref[half], spread, preferred_element_type=jnp.float32)
             parts.append((summed / total).astype(jnp.bfloat16).astype(jnp.float32))
             lses.append(jnp.where(sel >= 0.0, peak * scale + jnp.log(total), NONE))
         top = jnp.maximum(lses[0], lses[1])
@@ -71,17 +72,20 @@
         for j in range(2):
             out_ref[s + j, :width, :] = merged[:, j * cand : (j + 1) * cand]
             out_ref[s + j, width:, :] = tail[:, j * cand : (j + 1) * cand]
+        return carry
+
+    lax.fori_loop(0, members // 2, pair, 0)
 
 
 def attend(place, xa, xb, keys, vts, cand, stride):
     chips, _, width = xa.shape
     return pl.pallas_call(
         functools.partial(attend_kernel, stride),
-        in_specs=[SMEM] + [VMEM] * 6,
+        in_specs=[SMEM] + [VMEM] * 4,
         out_specs=VMEM,
         out_shape=jax.ShapeDtypeStruct((chips // stride, width + TAIL, cand), jnp.bfloat16),
         compiler_params=PARAMS,
-    )(place, xa, xb, *keys, *vts)
+    )(place, xa, xb, keys, vts)
 
 
 def mix(blocks):
@@ -150,22 +154,20 @@
     def exchange(x):
         return lax.all_to_all(x, ("z", "core"), 0, 0, tiled=True, axis_index_groups=far)
 
-    swap = [(0, 1), (1, 0)]
+    keys = lax.all_gather(hist_keys, "core")
+    vts = lax.all_gather(hist_values.T, "core")
     ids = (block_dev * nloc + block_local).astype(jnp.bfloat16).T
-    rest = 8
+    rest = cand // 4
     small = jnp.concatenate([queries[cand - rest :], jnp.pad(ids, ((0, 0), (0, width - cand)))], axis=0)
     xb = lax.all_to_all(
         jnp.broadcast_to(small[None], (chips, rest + topk, width)), "z", 0, 0, tiled=True
     )
-    vt = hist_values.T
-    keys = (hist_keys, lax.ppermute(hist_keys, "core", swap))
-    vts = (vt, lax.ppermute(vt, "core", swap))
     xa = lax.all_gather(queries[: cand - rest], "z")
     z = lax.axis_index("z").astype(jnp.int32)
     core = lax.axis_index("core").astype(jnp.int32)
 
     def part(by):
-        place = [(z + by + chips) % stride, (2 * z + core) * nloc, (2 * z + 1 - core) * nloc]
+        place = [(z + by + chips) % stride, 2 * z * nloc]
         return attend(jnp.stack(place), xa, xb, keys, vts, cand, stride)
 
     steps = (lambda c: 2 - 4 * c, lambda c: 1, lambda c: -1)

time: 112 us -> 135 us (1.21)
  between operations: 0.17 us -> 13.6 us
  blocking collectives: 60.1 us -> 67.4 us
  Pallas kernels: 14.5 us -> 18.7 us
  starting transfers between devices: 28.8 us -> 25.8 us
    all_gather x1, blocking collectives: 35.5 us -> 43.4 us  [body(): xa = lax.all_gather(queries[:cand - rest], 'z')]
    ppermute x2 -> x0, starting transfers between devices: 4.33 us -> none  [the longest x1 2.41 us: body(): keys = (hist_keys, lax.ppermute(hist_keys, 'core', swap))]
    pallas_call x4, Pallas kernels: 12.3 us -> 16.5 us  [attend(): pl.pallas_call(functools.partial(attend_kernel, stride), in_specs=[SMEM]...]
    all_gather x0 -> x1, local copies, waits for them, and re-layouts: none -> 1.48 us  [body(): vts = lax.all_gather(hist_values.T, 'core')]
    unnamed x0 -> x2, waiting for transfers between devices: none -> 1.41 us
  transfers between devices with their start and end apart: 6 -> 6, of which waited for: 1 -> 1; matrix products, arithmetic and copies ran while one was open for 1% -> 2% of each run, Pallas kernels for 9% -> 10%
where the time goes in v6:
time: 135 us; the launch traced here: 134 us
  blocking collectives  67.4 us (50%)
  starting transfers between devices  25.8 us (19%)
  Pallas kernels  18.7 us (14%)
  between operations  13.6 us (10%)
  local copies, waits for them, and re-layouts  4.73 us (4%)
  waiting for transfers between devices  3.58 us (3%)
    all_gather x1, blocking collectives, body(): xa = lax.all_gather(queries[:cand - rest], 'z')  43.4 us
    all_to_all x1, blocking collectives, exchange(): lax.all_to_all(x, ('z', 'core'), 0, 0, tiled=True, axis_index_groups=far)  24 us
    pallas_call x4, Pallas kernels, attend(): pl.pallas_call(functools.partial(attend_kernel, stride), in_specs=[SMEM]...  16.5 us
    all_to_all x1, starting transfers between devices, body(): lax.all_to_all(jnp.broadcast_to(small[None], (chips, rest + topk, width))...  15.2 us
    ppermute x3, starting transfers between devices, shift(): return lax.ppermute(x, ('z', 'core'), pairs)  10.5 us
  transfers between devices with their start and end apart: 6, of which 1 were waited for; matrix products, arithmetic and copies ran while one was open for 2% of the time, Pallas kernels for 10%

profile of v6, /device:TPU:6, one launch (start us, length us, event | category | flops | bytes accessed | tf_op | source)
XLA Modules:
  0.0 134.1 jit_solution(8177951267021569535)
XLA Ops:
  6.5 0.7 all-gather.8.cloned.1.call-update
  7.3 0.7 copy-done.2
  8.0 0.8 broadcast_in_dim.2
  8.8 15.2 %all-to-all-start = ((bf16[16,40,256]{2,1,0:T(8,128)(2,1)}), bf16[16,40,256]{2,1,0:T(8,128)(2,1)S(1)}, u32[]{:S(2)}, u32[]{:S(2)}) async-start(bf16[16,40,256]{2,1,0:T(8,128)(2,1)} %broadcast_in_dim.2), calls=%async_computation | async-start | bytes 655360 | tf_op jit(solution)/shard_map/all_to_all | solution.py:162
  24.0 0.7 all-gather.6.cloned.1.call-update
  24.8 0.1 pad_add_fusion.1.place_ref
  24.8 0.1 pad_add_fusion.2.place_ref
  24.9 0.1 pad_add_fusion.3.place_ref
  25.0 0.5 slice-done.1
  25.5 43.4 %all-gather = bf16[1536,256]{1,0:T(8,128)(2,1)S(1)} all-gather(bf16[96,256]{1,0:T(8,128)(2,1)S(1)} %slice-done.1), channel_id=2, replica_groups=mesh['group'=16,'z'=16,'core'=2] {'z'}, dimensions={0}, use_global_device_ids=true | all-gather | bytes 835584 | tf_op jit(solution)/shard_map/all_gather | solution.py:165
  68.9 1.5 %copy.6 = bf16[512,1024]{1,0:T(8,128)(2,1)S(1)} copy(bf16[512,1024]{0,1:T(8,128)(2,1)} %all-gather.8.cloned.1.call-done) | data formatting | bytes 2097152 | tf_op jit(solution)/shard_map/all_gather | solution.py:158
  70.4 1.2 copy-done
  71.7 3.8 %shard_map.56 = bf16[4,272,128]{2,1,0:T(8,128)(2,1)S(1)} custom-call(s32[2]{0:T(128)S(1)} %pad_add_fusion.1.place_ref, bf16[16,96,256]{2,1,0:T(8,128)(2,1)S(1)} %bitcast.15, bf16[16,40,256]{2,1,0:T(8,128)(2,1)S(1)} %all-to-all-done.xb_ref, bf16[2,1024,256]{2,1,0:T(8,128)(2,1)S(1)} %bitcast.19, bf16[2,256,1024]{2,1,0:T(8,128)(2,1)S(1)} %bitcast.11), custom_call_target="tpu_custom_call" | custom-call | tf_op jit(solution)/shard_map/pallas_call | solution.py:82
  75.4 3.4 %collective-permute-start = (bf16[4,272,128]{2,1,0:T(8,128)(2,1)S(1)}, bf16[4,272,128]{2,1,0:T(8,128)(2,1)}, u32[]{:S(2)}, u32[]{:S(2)}) collective-permute-start(bf16[4,272,128]{2,1,0:T(8,128)(2,1)S(1)} %shard_map.56), channel_id=1, source_target_pairs={{0,4},{1,29},{2,6},{3,31},{4,8},{5,1},{6,10},{7,3},{8,12},{9,5},{1... | collective-permute-start | bytes 835592 | tf_op jit(solution)/shard_map/ppermute | solution.py:150
  78.8 4.5 %shard_map.57 = bf16[4,272,128]{2,1,0:T(8,128)(2,1)} custom-call(s32[2]{0:T(128)S(1)} %pad_add_fusion.2.place_ref, bf16[16,96,256]{2,1,0:T(8,128)(2,1)S(1)} %bitcast.16, bf16[16,40,256]{2,1,0:T(8,128)(2,1)S(1)} %all-to-all-done.xb_ref, bf16[2,1024,256]{2,1,0:T(8,128)(2,1)S(1)} %bitcast.20, bf16[2,256,1024]{2,1,0:T(8,128)(2,1)S(1)} %bitcast.12), custom_call_target="tpu_custom_call" | custom-call | tf_op jit(solution)/shard_map/pallas_call | solution.py:82
  83.3 2.9 %collective-permute-start.1 = (bf16[4,272,128]{2,1,0:T(8,128)(2,1)}, bf16[4,272,128]{2,1,0:T(8,128)(2,1)}, u32[]{:S(2)}, u32[]{:S(2)}) collective-permute-start(bf16[4,272,128]{2,1,0:T(8,128)(2,1)} %shard_map.57), channel_id=1, source_target_pairs={{0,2},{1,3},{2,4},{3,5},{4,6},{5,7},{6,8},{7,9},{8,10},{9,11},{10,... | collective-permute-start | bytes 835592 | tf_op jit(solution)/shard_map/ppermute | solution.py:150
  86.3 4.5 %shard_map.58 = bf16[4,272,128]{2,1,0:T(8,128)(2,1)} custom-call(s32[2]{0:T(128)S(1)} %pad_add_fusion.3.place_ref, bf16[16,96,256]{2,1,0:T(8,128)(2,1)S(1)} %bitcast.17, bf16[16,40,256]{2,1,0:T(8,128)(2,1)S(1)} %all-to-all-done.xb_ref, bf16[2,1024,256]{2,1,0:T(8,128)(2,1)S(1)} %bitcast.21, bf16[2,256,1024]{2,1,0:T(8,128)(2,1)S(1)} %bitcast.13), custom_call_target="tpu_custom_call" | custom-call | tf_op jit(solution)/shard_map/pallas_call | solution.py:82
  90.7 4.2 %collective-permute-start.2 = (bf16[4,272,128]{2,1,0:T(8,128)(2,1)}, bf16[4,272,128]{2,1,0:T(8,128)(2,1)}, u32[]{:S(2)}, u32[]{:S(2)}) collective-permute-start(bf16[4,272,128]{2,1,0:T(8,128)(2,1)} %shard_map.58), channel_id=1, source_target_pairs={{0,30},{1,31},{2,0},{3,1},{4,2},{5,3},{6,4},{7,5},{8,6},{9,7},{10,... | collective-permute-start | bytes 835592 | tf_op jit(solution)/shard_map/ppermute | solution.py:150
  95.0 0.1 pad_add_fusion.place_ref
  95.1 3.8 %shard_map.55.refs_0_ = bf16[4,272,128]{2,1,0:T(8,128)(2,1)S(1)} custom-call(s32[2]{0:T(128)S(1)} %pad_add_fusion.place_ref, bf16[16,96,256]{2,1,0:T(8,128)(2,1)S(1)} %bitcast.18, bf16[16,40,256]{2,1,0:T(8,128)(2,1)S(1)} %all-to-all-done.xb_ref, bf16[2,1024,256]{2,1,0:T(8,128)(2,1)S(1)} %bitcast.22, bf16[2,256,1024]{2,1,0:T(8,128)(2,1)S(1)} %bitcast.14), custom_call_target="tpu_custom_call" | custom-call | tf_op jit(solution)/shard_map/pallas_call | solution.py:82
  98.9 2.1 %collective-permute-done.2.refs_3_ = bf16[4,272,128]{2,1,0:T(8,128)(2,1)} collective-permute-done((bf16[4,272,128]{2,1,0:T(8,128)(2,1)}, bf16[4,272,128]{2,1,0:T(8,128)(2,1)}, u32[]{:S(2)}, u32[]{:S(2)}) %collective-permute-start.2) | collective-permute-done | bytes 278560 | tf_op jit(solution)/shard_map/ppermute | solution.py:150
  101.0 1.4 %shard_map.59 = bf16[4,272,128]{2,1,0:T(8,128)(2,1)S(1)} custom-call(bf16[4,272,128]{2,1,0:T(8,128)(2,1)S(1)} %shard_map.55.refs_0_, bf16[4,272,128]{2,1,0:T(8,128)(2,1)} %collective-permute-done.refs_1_, bf16[4,272,128]{2,1,0:T(8,128)(2,1)} %collective-permute-done.1.refs_2_, bf16[4,272,128]{2,1,0:T(8,128)(2,1)} %collective-permute-done.2.refs_3_), custom_call_target="tpu_custom_call" | custom-call | tf_op jit(solution)/shard_map/pallas_call | solution.py:114
  102.5 24.0 %all_to_all.10.x_ref = bf16[4,272,128]{2,1,0:T(8,128)(2,1)S(1)} all-to-all(bf16[4,272,128]{2,1,0:T(8,128)(2,1)S(1)} %shard_map.59), channel_id=1, replica_groups={{0,8,16,24},{2,10,18,26},{4,12,20,28},{6,14,22,30},{1,9,17,25},{3,11,19..., dimensions={0} | all-to-all | bytes 557056 | tf_op jit(solution)/shard_map/all_to_all | solution.py:155
  126.5 0.8 shard_map.60
  (18 shorter events, 0.2 us)
Async XLA Ops:
  6.5 62.4 %all-gather.8.cloned.1.call-start = ((), (), s32[]{:S(2)}) async-start(), calls=%async_computation.3 | async-start | bytes 1572864 | tf_op jit(solution)/shard_map/all_gather | solution.py:158
  7.3 0.7 copy-start.2
  7.3 0.7 copy-start.3
  7.3 0.7 slice-start
  8.8 61.7 %all-to-all-start = ((bf16[16,40,256]{2,1,0:T(8,128)(2,1)}), bf16[16,40,256]{2,1,0:T(8,128)(2,1)S(1)}, u32[]{:S(2)}, u32[]{:S(2)}) async-start(bf16[16,40,256]{2,1,0:T(8,128)(2,1)} %broadcast_in_dim.2), calls=%async_computation | async-start | bytes 655360 | tf_op jit(solution)/shard_map/all_to_all | solution.py:162
  24.0 46.5 %all-gather.6.cloned.1.call-start = ((), (), s32[]{:S(2)}) async-start(), calls=%async_computation.2 | async-start | bytes 1572864 | tf_op jit(solution)/shard_map/all_gather | solution.py:157
  24.7 0.8 slice-start.1
  70.4 1.2 copy-start
  75.4 23.4 %collective-permute-start = (bf16[4,272,128]{2,1,0:T(8,128)(2,1)S(1)}, bf16[4,272,128]{2,1,0:T(8,128)(2,1)}, u32[]{:S(2)}, u32[]{:S(2)}) collective-permute-start(bf16[4,272,128]{2,1,0:T(8,128)(2,1)S(1)} %shard_map.56), channel_id=1, source_target_pairs={{0,4},{1,29},{2,6},{3,31},{4,8},{5,1},{6,10},{7,3},{8,12},{9,5},{1... | collective-permute-start | bytes 835592 | tf_op jit(solution)/shard_map/ppermute | solution.py:150
  83.3 11.8 %copy-start.1 = (bf16[2048,256]{1,0:T(8,128)(2,1)S(1)}, bf16[2048,256]{1,0:T(8,128)(2,1)}, u32[]{:S(2)}) copy-start(bf16[2048,256]{1,0:T(8,128)(2,1)} %all-gather.6.cloned.1.call-done) | copy-start | bytes 3145732
  83.3 15.6 %collective-permute-start.1 = (bf16[4,272,128]{2,1,0:T(8,128)(2,1)}, bf16[4,272,128]{2,1,0:T(8,128)(2,1)}, u32[]{:S(2)}, u32[]{:S(2)}) collective-permute-start(bf16[4,272,128]{2,1,0:T(8,128)(2,1)} %shard_map.57), channel_id=1, source_target_pairs={{0,2},{1,3},{2,4},{3,5},{4,6},{5,7},{6,8},{7,9},{8,10},{9,11},{10,... | collective-permute-start | bytes 835592 | tf_op jit(solution)/shard_map/ppermute | solution.py:150
  90.7 10.3 %collective-permute-start.2 = (bf16[4,272,128]{2,1,0:T(8,128)(2,1)}, bf16[4,272,128]{2,1,0:T(8,128)(2,1)}, u32[]{:S(2)}, u32[]{:S(2)}) collective-permute-start(bf16[4,272,128]{2,1,0:T(8,128)(2,1)} %shard_map.58), channel_id=1, source_target_pairs={{0,30},{1,31},{2,0},{3,1},{4,2},{5,3},{6,4},{7,5},{8,6},{9,7},{10,... | collective-permute-start | bytes 835592 | tf_op jit(solution)/shard_map/ppermute | solution.py:150
Sparse Core Ops, SparseCore 0:
  9.4 23.8 all-gather.7
  35.4 20.8 all-gather.5

commit v7 on v4

--- a/solution.py
+++ b/solution.py
@@ -87,6 +87,24 @@
     )(first, *keys, *vts, *xs, *after)
 
 
+def halves_kernel(x_ref, *refs):
+    low_ref, high_ref = refs[-2:]
+    half = low_ref.shape[0]
+    low_ref[...] = x_ref[:half]
+    high_ref[...] = x_ref[half:]
+
+
+def halves(x, others):
+    shape = jax.ShapeDtypeStruct((x.shape[0] // 2,) + x.shape[1:], x.dtype)
+    return pl.pallas_call(
+        halves_kernel,
+        in_specs=[VMEM] + [ANY] * len(others),
+        out_specs=[VMEM] * 2,
+        out_shape=[shape] * 2,
+        compiler_params=PARAMS,
+    )(x, *others)
+
+
 def mix(blocks):
     width = blocks[0].shape[0] - TAIL
     lses = [lse_row(one[width:, :]) for one in blocks]
@@ -100,77 +118,65 @@
     return total, top + jnp.log(mixed)
 
 
-def stack_kernel(*refs):
-    out_ref = refs[-1]
+def near_kernel(low0_ref, high0_ref, low1_ref, high1_ref, out_ref):
+    half, rows, _ = low0_ref.shape
     for s in range(out_ref.shape[0]):
-        out_ref[s] = refs[s][...]
-
-
-def stack(blocks, after):
-    return pl.pallas_call(
-        stack_kernel,
-        in_specs=[VMEM] * len(blocks) + [ANY] * len(after),
+        refs = (low0_ref, low1_ref) if s < half else (high0_ref, high1_ref)
+        total, lse = mix([ref[s % half] for ref in refs])
+        out_ref[s, : rows - TAIL, :] = total.astype(jnp.bfloat16)
+        out_ref[s, rows - TAIL :, :] = tail_rows(lse)
+
+
+def near_merge(own, other):
+    half, rows, cand = own[0].shape
+    return pl.pallas_call(
+        near_kernel,
+        in_specs=[VMEM] * 4,
         out_specs=VMEM,
-        out_shape=jax.ShapeDtypeStruct((len(blocks),) + blocks[0].shape, blocks[0].dtype),
-        compiler_params=PARAMS,
-    )(*blocks, *after)
-
-
-def near_kernel(*refs):
-    *parts, extra, out1_ref, out2_ref = refs
-    width = out1_ref.shape[0] - TAIL
-    for slot, out_ref in ((1, out1_ref), (2, out2_ref)):
-        blocks = [ref[slot] for ref in parts] + ([extra[0]] if slot == 1 else [])
-        total, lse = mix(blocks)
-        out_ref[:width, :] = total.astype(jnp.bfloat16)
-        out_ref[width:, :] = tail_rows(lse)
-
-
-def near_merge(parts, extra):
-    shape = jax.ShapeDtypeStruct(extra.shape[1:], extra.dtype)
-    return pl.pallas_call(
-        near_kernel,
-        in_specs=[VMEM] * (len(parts) + 1),
-        out_specs=[VMEM] * 2,
-        out_shape=[shape] * 2,
-        compiler_params=PARAMS,
-    )(*parts, extra)
-
-
-def far_kernel(*refs):
-    *parts, one, two, out_ref = refs
-    total, _ = mix([ref[0] for ref in parts] + [one[...], two[...]])
+        out_shape=jax.ShapeDtypeStruct((2 * half, rows, cand), own[0].dtype),
+        compiler_params=PARAMS,
+    )(*own, *other)
+
+
+def far_kernel(x_ref, out_ref):
+    total, _ = mix([x_ref[s] for s in range(x_ref.shape[0])])
     out_ref[...] = total.T.astype(jnp.bfloat16)
 
 
-def far_merge(parts, one, two):
-    rows, cand = one.shape
+def far_merge(x):
+    _, rows, cand = x.shape
     return pl.pallas_call(
         far_kernel,
-        in_specs=[VMEM] * (len(parts) + 2),
+        in_specs=[VMEM],
         out_specs=VMEM,
         out_shape=jax.ShapeDtypeStruct((cand, rows - TAIL), jnp.bfloat16),
         compiler_params=PARAMS,
-    )(*parts, one, two)
+    )(x)
 
 
 def body(chips, queries, hist_keys, hist_values, block_dev, block_local):
     cand, width = queries.shape
     nloc = hist_keys.shape[0] // BLK
-
-    def shift(x, by):
+    topk = block_dev.shape[1]
+    group = [0, 1, 3, 5, 7, 10, 12, 14]
+    groups = [group, [z for z in range(chips) if z not in group]]
+    far = [[2 * ((z + c) % chips) + c for z in one] for c in range(2) for one in groups]
+
+    def partner(x):
         pairs = [
-            (2 * z + c, 2 * ((z + by * (1 - 2 * c)) % chips) + c)
+            (2 * z + c, 2 * ((z + (1 if (z + c) % 2 else -1)) % chips) + c)
             for z in range(chips)
             for c in range(2)
         ]
         return lax.ppermute(x, ("z", "core"), pairs)
 
+    def exchange(x):
+        return lax.all_to_all(x, ("z", "core"), 0, 0, tiled=True, axis_index_groups=far)
+
+    swap = [(0, 1), (1, 0)]
     ids = (block_dev * nloc + block_local).astype(jnp.bfloat16).T
     mine = jnp.concatenate([queries, jnp.pad(ids, ((0, 0), (0, width - cand)))], axis=0)
-    up5, down5 = shift(mine, -5), shift(mine, 5)
-
-    swap = [(0, 1), (1, 0)]
+    own = exchange(jnp.broadcast_to(mine[None], (len(group), cand + topk, width)))
     vt = hist_values.T
     keys = (hist_keys, lax.ppermute(hist_keys, "core", swap))
     vts = (vt, lax.ppermute(vt, "core", swap))
@@ -178,20 +184,11 @@
     core = lax.axis_index("core").astype(jnp.int32)
     first = jnp.stack([here + core, here + 1 - core]) * nloc
 
-    own = stack([mine, up5, down5], (keys[1], vts[1]))
-    up2, down2 = shift(own, -2), shift(own, 2)
-    eight = shift(up5[None], -3)
-    up1, down1 = shift(own, -1), shift(own, 1)
-
-    part_up2, part_down2 = attend(first, (up2, down2), keys, vts, cand)
-    back = [shift(part_up2, 2), shift(part_down2, -2)]
-    part_own, part_eight = attend(first, (own, eight), keys, vts, cand, (part_up2,))
-    extra = shift(part_eight, 3)
-    part_up1, part_down1 = attend(first, (up1, down1), keys, vts, cand, (part_eight,))
-    back += [shift(part_up1, 1), shift(part_down1, -1)]
-    parts = [part_own] + back
-    slot1, slot2 = near_merge(parts, extra)
-    return far_merge(parts, shift(slot1, 5), shift(slot2, -5))
+    own = halves(own, (keys[1], vts[1]))
+    other = [partner(x) for x in own]
+    back = [partner(attend(first, (x,), keys, vts, cand)[0]) for x in other]
+    merged = near_merge(attend(first, own, keys, vts, cand), back)
+    return far_merge(exchange(merged))
 
 
 def solution(mesh):

time: 103 us -> 111 us (1.078)
  the two profiles are of different devices: /device:TPU:1 before, /device:TPU:6 now
where the time goes in v7:
time: 111 us; the launch traced here: 109 us
  starting transfers between devices  38.7 us (35%)
  blocking collectives  33.8 us (30%)
  waiting for transfers between devices  23.5 us (21%)
  Pallas kernels  10.4 us (9%)
  other arithmetic  1.63 us (1%)
    all_to_all x1, blocking collectives, exchange(): lax.all_to_all(x, ('z', 'core'), 0, 0, tiled=True, axis_index_groups=far)  33.8 us
    ppermute x4, starting transfers between devices, partner(): return lax.ppermute(x, ('z', 'core'), pairs)  18.9 us
    all_to_all x1, waiting for transfers between devices, exchange(): lax.all_to_all(x, ('z', 'core'), 0, 0, tiled=True, axis_index_groups=far)  15.2 us
    all_to_all x1, starting transfers between devices, exchange(): lax.all_to_all(x, ('z', 'core'), 0, 0, tiled=True, axis_index_groups=far)  14.3 us
    pallas_call x3, Pallas kernels, attend(): pl.pallas_call(functools.partial(attend_kernel, counts), in_specs=[SMEM]...  9.25 us
    ppermute x4, waiting for transfers between devices, partner(): return lax.ppermute(x, ('z', 'core'), pairs)  6.39 us
    ppermute x1, starting transfers between devices, body(): vts = (vt, lax.ppermute(vt, 'core', swap))  3.53 us
  transfers between devices with their start and end apart: 7, of which 4 were waited for; matrix products, arithmetic and copies ran while one was open for 0% of the time, Pallas kernels for 8%

profile of v7, /device:TPU:6, one launch (start us, length us, event | category | flops | bytes accessed | tf_op | source)
XLA Modules:
  0.0 109.2 jit_solution(12941253137329681129)
XLA Ops:
  0.0 0.7 fusion.2
  0.7 0.8 fusion.1
  1.6 0.8 broadcast_in_dim.2
  2.4 14.3 %all-to-all-start = ((bf16[8,136,256]{2,1,0:T(8,128)(2,1)}), bf16[8,136,256]{2,1,0:T(8,128)(2,1)S(1)}, u32[]{:S(2)}, u32[]{:S(2)}) async-start(bf16[8,136,256]{2,1,0:T(8,128)(2,1)} %broadcast_in_dim.2), calls=%async_computation | async-start | bytes 1114112 | tf_op jit(solution)/shard_map/all_to_all | solution.py:174
  16.7 0.0 copy-start
  16.8 0.2 copy.6
  17.0 3.5 %collective-permute-start.1 = (bf16[256,1024]{1,0:T(8,128)(2,1)S(1)}, bf16[256,1024]{1,0:T(8,128)(2,1)S(1)}, u32[]{:S(2)}, u32[]{:S(2)}) collective-permute-start(bf16[256,1024]{1,0:T(8,128)(2,1)S(1)} %bitcast.5), channel_id=1, source_target_pairs={{0,1},{1,0},{2,3},{3,2},{4,5},{5,4},{6,7},{7,6},{8,9},{9,8},{10,11... | collective-permute-start | bytes 1572872 | tf_op jit(solution)/shard_map/ppermute | solution.py:182
  20.5 1.9 %collective-permute-start = (bf16[1024,256]{1,0:T(8,128)(2,1)S(1)}, bf16[1024,256]{1,0:T(8,128)(2,1)S(1)}, u32[]{:S(2)}, u32[]{:S(2)}) collective-permute-start(bf16[1024,256]{1,0:T(8,128)(2,1)S(1)} %copy-done), channel_id=1, source_target_pairs={{0,1},{1,0},{2,3},{3,2},{4,5},{5,4},{6,7},{7,6},{8,9},{9,8},{10,11... | collective-permute-start | bytes 1572872 | tf_op jit(solution)/shard_map/ppermute | solution.py:181
  22.4 0.0 collective-permute-done.1.refs_1_.v1_ref
  22.4 1.9 %collective-permute-done.refs_0_.k1_ref = bf16[1024,256]{1,0:T(8,128)(2,1)S(1)} collective-permute-done((bf16[1024,256]{1,0:T(8,128)(2,1)S(1)}, bf16[1024,256]{1,0:T(8,128)(2,1)S(1)}, u32[]{:S(2)}, u32[]{:S(2)}) %collective-permute-start) | collective-permute-done | bytes 524320 | tf_op jit(solution)/shard_map/ppermute | solution.py:181
  24.3 15.2 %all-to-all-done.x_ref = bf16[8,136,256]{2,1,0:T(8,128)(2,1)S(1)} async-done(((bf16[8,136,256]{2,1,0:T(8,128)(2,1)}), bf16[8,136,256]{2,1,0:T(8,128)(2,1)S(1)}, u32[]{:S(2)}, u32[]{:S(2)}) %all-to-all-start) | async-done | bytes 557088 | tf_op jit(solution)/shard_map/all_to_all | solution.py:174
  39.6 9.9 %collective-permute-start.4 = (bf16[4,136,256]{2,1,0:T(8,128)(2,1)S(1)}, bf16[4,136,256]{2,1,0:T(8,128)(2,1)S(1)}, u32[]{:S(2)}, u32[]{:S(2)}) collective-permute-start(bf16[4,136,256]{2,1,0:T(8,128)(2,1)S(1)} %get-tuple-element.10.refs_1_), channel_id=1, source_target_pairs={{0,30},{1,3},{2,4},{3,1},{4,2},{5,7},{6,8},{7,5},{8,6},{9,11},{10,... | collective-permute-start | bytes 835592 | tf_op jit(solution)/shard_map/ppermute | solution.py:171
  49.5 1.9 %collective-permute-start.2 = (bf16[4,136,256]{2,1,0:T(8,128)(2,1)S(1)}, bf16[4,136,256]{2,1,0:T(8,128)(2,1)S(1)}, u32[]{:S(2)}, u32[]{:S(2)}) collective-permute-start(bf16[4,136,256]{2,1,0:T(8,128)(2,1)S(1)} %get-tuple-element.9.refs_0_), channel_id=1, source_target_pairs={{0,30},{1,3},{2,4},{3,1},{4,2},{5,7},{6,8},{7,5},{8,6},{9,11},{10,... | collective-permute-start | bytes 835592 | tf_op jit(solution)/shard_map/ppermute | solution.py:171
  51.4 0.1 add_multiply_fusion.first_ref
  51.5 2.5 %collective-permute-done.4.refs_0_ = bf16[4,136,256]{2,1,0:T(8,128)(2,1)S(1)} collective-permute-done((bf16[4,136,256]{2,1,0:T(8,128)(2,1)S(1)}, bf16[4,136,256]{2,1,0:T(8,128)(2,1)S(1)}, u32[]{:S(2)}, u32[]{:S(2)}) %collective-permute-start.4) | collective-permute-done | bytes 278560 | tf_op jit(solution)/shard_map/ppermute | solution.py:171
  54.0 2.7 %shard_map.58 = bf16[4,272,128]{2,1,0:T(8,128)(2,1)S(1)} custom-call(s32[2]{0:T(128)S(1)} %add_multiply_fusion.first_ref, bf16[1024,256]{1,0:T(8,128)(2,1)S(1)} %copy-done, bf16[1024,256]{1,0:T(8,128)(2,1)S(1)} %collective-permute-done.refs_0_.k1_ref, bf16[256,1024]{1,0:T(8,128)(2,1)S(1)} %bitcast.6, ...), custom_call_target="tpu_custom_call" | custom-call | tf_op jit(solution)/shard_map/pallas_call | solution.py:81
  56.7 5.1 %collective-permute-start.5 = (bf16[4,272,128]{2,1,0:T(8,128)(2,1)S(1)}, bf16[4,272,128]{2,1,0:T(8,128)(2,1)S(1)}, u32[]{:S(2)}, u32[]{:S(2)}) collective-permute-start(bf16[4,272,128]{2,1,0:T(8,128)(2,1)S(1)} %shard_map.58), channel_id=1, source_target_pairs={{0,30},{1,3},{2,4},{3,1},{4,2},{5,7},{6,8},{7,5},{8,6},{9,11},{10,... | collective-permute-start | bytes 835592 | tf_op jit(solution)/shard_map/ppermute | solution.py:171
  61.9 2.7 %shard_map.57 = bf16[4,272,128]{2,1,0:T(8,128)(2,1)S(1)} custom-call(s32[2]{0:T(128)S(1)} %add_multiply_fusion.first_ref, bf16[1024,256]{1,0:T(8,128)(2,1)S(1)} %copy-done, bf16[1024,256]{1,0:T(8,128)(2,1)S(1)} %collective-permute-done.refs_0_.k1_ref, bf16[256,1024]{1,0:T(8,128)(2,1)S(1)} %bitcast.7, ...), custom_call_target="tpu_custom_call" | custom-call | tf_op jit(solution)/shard_map/pallas_call | solution.py:81
  64.6 1.9 %collective-permute-start.3 = (bf16[4,272,128]{2,1,0:T(8,128)(2,1)S(1)}, bf16[4,272,128]{2,1,0:T(8,128)(2,1)S(1)}, u32[]{:S(2)}, u32[]{:S(2)}) collective-permute-start(bf16[4,272,128]{2,1,0:T(8,128)(2,1)S(1)} %shard_map.57), channel_id=1, source_target_pairs={{0,30},{1,3},{2,4},{3,1},{4,2},{5,7},{6,8},{7,5},{8,6},{9,11},{10,... | collective-permute-start | bytes 835592 | tf_op jit(solution)/shard_map/ppermute | solution.py:171
  66.5 3.8 %shard_map.56 = (bf16[4,272,128]{2,1,0:T(8,128)(2,1)S(1)}, bf16[4,272,128]{2,1,0:T(8,128)(2,1)S(1)}) custom-call(s32[2]{0:T(128)S(1)} %add_multiply_fusion.first_ref, bf16[1024,256]{1,0:T(8,128)(2,1)S(1)} %copy-done, bf16[1024,256]{1,0:T(8,128)(2,1)S(1)} %collective-permute-done.refs_0_.k1_ref, bf16[256,1024]{1,0:T(8,128)(2,1)S(1)} %bitcast.8, ...), custom_call_target="tpu_custom_call" | custom-call | tf_op jit(solution)/shard_map/pallas_call | solution.py:81
  70.4 3.9 %collective-permute-done.3.low1_ref = bf16[4,272,128]{2,1,0:T(8,128)(2,1)S(1)} collective-permute-done((bf16[4,272,128]{2,1,0:T(8,128)(2,1)S(1)}, bf16[4,272,128]{2,1,0:T(8,128)(2,1)S(1)}, u32[]{:S(2)}, u32[]{:S(2)}) %collective-permute-start.3) | collective-permute-done | bytes 278560 | tf_op jit(solution)/shard_map/ppermute | solution.py:171
  74.2 0.3 shard_map.59
  74.5 33.8 %all_to_all.10.x_ref = bf16[8,272,128]{2,1,0:T(8,128)(2,1)S(1)} all-to-all(bf16[8,272,128]{2,1,0:T(8,128)(2,1)S(1)} %shard_map.59), channel_id=1, replica_groups={{0,2,6,10,14,20,24,28},{4,8,12,16,18,22,26,30},{3,5,9,13,17,23,27,31},{..., dimensions={0} | all-to-all | bytes 1114112 | tf_op jit(solution)/shard_map/all_to_all | solution.py:174
  108.4 0.8 shard_map.60
  (6 shorter events, 0.0 us)
Async XLA Ops:
  2.4 14.3 %copy-start.1 = (bf16[1024,256]{1,0:T(8,128)(2,1)S(1)}, bf16[1024,256]{1,0:T(8,128)(2,1)}, u32[]{:S(2)}) copy-start(bf16[1024,256]{1,0:T(8,128)(2,1)} %param.7) | copy-start | bytes 1572868
  2.4 37.1 %all-to-all-start = ((bf16[8,136,256]{2,1,0:T(8,128)(2,1)}), bf16[8,136,256]{2,1,0:T(8,128)(2,1)S(1)}, u32[]{:S(2)}, u32[]{:S(2)}) async-start(bf16[8,136,256]{2,1,0:T(8,128)(2,1)} %broadcast_in_dim.2), calls=%async_computation | async-start | bytes 1114112 | tf_op jit(solution)/shard_map/all_to_all | solution.py:174
  16.7 3.8 %copy-start = (bf16[1024,256]{1,0:T(8,128)(2,1)S(1)}, bf16[1024,256]{1,0:T(8,128)(2,1)}, u32[]{:S(2)}) copy-start(bf16[1024,256]{1,0:T(8,128)(2,1)} %k0_ref.5) | copy-start | bytes 1572868
  17.0 5.5 %collective-permute-start.1 = (bf16[256,1024]{1,0:T(8,128)(2,1)S(1)}, bf16[256,1024]{1,0:T(8,128)(2,1)S(1)}, u32[]{:S(2)}, u32[]{:S(2)}) collective-permute-start(bf16[256,1024]{1,0:T(8,128)(2,1)S(1)} %bitcast.5), channel_id=1, source_target_pairs={{0,1},{1,0},{2,3},{3,2},{4,5},{5,4},{6,7},{7,6},{8,9},{9,8},{10,11... | collective-permute-start | bytes 1572872 | tf_op jit(solution)/shard_map/ppermute | solution.py:182
  20.5 3.8 %collective-permute-start = (bf16[1024,256]{1,0:T(8,128)(2,1)S(1)}, bf16[1024,256]{1,0:T(8,128)(2,1)S(1)}, u32[]{:S(2)}, u32[]{:S(2)}) collective-permute-start(bf16[1024,256]{1,0:T(8,128)(2,1)S(1)} %copy-done), channel_id=1, source_target_pairs={{0,1},{1,0},{2,3},{3,2},{4,5},{5,4},{6,7},{7,6},{8,9},{9,8},{10,11... | collective-permute-start | bytes 1572872 | tf_op jit(solution)/shard_map/ppermute | solution.py:181
  39.6 14.4 %collective-permute-start.4 = (bf16[4,136,256]{2,1,0:T(8,128)(2,1)S(1)}, bf16[4,136,256]{2,1,0:T(8,128)(2,1)S(1)}, u32[]{:S(2)}, u32[]{:S(2)}) collective-permute-start(bf16[4,136,256]{2,1,0:T(8,128)(2,1)S(1)} %get-tuple-element.10.refs_1_), channel_id=1, source_target_pairs={{0,30},{1,3},{2,4},{3,1},{4,2},{5,7},{6,8},{7,5},{8,6},{9,11},{10,... | collective-permute-start | bytes 835592 | tf_op jit(solution)/shard_map/ppermute | solution.py:171
  49.5 12.4 %collective-permute-start.2 = (bf16[4,136,256]{2,1,0:T(8,128)(2,1)S(1)}, bf16[4,136,256]{2,1,0:T(8,128)(2,1)S(1)}, u32[]{:S(2)}, u32[]{:S(2)}) collective-permute-start(bf16[4,136,256]{2,1,0:T(8,128)(2,1)S(1)} %get-tuple-element.9.refs_0_), channel_id=1, source_target_pairs={{0,30},{1,3},{2,4},{3,1},{4,2},{5,7},{6,8},{7,5},{8,6},{9,11},{10,... | collective-permute-start | bytes 835592 | tf_op jit(solution)/shard_map/ppermute | solution.py:171
  56.7 13.6 %collective-permute-start.5 = (bf16[4,272,128]{2,1,0:T(8,128)(2,1)S(1)}, bf16[4,272,128]{2,1,0:T(8,128)(2,1)S(1)}, u32[]{:S(2)}, u32[]{:S(2)}) collective-permute-start(bf16[4,272,128]{2,1,0:T(8,128)(2,1)S(1)} %shard_map.58), channel_id=1, source_target_pairs={{0,30},{1,3},{2,4},{3,1},{4,2},{5,7},{6,8},{7,5},{8,6},{9,11},{10,... | collective-permute-start | bytes 835592 | tf_op jit(solution)/shard_map/ppermute | solution.py:171
  64.6 9.7 %collective-permute-start.3 = (bf16[4,272,128]{2,1,0:T(8,128)(2,1)S(1)}, bf16[4,272,128]{2,1,0:T(8,128)(2,1)S(1)}, u32[]{:S(2)}, u32[]{:S(2)}) collective-permute-start(bf16[4,272,128]{2,1,0:T(8,128)(2,1)S(1)} %shard_map.57), channel_id=1, source_target_pairs={{0,30},{1,3},{2,4},{3,1},{4,2},{5,7},{6,8},{7,5},{8,6},{9,11},{10,... | collective-permute-start | bytes 835592 | tf_op jit(solution)/shard_map/ppermute | solution.py:171

commit v8 on v4

--- a/solution.py
+++ b/solution.py
@@ -100,22 +100,6 @@
     return total, top + jnp.log(mixed)
 
 
-def stack_kernel(*refs):
-    out_ref = refs[-1]
-    for s in range(out_ref.shape[0]):
-        out_ref[s] = refs[s][...]
-
-
-def stack(blocks, after):
-    return pl.pallas_call(
-        stack_kernel,
-        in_specs=[VMEM] * len(blocks) + [ANY] * len(after),
-        out_specs=VMEM,
-        out_shape=jax.ShapeDtypeStruct((len(blocks),) + blocks[0].shape, blocks[0].dtype),
-        compiler_params=PARAMS,
-    )(*blocks, *after)
-
-
 def near_kernel(*refs):
     *parts, extra, out1_ref, out2_ref = refs
     width = out1_ref.shape[0] - TAIL
@@ -178,7 +162,7 @@
     core = lax.axis_index("core").astype(jnp.int32)
     first = jnp.stack([here + core, here + 1 - core]) * nloc
 
-    own = stack([mine, up5, down5], (keys[1], vts[1]))
+    own = jnp.stack([mine, up5, down5])
     up2, down2 = shift(own, -2), shift(own, 2)
     eight = shift(up5[None], -3)
     up1, down1 = shift(own, -1), shift(own, 1)

time: 103 us -> 105 us (1.019)
  the two profiles are of different devices: /device:TPU:1 before, /device:TPU:6 now
where the time goes in v8:
time: 105 us; the launch traced here: 104 us
  starting transfers between devices  75.6 us (72%)
  waiting for transfers between devices  14.4 us (14%)
  Pallas kernels  10.3 us (10%)
  other arithmetic  1.66 us (2%)
  local copies, waits for them, and re-layouts  1.25 us (1%)
    ppermute x14, starting transfers between devices, shift(): return lax.ppermute(x, ('z', 'core'), pairs)  71.3 us
    ppermute x14, waiting for transfers between devices, shift(): return lax.ppermute(x, ('z', 'core'), pairs)  14.4 us
    pallas_call x3, Pallas kernels, attend(): pl.pallas_call(functools.partial(attend_kernel, counts), in_specs=[SMEM]...  9.26 us
    ppermute x1, starting transfers between devices, body(): vts = (vt, lax.ppermute(vt, 'core', swap))  2.41 us
  transfers between devices with their start and end apart: 16, of which 4 were waited for; matrix products, arithmetic and copies ran while one was open for 1% of the time, Pallas kernels for 9%

profile of v8, /device:TPU:6, one launch (start us, length us, event | category | flops | bytes accessed | tf_op | source)
XLA Modules:
  0.0 103.6 jit_solution(8272402631306024228)
XLA Ops:
  0.7 0.8 fusion.3
  1.6 10.6 %collective-permute-start.3 = (bf16[136,256]{1,0:T(8,128)(2,1)S(1)}, bf16[136,256]{1,0:T(8,128)(2,1)S(1)}, u32[]{:S(2)}, u32[]{:S(2)}) collective-permute-start(bf16[136,256]{1,0:T(8,128)(2,1)S(1)} %get-tuple-element.22), channel_id=1, source_target_pairs={{0,10},{1,23},{2,12},{3,25},{4,14},{5,27},{6,16},{7,29},{8,18},{9,... | collective-permute-start | bytes 208904 | tf_op jit(solution)/shard_map/ppermute | solution.py:151
  12.2 5.9 %collective-permute-start.2 = (bf16[136,256]{1,0:T(8,128)(2,1)S(1)}, bf16[136,256]{1,0:T(8,128)(2,1)S(1)}, u32[]{:S(2)}, u32[]{:S(2)}) collective-permute-start(bf16[136,256]{1,0:T(8,128)(2,1)S(1)} %get-tuple-element.22), channel_id=1, source_target_pairs={{0,22},{1,11},{2,24},{3,13},{4,26},{5,15},{6,28},{7,17},{8,30},{9,... | collective-permute-start | bytes 208904 | tf_op jit(solution)/shard_map/ppermute | solution.py:151
  18.0 1.9 %collective-permute-start = (bf16[1024,256]{1,0:T(8,128)(2,1)}, bf16[1024,256]{1,0:T(8,128)(2,1)S(1)}, u32[]{:S(2)}, u32[]{:S(2)}) collective-permute-start(bf16[1024,256]{1,0:T(8,128)(2,1)} %k0_ref.5), channel_id=1, source_target_pairs={{0,1},{1,0},{2,3},{3,2},{4,5},{5,4},{6,7},{7,6},{8,9},{9,8},{10,11... | collective-permute-start | bytes 1572872 | tf_op jit(solution)/shard_map/ppermute | solution.py:159
  20.0 1.2 %copy.6 = bf16[1024,256]{0,1:T(8,128)(2,1)S(1)} copy(bf16[1024,256]{1,0:T(8,128)(2,1)} %param.7) | data formatting | bytes 1048576 | tf_op args[2]
  21.2 2.4 %collective-permute-start.1 = (bf16[256,1024]{1,0:T(8,128)(2,1)S(1)}, bf16[256,1024]{1,0:T(8,128)(2,1)S(1)}, u32[]{:S(2)}, u32[]{:S(2)}) collective-permute-start(bf16[256,1024]{1,0:T(8,128)(2,1)S(1)} %bitcast.9), channel_id=1, source_target_pairs={{0,1},{1,0},{2,3},{3,2},{4,5},{5,4},{6,7},{7,6},{8,9},{9,8},{10,11... | collective-permute-start | bytes 1572872 | tf_op jit(solution)/shard_map/ppermute | solution.py:160
  23.7 6.2 %collective-permute-start.5 = (bf16[3,136,256]{2,1,0:T(8,128)(2,1)S(1)}, bf16[3,136,256]{2,1,0:T(8,128)(2,1)S(1)}, u32[]{:S(2)}, u32[]{:S(2)}) collective-permute-start(bf16[3,136,256]{2,1,0:T(8,128)(2,1)S(1)} %pad_maximum_fusion.refs_0_), channel_id=1, source_target_pairs={{0,28},{1,5},{2,30},{3,7},{4,0},{5,9},{6,2},{7,11},{8,4},{9,13},{1... | collective-permute-start | bytes 626696 | tf_op jit(solution)/shard_map/ppermute | solution.py:151
  29.9 1.9 %collective-permute-start.6 = (bf16[3,136,256]{2,1,0:T(8,128)(2,1)S(1)}, bf16[3,136,256]{2,1,0:T(8,128)(2,1)S(1)}, u32[]{:S(2)}, u32[]{:S(2)}) collective-permute-start(bf16[3,136,256]{2,1,0:T(8,128)(2,1)S(1)} %pad_maximum_fusion.refs_0_), channel_id=1, source_target_pairs={{0,4},{1,29},{2,6},{3,31},{4,8},{5,1},{6,10},{7,3},{8,12},{9,5},{1... | collective-permute-start | bytes 626696 | tf_op jit(solution)/shard_map/ppermute | solution.py:151
  31.8 5.6 %collective-permute-start.9 = (bf16[3,136,256]{2,1,0:T(8,128)(2,1)S(1)}, bf16[3,136,256]{2,1,0:T(8,128)(2,1)S(1)}, u32[]{:S(2)}, u32[]{:S(2)}) collective-permute-start(bf16[3,136,256]{2,1,0:T(8,128)(2,1)S(1)} %pad_maximum_fusion.refs_0_), channel_id=1, source_target_pairs={{0,30},{1,3},{2,0},{3,5},{4,2},{5,7},{6,4},{7,9},{8,6},{9,11},{10,... | collective-permute-start | bytes 626696 | tf_op jit(solution)/shard_map/ppermute | solution.py:151
  37.6 8.7 %collective-permute-start.10 = (bf16[3,136,256]{2,1,0:T(8,128)(2,1)S(1)}, bf16[3,136,256]{2,1,0:T(8,128)(2,1)S(1)}, u32[]{:S(2)}, u32[]{:S(2)}) collective-permute-start(bf16[3,136,256]{2,1,0:T(8,128)(2,1)S(1)} %pad_maximum_fusion.refs_0_), channel_id=1, source_target_pairs={{0,2},{1,31},{2,4},{3,1},{4,6},{5,3},{6,8},{7,5},{8,10},{9,7},{10,... | collective-permute-start | bytes 626696 | tf_op jit(solution)/shard_map/ppermute | solution.py:151
  46.3 2.0 %collective-permute-start.4 = (bf16[1,136,256]{2,1,0:T(8,128)(2,1)S(1)}, bf16[1,136,256]{2,1,0:T(8,128)(2,1)S(1)}, u32[]{:S(2)}, u32[]{:S(2)}) collective-permute-start(bf16[1,136,256]{2,1,0:T(8,128)(2,1)S(1)} %bitcast.14), channel_id=1, source_target_pairs={{0,26},{1,7},{2,28},{3,9},{4,30},{5,11},{6,0},{7,13},{8,2},{9,15},... | collective-permute-start | bytes 208904 | tf_op jit(solution)/shard_map/ppermute | solution.py:151
  48.4 3.3 %shard_map.55 = (bf16[3,272,128]{2,1,0:T(8,128)(2,1)S(1)}, bf16[3,272,128]{2,1,0:T(8,128)(2,1)S(1)}) custom-call(s32[2]{0:T(128)S(1)} %add_multiply_fusion.first_ref, bf16[1024,256]{1,0:T(8,128)(2,1)S(1)} %copy-done, bf16[1024,256]{1,0:T(8,128)(2,1)S(1)} %collective-permute-done.k1_ref, bf16[256,1024]{1,0:T(8,128)(2,1)S(1)} %bitcast.10, ...), custom_call_target="tpu_custom_call" | custom-call | tf_op jit(solution)/shard_map/pallas_call | solution.py:81
  51.7 3.6 %collective-permute-start.7 = (bf16[3,272,128]{2,1,0:T(8,128)(2,1)S(1)}, bf16[3,272,128]{2,1,0:T(8,128)(2,1)S(1)}, u32[]{:S(2)}, u32[]{:S(2)}) collective-permute-start(bf16[3,272,128]{2,1,0:T(8,128)(2,1)S(1)} %get-tuple-element.13.refs_2_), channel_id=1, source_target_pairs={{0,4},{1,29},{2,6},{3,31},{4,8},{5,1},{6,10},{7,3},{8,12},{9,5},{1... | collective-permute-start | bytes 626696 | tf_op jit(solution)/shard_map/ppermute | solution.py:151
  55.3 4.4 %collective-permute-start.8 = (bf16[3,272,128]{2,1,0:T(8,128)(2,1)S(1)}, bf16[3,272,128]{2,1,0:T(8,128)(2,1)S(1)}, u32[]{:S(2)}, u32[]{:S(2)}) collective-permute-start(bf16[3,272,128]{2,1,0:T(8,128)(2,1)S(1)} %get-tuple-element.15), channel_id=1, source_target_pairs={{0,28},{1,5},{2,30},{3,7},{4,0},{5,9},{6,2},{7,11},{8,4},{9,13},{1... | collective-permute-start | bytes 626696 | tf_op jit(solution)/shard_map/ppermute | solution.py:151
  59.7 2.7 %shard_map.56 = (bf16[3,272,128]{2,1,0:T(8,128)(2,1)S(1)}, bf16[1,272,128]{2,1,0:T(8,128)(2,1)S(1)}) custom-call(s32[2]{0:T(128)S(1)} %add_multiply_fusion.first_ref, bf16[1024,256]{1,0:T(8,128)(2,1)S(1)} %copy-done, bf16[1024,256]{1,0:T(8,128)(2,1)S(1)} %collective-permute-done.k1_ref, bf16[256,1024]{1,0:T(8,128)(2,1)S(1)} %bitcast.11, ...), custom_call_target="tpu_custom_call" | custom-call | tf_op jit(solution)/shard_map/pallas_call | solution.py:81
  62.4 3.3 %shard_map.57 = (bf16[3,272,128]{2,1,0:T(8,128)(2,1)S(1)}, bf16[3,272,128]{2,1,0:T(8,128)(2,1)S(1)}) custom-call(s32[2]{0:T(128)S(1)} %add_multiply_fusion.first_ref, bf16[1024,256]{1,0:T(8,128)(2,1)S(1)} %copy-done, bf16[1024,256]{1,0:T(8,128)(2,1)S(1)} %collective-permute-done.k1_ref, bf16[256,1024]{1,0:T(8,128)(2,1)S(1)} %bitcast.12, ...), custom_call_target="tpu_custom_call" | custom-call | tf_op jit(solution)/shard_map/pallas_call | solution.py:81
  65.7 2.2 %collective-permute-start.11 = (bf16[3,272,128]{2,1,0:T(8,128)(2,1)S(1)}, bf16[3,272,128]{2,1,0:T(8,128)(2,1)S(1)}, u32[]{:S(2)}, u32[]{:S(2)}) collective-permute-start(bf16[3,272,128]{2,1,0:T(8,128)(2,1)S(1)} %get-tuple-element.17), channel_id=1, source_target_pairs={{0,2},{1,31},{2,4},{3,1},{4,6},{5,3},{6,8},{7,5},{8,10},{9,7},{10,... | collective-permute-start | bytes 626696 | tf_op jit(solution)/shard_map/ppermute | solution.py:151
  67.9 4.9 %collective-permute-start.12 = (bf16[3,272,128]{2,1,0:T(8,128)(2,1)S(1)}, bf16[3,272,128]{2,1,0:T(8,128)(2,1)S(1)}, u32[]{:S(2)}, u32[]{:S(2)}) collective-permute-start(bf16[3,272,128]{2,1,0:T(8,128)(2,1)S(1)} %get-tuple-element.18), channel_id=1, source_target_pairs={{0,30},{1,3},{2,0},{3,5},{4,2},{5,7},{6,4},{7,9},{8,6},{9,11},{10,... | collective-permute-start | bytes 626696 | tf_op jit(solution)/shard_map/ppermute | solution.py:151
  72.8 3.6 %collective-permute-start.13 = (bf16[1,272,128]{2,1,0:T(8,128)(2,1)S(1)}, bf16[1,272,128]{2,1,0:T(8,128)(2,1)S(1)}, u32[]{:S(2)}, u32[]{:S(2)}) collective-permute-start(bf16[1,272,128]{2,1,0:T(8,128)(2,1)S(1)} %get-tuple-element.16.refs_2_), channel_id=1, source_target_pairs={{0,6},{1,27},{2,8},{3,29},{4,10},{5,31},{6,12},{7,1},{8,14},{9,3},... | collective-permute-start | bytes 208904 | tf_op jit(solution)/shard_map/ppermute | solution.py:151
  76.4 5.6 %collective-permute-done.13.refs_5_ = bf16[1,272,128]{2,1,0:T(8,128)(2,1)S(1)} collective-permute-done((bf16[1,272,128]{2,1,0:T(8,128)(2,1)S(1)}, bf16[1,272,128]{2,1,0:T(8,128)(2,1)S(1)}, u32[]{:S(2)}, u32[]{:S(2)}) %collective-permute-start.13) | collective-permute-done | bytes 69664 | tf_op jit(solution)/shard_map/ppermute | solution.py:151
  82.2 7.9 %collective-permute-start.14 = (bf16[272,128]{1,0:T(8,128)(2,1)S(1)}, bf16[272,128]{1,0:T(8,128)(2,1)S(1)}, u32[]{:S(2)}, u32[]{:S(2)}) collective-permute-start(bf16[272,128]{1,0:T(8,128)(2,1)S(1)} %get-tuple-element.19), channel_id=1, source_target_pairs={{0,10},{1,23},{2,12},{3,25},{4,14},{5,27},{6,16},{7,29},{8,18},{9,... | collective-permute-start | bytes 208904 | tf_op jit(solution)/shard_map/ppermute | solution.py:151
  90.1 4.0 %collective-permute-start.15 = (bf16[272,128]{1,0:T(8,128)(2,1)S(1)}, bf16[272,128]{1,0:T(8,128)(2,1)S(1)}, u32[]{:S(2)}, u32[]{:S(2)}) collective-permute-start(bf16[272,128]{1,0:T(8,128)(2,1)S(1)} %get-tuple-element.20), channel_id=1, source_target_pairs={{0,22},{1,11},{2,24},{3,13},{4,26},{5,15},{6,28},{7,17},{8,30},{9,... | collective-permute-start | bytes 208904 | tf_op jit(solution)/shard_map/ppermute | solution.py:151
  94.1 4.3 %collective-permute-done.14.refs_5_ = bf16[272,128]{1,0:T(8,128)(2,1)S(1)} collective-permute-done((bf16[272,128]{1,0:T(8,128)(2,1)S(1)}, bf16[272,128]{1,0:T(8,128)(2,1)S(1)}, u32[]{:S(2)}, u32[]{:S(2)}) %collective-permute-start.14) | collective-permute-done | bytes 69664 | tf_op jit(solution)/shard_map/ppermute | solution.py:151
  98.4 4.3 %collective-permute-done.15.refs_6_ = bf16[272,128]{1,0:T(8,128)(2,1)S(1)} collective-permute-done((bf16[272,128]{1,0:T(8,128)(2,1)S(1)}, bf16[272,128]{1,0:T(8,128)(2,1)S(1)}, u32[]{:S(2)}, u32[]{:S(2)}) %collective-permute-start.15) | collective-permute-done | bytes 69664 | tf_op jit(solution)/shard_map/ppermute | solution.py:151
  (20 shorter events, 2.1 us)
Async XLA Ops:
  1.6 46.8 %copy-start = (bf16[1024,256]{1,0:T(8,128)(2,1)S(1)}, bf16[1024,256]{1,0:T(8,128)(2,1)}, u32[]{:S(2)}) copy-start(bf16[1024,256]{1,0:T(8,128)(2,1)} %k0_ref.5) | copy-start | bytes 1572868
  1.6 22.1 %collective-permute-start.3 = (bf16[136,256]{1,0:T(8,128)(2,1)S(1)}, bf16[136,256]{1,0:T(8,128)(2,1)S(1)}, u32[]{:S(2)}, u32[]{:S(2)}) collective-permute-start(bf16[136,256]{1,0:T(8,128)(2,1)S(1)} %get-tuple-element.22), channel_id=1, source_target_pairs={{0,10},{1,23},{2,12},{3,25},{4,14},{5,27},{6,16},{7,29},{8,18},{9,... | collective-permute-start | bytes 208904 | tf_op jit(solution)/shard_map/ppermute | solution.py:151
  12.2 11.5 %collective-permute-start.2 = (bf16[136,256]{1,0:T(8,128)(2,1)S(1)}, bf16[136,256]{1,0:T(8,128)(2,1)S(1)}, u32[]{:S(2)}, u32[]{:S(2)}) collective-permute-start(bf16[136,256]{1,0:T(8,128)(2,1)S(1)} %get-tuple-element.22), channel_id=1, source_target_pairs={{0,22},{1,11},{2,24},{3,13},{4,26},{5,15},{6,28},{7,17},{8,30},{9,... | collective-permute-start | bytes 208904 | tf_op jit(solution)/shard_map/ppermute | solution.py:151
  18.0 30.4 %collective-permute-start = (bf16[1024,256]{1,0:T(8,128)(2,1)}, bf16[1024,256]{1,0:T(8,128)(2,1)S(1)}, u32[]{:S(2)}, u32[]{:S(2)}) collective-permute-start(bf16[1024,256]{1,0:T(8,128)(2,1)} %k0_ref.5), channel_id=1, source_target_pairs={{0,1},{1,0},{2,3},{3,2},{4,5},{5,4},{6,7},{7,6},{8,9},{9,8},{10,11... | collective-permute-start | bytes 1572872 | tf_op jit(solution)/shard_map/ppermute | solution.py:159
  21.2 27.2 %collective-permute-start.1 = (bf16[256,1024]{1,0:T(8,128)(2,1)S(1)}, bf16[256,1024]{1,0:T(8,128)(2,1)S(1)}, u32[]{:S(2)}, u32[]{:S(2)}) collective-permute-start(bf16[256,1024]{1,0:T(8,128)(2,1)S(1)} %bitcast.9), channel_id=1, source_target_pairs={{0,1},{1,0},{2,3},{3,2},{4,5},{5,4},{6,7},{7,6},{8,9},{9,8},{10,11... | collective-permute-start | bytes 1572872 | tf_op jit(solution)/shard_map/ppermute | solution.py:160
  23.7 13.9 %collective-permute-start.5 = (bf16[3,136,256]{2,1,0:T(8,128)(2,1)S(1)}, bf16[3,136,256]{2,1,0:T(8,128)(2,1)S(1)}, u32[]{:S(2)}, u32[]{:S(2)}) collective-permute-start(bf16[3,136,256]{2,1,0:T(8,128)(2,1)S(1)} %pad_maximum_fusion.refs_0_), channel_id=1, source_target_pairs={{0,28},{1,5},{2,30},{3,7},{4,0},{5,9},{6,2},{7,11},{8,4},{9,13},{1... | collective-permute-start | bytes 626696 | tf_op jit(solution)/shard_map/ppermute | solution.py:151
  29.9 16.4 %collective-permute-start.6 = (bf16[3,136,256]{2,1,0:T(8,128)(2,1)S(1)}, bf16[3,136,256]{2,1,0:T(8,128)(2,1)S(1)}, u32[]{:S(2)}, u32[]{:S(2)}) collective-permute-start(bf16[3,136,256]{2,1,0:T(8,128)(2,1)S(1)} %pad_maximum_fusion.refs_0_), channel_id=1, source_target_pairs={{0,4},{1,29},{2,6},{3,31},{4,8},{5,1},{6,10},{7,3},{8,12},{9,5},{1... | collective-permute-start | bytes 626696 | tf_op jit(solution)/shard_map/ppermute | solution.py:151
  31.8 30.6 %collective-permute-start.9 = (bf16[3,136,256]{2,1,0:T(8,128)(2,1)S(1)}, bf16[3,136,256]{2,1,0:T(8,128)(2,1)S(1)}, u32[]{:S(2)}, u32[]{:S(2)}) collective-permute-start(bf16[3,136,256]{2,1,0:T(8,128)(2,1)S(1)} %pad_maximum_fusion.refs_0_), channel_id=1, source_target_pairs={{0,30},{1,3},{2,0},{3,5},{4,2},{5,7},{6,4},{7,9},{8,6},{9,11},{10,... | collective-permute-start | bytes 626696 | tf_op jit(solution)/shard_map/ppermute | solution.py:151
  37.6 24.8 %collective-permute-start.10 = (bf16[3,136,256]{2,1,0:T(8,128)(2,1)S(1)}, bf16[3,136,256]{2,1,0:T(8,128)(2,1)S(1)}, u32[]{:S(2)}, u32[]{:S(2)}) collective-permute-start(bf16[3,136,256]{2,1,0:T(8,128)(2,1)S(1)} %pad_maximum_fusion.refs_0_), channel_id=1, source_target_pairs={{0,2},{1,31},{2,4},{3,1},{4,6},{5,3},{6,8},{7,5},{8,10},{9,7},{10,... | collective-permute-start | bytes 626696 | tf_op jit(solution)/shard_map/ppermute | solution.py:151
  46.3 13.4 %collective-permute-start.4 = (bf16[1,136,256]{2,1,0:T(8,128)(2,1)S(1)}, bf16[1,136,256]{2,1,0:T(8,128)(2,1)S(1)}, u32[]{:S(2)}, u32[]{:S(2)}) collective-permute-start(bf16[1,136,256]{2,1,0:T(8,128)(2,1)S(1)} %bitcast.14), channel_id=1, source_target_pairs={{0,26},{1,7},{2,28},{3,9},{4,30},{5,11},{6,0},{7,13},{8,2},{9,15},... | collective-permute-start | bytes 208904 | tf_op jit(solution)/shard_map/ppermute | solution.py:151
  51.7 30.3 %collective-permute-start.7 = (bf16[3,272,128]{2,1,0:T(8,128)(2,1)S(1)}, bf16[3,272,128]{2,1,0:T(8,128)(2,1)S(1)}, u32[]{:S(2)}, u32[]{:S(2)}) collective-permute-start(bf16[3,272,128]{2,1,0:T(8,128)(2,1)S(1)} %get-tuple-element.13.refs_2_), channel_id=1, source_target_pairs={{0,4},{1,29},{2,6},{3,31},{4,8},{5,1},{6,10},{7,3},{8,12},{9,5},{1... | collective-permute-start | bytes 626696 | tf_op jit(solution)/shard_map/ppermute | solution.py:151
  55.3 26.7 %collective-permute-start.8 = (bf16[3,272,128]{2,1,0:T(8,128)(2,1)S(1)}, bf16[3,272,128]{2,1,0:T(8,128)(2,1)S(1)}, u32[]{:S(2)}, u32[]{:S(2)}) collective-permute-start(bf16[3,272,128]{2,1,0:T(8,128)(2,1)S(1)} %get-tuple-element.15), channel_id=1, source_target_pairs={{0,28},{1,5},{2,30},{3,7},{4,0},{5,9},{6,2},{7,11},{8,4},{9,13},{1... | collective-permute-start | bytes 626696 | tf_op jit(solution)/shard_map/ppermute | solution.py:151
  65.7 16.3 %collective-permute-start.11 = (bf16[3,272,128]{2,1,0:T(8,128)(2,1)S(1)}, bf16[3,272,128]{2,1,0:T(8,128)(2,1)S(1)}, u32[]{:S(2)}, u32[]{:S(2)}) collective-permute-start(bf16[3,272,128]{2,1,0:T(8,128)(2,1)S(1)} %get-tuple-element.17), channel_id=1, source_target_pairs={{0,2},{1,31},{2,4},{3,1},{4,6},{5,3},{6,8},{7,5},{8,10},{9,7},{10,... | collective-permute-start | bytes 626696 | tf_op jit(solution)/shard_map/ppermute | solution.py:151
  67.9 14.1 %collective-permute-start.12 = (bf16[3,272,128]{2,1,0:T(8,128)(2,1)S(1)}, bf16[3,272,128]{2,1,0:T(8,128)(2,1)S(1)}, u32[]{:S(2)}, u32[]{:S(2)}) collective-permute-start(bf16[3,272,128]{2,1,0:T(8,128)(2,1)S(1)} %get-tuple-element.18), channel_id=1, source_target_pairs={{0,30},{1,3},{2,0},{3,5},{4,2},{5,7},{6,4},{7,9},{8,6},{9,11},{10,... | collective-permute-start | bytes 626696 | tf_op jit(solution)/shard_map/ppermute | solution.py:151
  72.8 9.2 %collective-permute-start.13 = (bf16[1,272,128]{2,1,0:T(8,128)(2,1)S(1)}, bf16[1,272,128]{2,1,0:T(8,128)(2,1)S(1)}, u32[]{:S(2)}, u32[]{:S(2)}) collective-permute-start(bf16[1,272,128]{2,1,0:T(8,128)(2,1)S(1)} %get-tuple-element.16.refs_2_), channel_id=1, source_target_pairs={{0,6},{1,27},{2,8},{3,29},{4,10},{5,31},{6,12},{7,1},{8,14},{9,3},... | collective-permute-start | bytes 208904 | tf_op jit(solution)/shard_map/ppermute | solution.py:151
  82.2 16.2 %collective-permute-start.14 = (bf16[272,128]{1,0:T(8,128)(2,1)S(1)}, bf16[272,128]{1,0:T(8,128)(2,1)S(1)}, u32[]{:S(2)}, u32[]{:S(2)}) collective-permute-start(bf16[272,128]{1,0:T(8,128)(2,1)S(1)} %get-tuple-element.19), channel_id=1, source_target_pairs={{0,10},{1,23},{2,12},{3,25},{4,14},{5,27},{6,16},{7,29},{8,18},{9,... | collective-permute-start | bytes 208904 | tf_op jit(solution)/shard_map/ppermute | solution.py:151
  90.1 12.6 %collective-permute-start.15 = (bf16[272,128]{1,0:T(8,128)(2,1)S(1)}, bf16[272,128]{1,0:T(8,128)(2,1)S(1)}, u32[]{:S(2)}, u32[]{:S(2)}) collective-permute-start(bf16[272,128]{1,0:T(8,128)(2,1)S(1)} %get-tuple-element.20), channel_id=1, source_target_pairs={{0,22},{1,11},{2,24},{3,13},{4,26},{5,15},{6,28},{7,17},{8,30},{9,... | collective-permute-start | bytes 208904 | tf_op jit(solution)/shard_map/ppermute | solution.py:151

commit v9 on v2

--- a/solution.py
+++ b/solution.py
@@ -28,23 +28,24 @@
     return tail[0:1] + tail[1:2] + tail[2:3]
 
 
-def attend_kernel(first_ref, x_ref, k0_ref, k1_ref, v0_ref, v1_ref, out_ref):
+def attend_kernel(place_ref, x_ref, k0_ref, k1_ref, v0_ref, v1_ref, out_ref):
     sources, _, cand = out_ref.shape
     positions, width = k0_ref.shape
     nloc = positions // BLK
     scale = 1.0 / width**0.5
     for s in range(0, sources, 2):
-        query = jnp.concatenate([x_ref[s, :cand, :], x_ref[s + 1, :cand, :]], axis=0)
+        one, two = place_ref[0] + s, place_ref[0] + s + 1
+        query = jnp.concatenate([x_ref[one, :cand, :], x_ref[two, :cand, :]], axis=0)
         ids = jnp.concatenate(
             [
-                x_ref[s, cand:, :cand].astype(jnp.float32),
-                x_ref[s + 1, cand:, :cand].astype(jnp.float32),
+                x_ref[one, cand:, :cand].astype(jnp.float32),
+                x_ref[two, cand:, :cand].astype(jnp.float32),
             ],
             axis=1,
         )
         parts, lses = [], []
         for half, (k_ref, v_ref) in enumerate(((k0_ref, v0_ref), (k1_ref, v1_ref))):
-            near = ids - first_ref[half].astype(jnp.float32)
+            near = ids - place_ref[1 + half].astype(jnp.float32)
             inside = jnp.logical_and(near >= 0.0, near < nloc)
             sel = jnp.max(jnp.where(inside, near, -1.0), axis=0, keepdims=True)
             scores = lax.dot_general(
@@ -72,15 +73,15 @@
             out_ref[s + j, width:, :] = tail[:, j * cand : (j + 1) * cand]
 
 
-def attend(first, x, keys, vts, cand):
-    sources, _, width = x.shape
+def attend(place, x, keys, vts, cand, sources):
+    width = x.shape[2]
     return pl.pallas_call(
         attend_kernel,
         in_specs=[SMEM] + [VMEM] * 5,
         out_specs=VMEM,
         out_shape=jax.ShapeDtypeStruct((sources, width + TAIL, cand), jnp.bfloat16),
         compiler_params=PARAMS,
-    )(first, x, *keys, *vts)
+    )(jnp.stack(place), x, *keys, *vts)
 
 
 def mix(blocks):
@@ -146,29 +147,37 @@
 
     far = [[2 * (r + stride * j) + c for j in range(members)] for c in range(2) for r in range(stride)]
 
-    def exchange(x):
-        return lax.all_to_all(x, ("z", "core"), 0, 0, tiled=True, axis_index_groups=far)
+    near = [
+        [2 * ((stride * i + 2 * c + j) % chips) + c for j in range(stride)]
+        for c in range(2)
+        for i in range(members)
+    ]
+
+    def exchange(x, groups):
+        return lax.all_to_all(x, ("z", "core"), 0, 0, tiled=True, axis_index_groups=groups)
 
     swap = [(0, 1), (1, 0)]
     ids = (block_dev * nloc + block_local).astype(jnp.bfloat16).T
     mine = jnp.concatenate([queries, jnp.pad(ids, ((0, 0), (0, width - cand)))], axis=0)
-    own = exchange(jnp.broadcast_to(mine[None], (members, cand + topk, width)))
+    own = exchange(jnp.broadcast_to(mine[None], (members, cand + topk, width)), far)
     vt = hist_values.T
     keys = (hist_keys, lax.ppermute(hist_keys, "core", swap))
     vts = (vt, lax.ppermute(vt, "core", swap))
-    here = 2 * lax.axis_index("z").astype(jnp.int32)
+    z = lax.axis_index("z").astype(jnp.int32)
     core = lax.axis_index("core").astype(jnp.int32)
-    first = jnp.stack([here + core, here + 1 - core]) * nloc
+    halves = [(2 * z + core) * nloc, (2 * z + 1 - core) * nloc]
+    every = exchange(jnp.broadcast_to(own[None], (stride,) + own.shape), near)
+    every = every.reshape((stride * members,) + own.shape[1:])
 
+    def part(by):
+        line = (z + by - 2 * core + 2 * stride) % stride
+        return attend([line * members] + halves, every, keys, vts, cand, members)
+
+    mine_part = attend([jnp.int32(0)] + halves, own, keys, vts, cand, members)
     steps = (lambda c: 2 - 4 * c, lambda c: 1, lambda c: -1)
-    others = [shift(own, by) for by in steps]
-    mine_part = attend(first, own, keys, vts, cand)
-    back = [
-        shift(attend(first, x, keys, vts, cand), lambda c, by=by: -by(c))
-        for x, by in zip(others, steps)
-    ]
+    back = [shift(part(by(core)), by) for by in steps]
     merged = near_merge(mine_part, *back)
-    return far_merge(exchange(merged))
+    return far_merge(exchange(merged, far))
 
 
 def solution(mesh):

time: 104 us -> 116 us (1.12)
  blocking collectives: 23 us -> 59.5 us
  starting transfers between devices: 40.4 us -> 20.9 us
  waiting for transfers between devices: 25.6 us -> 19.8 us
    all_to_all x1 -> x2, blocking collectives: 23 us -> 59.5 us  [exchange(): lax.all_to_all(x, ('z', 'core'), 0, 0, tiled=True, axis_index_groups=groups)]
    all_to_all x1, starting transfers between devices: 15.1 us -> 5.02 us  [exchange(): lax.all_to_all(x, ('z', 'core'), 0, 0, tiled=True, axis_index_groups=groups)]
    ppermute x6 -> x3, starting transfers between devices: 21 us -> 11 us  [shift(): return lax.ppermute(x, ('z', 'core'), pairs)]
    ppermute x6 -> x3, waiting for transfers between devices: 11.3 us -> 5.89 us  [shift(): return lax.ppermute(x, ('z', 'core'), pairs)]
    all_to_all x1, waiting for transfers between devices: 14.2 us -> 12.3 us  [exchange(): lax.all_to_all(x, ('z', 'core'), 0, 0, tiled=True, axis_index_groups=groups)]
    ppermute x1, waiting for transfers between devices: 0.01 us -> 1.6 us  [body(): keys = (hist_keys, lax.ppermute(hist_keys, 'core', swap))]
  transfers between devices with their start and end apart: 9 -> 6, of which waited for: 4 -> 3; matrix products, arithmetic and copies ran while one was open for 0% -> 0% of each run, Pallas kernels for 10% -> 7%
where the time goes in v9:
time: 116 us
  blocking collectives  59.5 us (51%)
  starting transfers between devices  20.9 us (18%)
  waiting for transfers between devices  19.8 us (17%)
  Pallas kernels  12 us (10%)
  other arithmetic  1.86 us (2%)
  local copies, waits for them, and re-layouts  1.3 us (1%)
    all_to_all x2, blocking collectives, exchange(): lax.all_to_all(x, ('z', 'core'), 0, 0, tiled=True, axis_index_groups=groups)  59.5 us
    all_to_all x1, waiting for transfers between devices, exchange(): lax.all_to_all(x, ('z', 'core'), 0, 0, tiled=True, axis_index_groups=groups)  12.3 us
    ppermute x3, starting transfers between devices, shift(): return lax.ppermute(x, ('z', 'core'), pairs)  11 us
    pallas_call x4, Pallas kernels, attend(): pl.pallas_call(attend_kernel, in_specs=[SMEM] + [VMEM] * 5, out_specs=VME...  10.9 us
    ppermute x3, waiting for transfers between devices, shift(): return lax.ppermute(x, ('z', 'core'), pairs)  5.89 us
    all_to_all x1, starting transfers between devices, exchange(): lax.all_to_all(x, ('z', 'core'), 0, 0, tiled=True, axis_index_groups=groups)  5.02 us
    ppermute x1, starting transfers between devices, body(): vts = (vt, lax.ppermute(vt, 'core', swap))  2.93 us
  transfers between devices with their start and end apart: 6, of which 3 were waited for; matrix products, arithmetic and copies ran while one was open for 0% of the time, Pallas kernels for 7%

profile of v9, /device:TPU:6, one launch (start us, length us, event | category | flops | bytes accessed | tf_op | source)
XLA Modules:
  0.0 115.5 jit_solution(7338654495499788623)
XLA Ops:
  0.0 0.7 fusion.2
  0.7 0.8 fusion.1
  1.6 35.2 %all_to_all.15.x_ref = bf16[4,136,256]{2,1,0:T(8,128)(2,1)S(1)} all-to-all(bf16[4,136,256]{2,1,0:T(8,128)(2,1)S(1)} %broadcast_in_dim.4), channel_id=1, replica_groups={{0,8,16,24},{2,10,18,26},{4,12,20,28},{6,14,22,30},{1,9,17,25},{3,11,19..., dimensions={0} | all-to-all | bytes 557056 | tf_op jit(solution)/shard_map/all_to_all | solution.py:157
  36.8 1.1 broadcast_in_dim.5
  37.8 5.0 %all-to-all-start.1 = ((bf16[4,4,136,256]{3,2,1,0:T(8,128)(2,1)}), bf16[4,4,136,256]{3,2,1,0:T(8,128)(2,1)S(1)}, u32[]{:S(2)}, u32[]{:S(2)}) async-start(bf16[4,4,136,256]{3,2,1,0:T(8,128)(2,1)} %broadcast_in_dim.5), calls=%async_computation.1 | async-start | bytes 2228224 | tf_op jit(solution)/shard_map/all_to_all | solution.py:157
  42.9 0.2 copy.6
  43.1 2.9 %collective-permute-start.1 = (bf16[256,1024]{1,0:T(8,128)(2,1)S(1)}, bf16[256,1024]{1,0:T(8,128)(2,1)S(1)}, u32[]{:S(2)}, u32[]{:S(2)}) collective-permute-start(bf16[256,1024]{1,0:T(8,128)(2,1)S(1)} %bitcast.12), channel_id=1, source_target_pairs={{0,1},{1,0},{2,3},{3,2},{4,5},{5,4},{6,7},{7,6},{8,9},{9,8},{10,11... | collective-permute-start | bytes 1572872 | tf_op jit(solution)/shard_map/ppermute | solution.py:165
  46.0 1.9 %collective-permute-start = (bf16[1024,256]{1,0:T(8,128)(2,1)S(1)}, bf16[1024,256]{1,0:T(8,128)(2,1)S(1)}, u32[]{:S(2)}, u32[]{:S(2)}) collective-permute-start(bf16[1024,256]{1,0:T(8,128)(2,1)S(1)} %copy-done), channel_id=1, source_target_pairs={{0,1},{1,0},{2,3},{3,2},{4,5},{5,4},{6,7},{7,6},{8,9},{9,8},{10,11... | collective-permute-start | bytes 1572872 | tf_op jit(solution)/shard_map/ppermute | solution.py:164
  48.0 0.1 add_add_fusion.2.place_ref
  48.2 0.1 add_add_fusion.1.place_ref
  48.2 1.6 %collective-permute-done.k1_ref = bf16[1024,256]{1,0:T(8,128)(2,1)S(1)} collective-permute-done((bf16[1024,256]{1,0:T(8,128)(2,1)S(1)}, bf16[1024,256]{1,0:T(8,128)(2,1)S(1)}, u32[]{:S(2)}, u32[]{:S(2)}) %collective-permute-start) | collective-permute-done | bytes 524320 | tf_op jit(solution)/shard_map/ppermute | solution.py:164
  49.8 12.3 %all-to-all-done.1 = bf16[4,4,136,256]{3,2,1,0:T(8,128)(2,1)S(1)} async-done(((bf16[4,4,136,256]{3,2,1,0:T(8,128)(2,1)}), bf16[4,4,136,256]{3,2,1,0:T(8,128)(2,1)S(1)}, u32[]{:S(2)}, u32[]{:S(2)}) %all-to-all-start.1) | async-done | bytes 1114144 | tf_op jit(solution)/shard_map/all_to_all | solution.py:157
  62.2 2.7 %shard_map.57 = bf16[4,272,128]{2,1,0:T(8,128)(2,1)S(1)} custom-call(s32[3]{0:T(128)S(1)} %add_add_fusion.2.place_ref, bf16[16,136,256]{2,1,0:T(8,128)(2,1)S(1)} %bitcast.9, bf16[1024,256]{1,0:T(8,128)(2,1)S(1)} %copy-done, bf16[1024,256]{1,0:T(8,128)(2,1)S(1)} %collective-permute-done.k1_ref, bf16[256,1024]{1,0:T(8,128)(2,1)S(1)} %bitcast.13, ...), custom_call_target="tpu_custom_call" | custom-call | tf_op jit(solution)/shard_map/pallas_call | solution.py:78
  64.9 4.0 %collective-permute-start.3 = (bf16[4,272,128]{2,1,0:T(8,128)(2,1)S(1)}, bf16[4,272,128]{2,1,0:T(8,128)(2,1)S(1)}, u32[]{:S(2)}, u32[]{:S(2)}) collective-permute-start(bf16[4,272,128]{2,1,0:T(8,128)(2,1)S(1)} %shard_map.57), channel_id=1, source_target_pairs={{0,2},{1,3},{2,4},{3,5},{4,6},{5,7},{6,8},{7,9},{8,10},{9,11},{10,... | collective-permute-start | bytes 835592 | tf_op jit(solution)/shard_map/ppermute | solution.py:146
  68.9 2.7 %shard_map.58 = bf16[4,272,128]{2,1,0:T(8,128)(2,1)S(1)} custom-call(s32[3]{0:T(128)S(1)} %add_add_fusion.3.place_ref, bf16[16,136,256]{2,1,0:T(8,128)(2,1)S(1)} %bitcast.10, bf16[1024,256]{1,0:T(8,128)(2,1)S(1)} %copy-done, bf16[1024,256]{1,0:T(8,128)(2,1)S(1)} %collective-permute-done.k1_ref, bf16[256,1024]{1,0:T(8,128)(2,1)S(1)} %bitcast.14, ...), custom_call_target="tpu_custom_call" | custom-call | tf_op jit(solution)/shard_map/pallas_call | solution.py:78
  71.7 3.0 %collective-permute-start.4 = (bf16[4,272,128]{2,1,0:T(8,128)(2,1)S(1)}, bf16[4,272,128]{2,1,0:T(8,128)(2,1)S(1)}, u32[]{:S(2)}, u32[]{:S(2)}) collective-permute-start(bf16[4,272,128]{2,1,0:T(8,128)(2,1)S(1)} %shard_map.58), channel_id=1, source_target_pairs={{0,30},{1,31},{2,0},{3,1},{4,2},{5,3},{6,4},{7,5},{8,6},{9,7},{10,... | collective-permute-start | bytes 835592 | tf_op jit(solution)/shard_map/ppermute | solution.py:146
  74.7 2.7 %shard_map.56 = bf16[4,272,128]{2,1,0:T(8,128)(2,1)S(1)} custom-call(s32[3]{0:T(128)S(1)} %add_add_fusion.1.place_ref, bf16[16,136,256]{2,1,0:T(8,128)(2,1)S(1)} %bitcast.11, bf16[1024,256]{1,0:T(8,128)(2,1)S(1)} %copy-done, bf16[1024,256]{1,0:T(8,128)(2,1)S(1)} %collective-permute-done.k1_ref, bf16[256,1024]{1,0:T(8,128)(2,1)S(1)} %bitcast.15, ...), custom_call_target="tpu_custom_call" | custom-call | tf_op jit(solution)/shard_map/pallas_call | solution.py:78
  77.4 4.0 %collective-permute-start.2 = (bf16[4,272,128]{2,1,0:T(8,128)(2,1)S(1)}, bf16[4,272,128]{2,1,0:T(8,128)(2,1)S(1)}, u32[]{:S(2)}, u32[]{:S(2)}) collective-permute-start(bf16[4,272,128]{2,1,0:T(8,128)(2,1)S(1)} %shard_map.56), channel_id=1, source_target_pairs={{0,4},{1,29},{2,6},{3,31},{4,8},{5,1},{6,10},{7,3},{8,12},{9,5},{1... | collective-permute-start | bytes 835592 | tf_op jit(solution)/shard_map/ppermute | solution.py:146
  81.4 0.1 add_add_fusion.place_ref
  81.5 2.7 %shard_map.55.refs_0_ = bf16[4,272,128]{2,1,0:T(8,128)(2,1)S(1)} custom-call(s32[3]{0:T(128)S(1)} %add_add_fusion.place_ref, bf16[4,136,256]{2,1,0:T(8,128)(2,1)S(1)} %all_to_all.15.x_ref, bf16[1024,256]{1,0:T(8,128)(2,1)S(1)} %copy-done, bf16[1024,256]{1,0:T(8,128)(2,1)S(1)} %collective-permute-done.k1_ref, bf16[256,1024]{1,0:T(8,128)(2,1)S(1)} %bitcast.16, ...), custom_call_target="tpu_custom_call" | custom-call | tf_op jit(solution)/shard_map/pallas_call | solution.py:78
  84.2 5.9 %collective-permute-done.2.refs_1_ = bf16[4,272,128]{2,1,0:T(8,128)(2,1)S(1)} collective-permute-done((bf16[4,272,128]{2,1,0:T(8,128)(2,1)S(1)}, bf16[4,272,128]{2,1,0:T(8,128)(2,1)S(1)}, u32[]{:S(2)}, u32[]{:S(2)}) %collective-permute-start.2) | collective-permute-done | bytes 278560 | tf_op jit(solution)/shard_map/ppermute | solution.py:146
  90.1 0.3 shard_map.59
  90.4 24.3 %all_to_all.16.x_ref = bf16[4,272,128]{2,1,0:T(8,128)(2,1)S(1)} all-to-all(bf16[4,272,128]{2,1,0:T(8,128)(2,1)S(1)} %shard_map.59), channel_id=1, replica_groups={{0,8,16,24},{2,10,18,26},{4,12,20,28},{6,14,22,30},{1,9,17,25},{3,11,19..., dimensions={0} | all-to-all | bytes 557056 | tf_op jit(solution)/shard_map/all_to_all | solution.py:157
  114.7 0.8 shard_map.60
  (9 shorter events, 0.1 us)
Async XLA Ops:
  37.8 5.0 %copy-start.1 = (bf16[1024,256]{1,0:T(8,128)(2,1)S(1)}, bf16[1024,256]{1,0:T(8,128)(2,1)}, u32[]{:S(2)}) copy-start(bf16[1024,256]{1,0:T(8,128)(2,1)} %param.7) | copy-start | bytes 1572868
  37.8 8.2 %copy-start = (bf16[1024,256]{1,0:T(8,128)(2,1)S(1)}, bf16[1024,256]{1,0:T(8,128)(2,1)}, u32[]{:S(2)}) copy-start(bf16[1024,256]{1,0:T(8,128)(2,1)} %k0_ref.7) | copy-start | bytes 1572868
  37.8 24.3 %all-to-all-start.1 = ((bf16[4,4,136,256]{3,2,1,0:T(8,128)(2,1)}), bf16[4,4,136,256]{3,2,1,0:T(8,128)(2,1)S(1)}, u32[]{:S(2)}, u32[]{:S(2)}) async-start(bf16[4,4,136,256]{3,2,1,0:T(8,128)(2,1)} %broadcast_in_dim.5), calls=%async_computation.1 | async-start | bytes 2228224 | tf_op jit(solution)/shard_map/all_to_all | solution.py:157
  43.1 5.1 %collective-permute-start.1 = (bf16[256,1024]{1,0:T(8,128)(2,1)S(1)}, bf16[256,1024]{1,0:T(8,128)(2,1)S(1)}, u32[]{:S(2)}, u32[]{:S(2)}) collective-permute-start(bf16[256,1024]{1,0:T(8,128)(2,1)S(1)} %bitcast.12), channel_id=1, source_target_pairs={{0,1},{1,0},{2,3},{3,2},{4,5},{5,4},{6,7},{7,6},{8,9},{9,8},{10,11... | collective-permute-start | bytes 1572872 | tf_op jit(solution)/shard_map/ppermute | solution.py:165
  46.0 3.8 %collective-permute-start = (bf16[1024,256]{1,0:T(8,128)(2,1)S(1)}, bf16[1024,256]{1,0:T(8,128)(2,1)S(1)}, u32[]{:S(2)}, u32[]{:S(2)}) collective-permute-start(bf16[1024,256]{1,0:T(8,128)(2,1)S(1)} %copy-done), channel_id=1, source_target_pairs={{0,1},{1,0},{2,3},{3,2},{4,5},{5,4},{6,7},{7,6},{8,9},{9,8},{10,11... | collective-permute-start | bytes 1572872 | tf_op jit(solution)/shard_map/ppermute | solution.py:164
  64.9 19.3 %collective-permute-start.3 = (bf16[4,272,128]{2,1,0:T(8,128)(2,1)S(1)}, bf16[4,272,128]{2,1,0:T(8,128)(2,1)S(1)}, u32[]{:S(2)}, u32[]{:S(2)}) collective-permute-start(bf16[4,272,128]{2,1,0:T(8,128)(2,1)S(1)} %shard_map.57), channel_id=1, source_target_pairs={{0,2},{1,3},{2,4},{3,5},{4,6},{5,7},{6,8},{7,9},{8,10},{9,11},{10,... | collective-permute-start | bytes 835592 | tf_op jit(solution)/shard_map/ppermute | solution.py:146
  71.7 12.6 %collective-permute-start.4 = (bf16[4,272,128]{2,1,0:T(8,128)(2,1)S(1)}, bf16[4,272,128]{2,1,0:T(8,128)(2,1)S(1)}, u32[]{:S(2)}, u32[]{:S(2)}) collective-permute-start(bf16[4,272,128]{2,1,0:T(8,128)(2,1)S(1)} %shard_map.58), channel_id=1, source_target_pairs={{0,30},{1,31},{2,0},{3,1},{4,2},{5,3},{6,4},{7,5},{8,6},{9,7},{10,... | collective-permute-start | bytes 835592 | tf_op jit(solution)/shard_map/ppermute | solution.py:146
  77.4 12.7 %collective-permute-start.2 = (bf16[4,272,128]{2,1,0:T(8,128)(2,1)S(1)}, bf16[4,272,128]{2,1,0:T(8,128)(2,1)S(1)}, u32[]{:S(2)}, u32[]{:S(2)}) collective-permute-start(bf16[4,272,128]{2,1,0:T(8,128)(2,1)S(1)} %shard_map.56), channel_id=1, source_target_pairs={{0,4},{1,29},{2,6},{3,31},{4,8},{5,1},{6,10},{7,3},{8,12},{9,5},{1... | collective-permute-start | bytes 835592 | tf_op jit(solution)/shard_map/ppermute | solution.py:146

commit v10 on v8

--- a/solution.py
+++ b/solution.py
@@ -101,41 +101,40 @@
 
 
 def near_kernel(*refs):
-    *parts, extra, out1_ref, out2_ref = refs
+    *parts, out1_ref, out2_ref = refs
     width = out1_ref.shape[0] - TAIL
     for slot, out_ref in ((1, out1_ref), (2, out2_ref)):
-        blocks = [ref[slot] for ref in parts] + ([extra[0]] if slot == 1 else [])
-        total, lse = mix(blocks)
+        total, lse = mix([ref[slot] for ref in parts])
         out_ref[:width, :] = total.astype(jnp.bfloat16)
         out_ref[width:, :] = tail_rows(lse)
 
 
-def near_merge(parts, extra):
-    shape = jax.ShapeDtypeStruct(extra.shape[1:], extra.dtype)
+def near_merge(parts):
+    shape = jax.ShapeDtypeStruct(parts[0].shape[1:], parts[0].dtype)
     return pl.pallas_call(
         near_kernel,
-        in_specs=[VMEM] * (len(parts) + 1),
+        in_specs=[VMEM] * len(parts),
         out_specs=[VMEM] * 2,
         out_shape=[shape] * 2,
         compiler_params=PARAMS,
-    )(*parts, extra)
+    )(*parts)
 
 
 def far_kernel(*refs):
-    *parts, one, two, out_ref = refs
-    total, _ = mix([ref[0] for ref in parts] + [one[...], two[...]])
+    *parts, out_ref = refs
+    total, _ = mix([ref[0] for ref in parts])
     out_ref[...] = total.T.astype(jnp.bfloat16)
 
 
-def far_merge(parts, one, two):
-    rows, cand = one.shape
+def far_merge(parts):
+    _, rows, cand = parts[0].shape
     return pl.pallas_call(
         far_kernel,
-        in_specs=[VMEM] * (len(parts) + 2),
+        in_specs=[VMEM] * len(parts),
         out_specs=VMEM,
         out_shape=jax.ShapeDtypeStruct((cand, rows - TAIL), jnp.bfloat16),
         compiler_params=PARAMS,
-    )(*parts, one, two)
+    )(*parts)
 
 
 def body(chips, queries, hist_keys, hist_values, block_dev, block_local):
@@ -153,6 +152,7 @@
     ids = (block_dev * nloc + block_local).astype(jnp.bfloat16).T
     mine = jnp.concatenate([queries, jnp.pad(ids, ((0, 0), (0, width - cand)))], axis=0)
     up5, down5 = shift(mine, -5), shift(mine, 5)
+    eight = shift(mine[None], 8)
 
     swap = [(0, 1), (1, 0)]
     vt = hist_values.T
@@ -164,18 +164,17 @@
 
     own = jnp.stack([mine, up5, down5])
     up2, down2 = shift(own, -2), shift(own, 2)
-    eight = shift(up5[None], -3)
     up1, down1 = shift(own, -1), shift(own, 1)
 
     part_up2, part_down2 = attend(first, (up2, down2), keys, vts, cand)
     back = [shift(part_up2, 2), shift(part_down2, -2)]
     part_own, part_eight = attend(first, (own, eight), keys, vts, cand, (part_up2,))
-    extra = shift(part_eight, 3)
     part_up1, part_down1 = attend(first, (up1, down1), keys, vts, cand, (part_eight,))
     back += [shift(part_up1, 1), shift(part_down1, -1)]
+    across = shift(part_eight, 8)
     parts = [part_own] + back
-    slot1, slot2 = near_merge(parts, extra)
-    return far_merge(parts, shift(slot1, 5), shift(slot2, -5))
+    slot1, slot2 = near_merge(parts)
+    return far_merge(parts + [shift(slot1, 5)[None], shift(slot2, -5)[None], across])
 
 
 def solution(mesh):

time: 105 us -> 110 us (1.048)
  the two profiles are of different devices: /device:TPU:6 before, /device:TPU:92 now
where the time goes in v10:
time: 110 us; the launch traced here: 109 us
  starting transfers between devices  83 us (75%)
  waiting for transfers between devices  12.4 us (11%)
  Pallas kernels  10.3 us (9%)
  other arithmetic  1.66 us (2%)
  local copies, waits for them, and re-layouts  1.25 us (1%)
    ppermute x14, starting transfers between devices, shift(): return lax.ppermute(x, ('z', 'core'), pairs)  78.7 us
    ppermute x14, waiting for transfers between devices, shift(): return lax.ppermute(x, ('z', 'core'), pairs)  12.4 us
    pallas_call x3, Pallas kernels, attend(): pl.pallas_call(functools.partial(attend_kernel, counts), in_specs=[SMEM]...  9.26 us
    ppermute x1, starting transfers between devices, body(): vts = (vt, lax.ppermute(vt, 'core', swap))  2.41 us
  transfers between devices with their start and end apart: 16, of which 3 were waited for; matrix products, arithmetic and copies ran while one was open for 1% of the time, Pallas kernels for 9%

profile of v10, /device:TPU:92, one launch (start us, length us, event | category | flops | bytes accessed | tf_op | source)
XLA Modules:
  0.0 108.9 jit_solution(14163530341968915330)
XLA Ops:
  1.6 10.6 %collective-permute-start.3 = (bf16[136,256]{1,0:T(8,128)(2,1)S(1)}, bf16[136,256]{1,0:T(8,128)(2,1)S(1)}, u32[]{:S(2)}, u32[]{:S(2)}) collective-permute-start(bf16[136,256]{1,0:T(8,128)(2,1)S(1)} %get-tuple-element.22), channel_id=1, source_target_pairs={{0,10},{1,23},{2,12},{3,25},{4,14},{5,27},{6,16},{7,29},{8,18},{9,... | collective-permute-start | bytes 208904 | tf_op jit(solution)/shard_map/ppermute | solution.py:150
  12.2 2.9 %collective-permute-start.2 = (bf16[136,256]{1,0:T(8,128)(2,1)S(1)}, bf16[136,256]{1,0:T(8,128)(2,1)S(1)}, u32[]{:S(2)}, u32[]{:S(2)}) collective-permute-start(bf16[136,256]{1,0:T(8,128)(2,1)S(1)} %get-tuple-element.22), channel_id=1, source_target_pairs={{0,22},{1,11},{2,24},{3,13},{4,26},{5,15},{6,28},{7,17},{8,30},{9,... | collective-permute-start | bytes 208904 | tf_op jit(solution)/shard_map/ppermute | solution.py:150
  15.0 1.9 %collective-permute-start = (bf16[1024,256]{1,0:T(8,128)(2,1)}, bf16[1024,256]{1,0:T(8,128)(2,1)S(1)}, u32[]{:S(2)}, u32[]{:S(2)}) collective-permute-start(bf16[1024,256]{1,0:T(8,128)(2,1)} %k0_ref.5), channel_id=1, source_target_pairs={{0,1},{1,0},{2,3},{3,2},{4,5},{5,4},{6,7},{7,6},{8,9},{9,8},{10,11... | collective-permute-start | bytes 1572872 | tf_op jit(solution)/shard_map/ppermute | solution.py:159
  17.0 1.2 %copy.6 = bf16[1024,256]{0,1:T(8,128)(2,1)S(1)} copy(bf16[1024,256]{1,0:T(8,128)(2,1)} %param.7) | data formatting | bytes 1048576 | tf_op args[2]
  18.2 2.4 %collective-permute-start.1 = (bf16[256,1024]{1,0:T(8,128)(2,1)S(1)}, bf16[256,1024]{1,0:T(8,128)(2,1)S(1)}, u32[]{:S(2)}, u32[]{:S(2)}) collective-permute-start(bf16[256,1024]{1,0:T(8,128)(2,1)S(1)} %bitcast.11), channel_id=1, source_target_pairs={{0,1},{1,0},{2,3},{3,2},{4,5},{5,4},{6,7},{7,6},{8,9},{9,8},{10,11... | collective-permute-start | bytes 1572872 | tf_op jit(solution)/shard_map/ppermute | solution.py:160
  20.6 2.5 %collective-permute-done.2 = bf16[136,256]{1,0:T(8,128)(2,1)S(1)} collective-permute-done((bf16[136,256]{1,0:T(8,128)(2,1)S(1)}, bf16[136,256]{1,0:T(8,128)(2,1)S(1)}, u32[]{:S(2)}, u32[]{:S(2)}) %collective-permute-start.2) | collective-permute-done | bytes 69664 | tf_op jit(solution)/shard_map/ppermute | solution.py:150
  23.2 2.0 %collective-permute-start.5 = (bf16[3,136,256]{2,1,0:T(8,128)(2,1)S(1)}, bf16[3,136,256]{2,1,0:T(8,128)(2,1)S(1)}, u32[]{:S(2)}, u32[]{:S(2)}) collective-permute-start(bf16[3,136,256]{2,1,0:T(8,128)(2,1)S(1)} %pad_maximum_fusion.refs_0_), channel_id=1, source_target_pairs={{0,28},{1,5},{2,30},{3,7},{4,0},{5,9},{6,2},{7,11},{8,4},{9,13},{1... | collective-permute-start | bytes 626696 | tf_op jit(solution)/shard_map/ppermute | solution.py:150
  25.3 7.2 %collective-permute-start.6 = (bf16[3,136,256]{2,1,0:T(8,128)(2,1)S(1)}, bf16[3,136,256]{2,1,0:T(8,128)(2,1)S(1)}, u32[]{:S(2)}, u32[]{:S(2)}) collective-permute-start(bf16[3,136,256]{2,1,0:T(8,128)(2,1)S(1)} %pad_maximum_fusion.refs_0_), channel_id=1, source_target_pairs={{0,4},{1,29},{2,6},{3,31},{4,8},{5,1},{6,10},{7,3},{8,12},{9,5},{1... | collective-permute-start | bytes 626696 | tf_op jit(solution)/shard_map/ppermute | solution.py:150
  32.4 4.0 %collective-permute-start.9 = (bf16[3,136,256]{2,1,0:T(8,128)(2,1)S(1)}, bf16[3,136,256]{2,1,0:T(8,128)(2,1)S(1)}, u32[]{:S(2)}, u32[]{:S(2)}) collective-permute-start(bf16[3,136,256]{2,1,0:T(8,128)(2,1)S(1)} %pad_maximum_fusion.refs_0_), channel_id=1, source_target_pairs={{0,30},{1,3},{2,0},{3,5},{4,2},{5,7},{6,4},{7,9},{8,6},{9,11},{10,... | collective-permute-start | bytes 626696 | tf_op jit(solution)/shard_map/ppermute | solution.py:150
  36.5 8.3 %collective-permute-start.10 = (bf16[3,136,256]{2,1,0:T(8,128)(2,1)S(1)}, bf16[3,136,256]{2,1,0:T(8,128)(2,1)S(1)}, u32[]{:S(2)}, u32[]{:S(2)}) collective-permute-start(bf16[3,136,256]{2,1,0:T(8,128)(2,1)S(1)} %pad_maximum_fusion.refs_0_), channel_id=1, source_target_pairs={{0,2},{1,31},{2,4},{3,1},{4,6},{5,3},{6,8},{7,5},{8,10},{9,7},{10,... | collective-permute-start | bytes 626696 | tf_op jit(solution)/shard_map/ppermute | solution.py:150
  44.8 4.4 %collective-permute-start.4 = (bf16[1,136,256]{2,1,0:T(8,128)(2,1)S(1)}, bf16[1,136,256]{2,1,0:T(8,128)(2,1)S(1)}, u32[]{:S(2)}, u32[]{:S(2)}) collective-permute-start(bf16[1,136,256]{2,1,0:T(8,128)(2,1)S(1)} %get-tuple-element.21), channel_id=1, source_target_pairs={{0,16},{1,17},{2,18},{3,19},{4,20},{5,21},{6,22},{7,23},{8,24},{9,... | collective-permute-start | bytes 208904 | tf_op jit(solution)/shard_map/ppermute | solution.py:150
  49.3 3.3 %shard_map.55 = (bf16[3,272,128]{2,1,0:T(8,128)(2,1)S(1)}, bf16[3,272,128]{2,1,0:T(8,128)(2,1)S(1)}) custom-call(s32[2]{0:T(128)S(1)} %add_multiply_fusion.first_ref, bf16[1024,256]{1,0:T(8,128)(2,1)S(1)} %copy-done, bf16[1024,256]{1,0:T(8,128)(2,1)S(1)} %collective-permute-done.k1_ref, bf16[256,1024]{1,0:T(8,128)(2,1)S(1)} %bitcast.12, ...), custom_call_target="tpu_custom_call" | custom-call | tf_op jit(solution)/shard_map/pallas_call | solution.py:81
  52.6 4.5 %collective-permute-start.7 = (bf16[3,272,128]{2,1,0:T(8,128)(2,1)S(1)}, bf16[3,272,128]{2,1,0:T(8,128)(2,1)S(1)}, u32[]{:S(2)}, u32[]{:S(2)}) collective-permute-start(bf16[3,272,128]{2,1,0:T(8,128)(2,1)S(1)} %get-tuple-element.13.refs_2_), channel_id=1, source_target_pairs={{0,4},{1,29},{2,6},{3,31},{4,8},{5,1},{6,10},{7,3},{8,12},{9,5},{1... | collective-permute-start | bytes 626696 | tf_op jit(solution)/shard_map/ppermute | solution.py:150
  57.1 4.7 %collective-permute-start.8 = (bf16[3,272,128]{2,1,0:T(8,128)(2,1)S(1)}, bf16[3,272,128]{2,1,0:T(8,128)(2,1)S(1)}, u32[]{:S(2)}, u32[]{:S(2)}) collective-permute-start(bf16[3,272,128]{2,1,0:T(8,128)(2,1)S(1)} %get-tuple-element.15), channel_id=1, source_target_pairs={{0,28},{1,5},{2,30},{3,7},{4,0},{5,9},{6,2},{7,11},{8,4},{9,13},{1... | collective-permute-start | bytes 626696 | tf_op jit(solution)/shard_map/ppermute | solution.py:150
  61.8 2.7 %shard_map.56 = (bf16[3,272,128]{2,1,0:T(8,128)(2,1)S(1)}, bf16[1,272,128]{2,1,0:T(8,128)(2,1)S(1)}) custom-call(s32[2]{0:T(128)S(1)} %add_multiply_fusion.first_ref, bf16[1024,256]{1,0:T(8,128)(2,1)S(1)} %copy-done, bf16[1024,256]{1,0:T(8,128)(2,1)S(1)} %collective-permute-done.k1_ref, bf16[256,1024]{1,0:T(8,128)(2,1)S(1)} %bitcast.13, ...), custom_call_target="tpu_custom_call" | custom-call | tf_op jit(solution)/shard_map/pallas_call | solution.py:81
  64.5 3.3 %shard_map.57 = (bf16[3,272,128]{2,1,0:T(8,128)(2,1)S(1)}, bf16[3,272,128]{2,1,0:T(8,128)(2,1)S(1)}) custom-call(s32[2]{0:T(128)S(1)} %add_multiply_fusion.first_ref, bf16[1024,256]{1,0:T(8,128)(2,1)S(1)} %copy-done, bf16[1024,256]{1,0:T(8,128)(2,1)S(1)} %collective-permute-done.k1_ref, bf16[256,1024]{1,0:T(8,128)(2,1)S(1)} %bitcast.14, ...), custom_call_target="tpu_custom_call" | custom-call | tf_op jit(solution)/shard_map/pallas_call | solution.py:81
  67.8 2.4 %collective-permute-start.11 = (bf16[3,272,128]{2,1,0:T(8,128)(2,1)S(1)}, bf16[3,272,128]{2,1,0:T(8,128)(2,1)S(1)}, u32[]{:S(2)}, u32[]{:S(2)}) collective-permute-start(bf16[3,272,128]{2,1,0:T(8,128)(2,1)S(1)} %get-tuple-element.17), channel_id=1, source_target_pairs={{0,2},{1,31},{2,4},{3,1},{4,6},{5,3},{6,8},{7,5},{8,10},{9,7},{10,... | collective-permute-start | bytes 626696 | tf_op jit(solution)/shard_map/ppermute | solution.py:150
  70.2 4.5 %collective-permute-start.12 = (bf16[3,272,128]{2,1,0:T(8,128)(2,1)S(1)}, bf16[3,272,128]{2,1,0:T(8,128)(2,1)S(1)}, u32[]{:S(2)}, u32[]{:S(2)}) collective-permute-start(bf16[3,272,128]{2,1,0:T(8,128)(2,1)S(1)} %get-tuple-element.18), channel_id=1, source_target_pairs={{0,30},{1,3},{2,0},{3,5},{4,2},{5,7},{6,4},{7,9},{8,6},{9,11},{10,... | collective-permute-start | bytes 626696 | tf_op jit(solution)/shard_map/ppermute | solution.py:150
  74.8 6.6 %collective-permute-start.15 = (bf16[1,272,128]{2,1,0:T(8,128)(2,1)S(1)}, bf16[1,272,128]{2,1,0:T(8,128)(2,1)S(1)}, u32[]{:S(2)}, u32[]{:S(2)}) collective-permute-start(bf16[1,272,128]{2,1,0:T(8,128)(2,1)S(1)} %get-tuple-element.16.refs_2_), channel_id=1, source_target_pairs={{0,16},{1,17},{2,18},{3,19},{4,20},{5,21},{6,22},{7,23},{8,24},{9,... | collective-permute-start | bytes 208904 | tf_op jit(solution)/shard_map/ppermute | solution.py:150
  81.6 14.7 %collective-permute-start.13 = (bf16[272,128]{1,0:T(8,128)(2,1)S(1)}, bf16[272,128]{1,0:T(8,128)(2,1)S(1)}, u32[]{:S(2)}, u32[]{:S(2)}) collective-permute-start(bf16[272,128]{1,0:T(8,128)(2,1)S(1)} %get-tuple-element.19), channel_id=1, source_target_pairs={{0,10},{1,23},{2,12},{3,25},{4,14},{5,27},{6,16},{7,29},{8,18},{9,... | collective-permute-start | bytes 208904 | tf_op jit(solution)/shard_map/ppermute | solution.py:150
  96.3 1.9 %collective-permute-start.14 = (bf16[272,128]{1,0:T(8,128)(2,1)S(1)}, bf16[272,128]{1,0:T(8,128)(2,1)S(1)}, u32[]{:S(2)}, u32[]{:S(2)}) collective-permute-start(bf16[272,128]{1,0:T(8,128)(2,1)S(1)} %get-tuple-element.20), channel_id=1, source_target_pairs={{0,22},{1,11},{2,24},{3,13},{4,26},{5,15},{6,28},{7,17},{8,30},{9,... | collective-permute-start | bytes 208904 | tf_op jit(solution)/shard_map/ppermute | solution.py:150
  98.3 0.9 collective-permute-done.13
  99.2 8.9 %collective-permute-done.14 = bf16[272,128]{1,0:T(8,128)(2,1)S(1)} collective-permute-done((bf16[272,128]{1,0:T(8,128)(2,1)S(1)}, bf16[272,128]{1,0:T(8,128)(2,1)S(1)}, u32[]{:S(2)}, u32[]{:S(2)}) %collective-permute-start.14) | collective-permute-done | bytes 69664 | tf_op jit(solution)/shard_map/ppermute | solution.py:150
  108.1 0.9 shard_map.59
  (20 shorter events, 1.9 us)
Async XLA Ops:
  1.6 47.7 %copy-start = (bf16[1024,256]{1,0:T(8,128)(2,1)S(1)}, bf16[1024,256]{1,0:T(8,128)(2,1)}, u32[]{:S(2)}) copy-start(bf16[1024,256]{1,0:T(8,128)(2,1)} %k0_ref.5) | copy-start | bytes 1572868
  1.6 19.1 %collective-permute-start.3 = (bf16[136,256]{1,0:T(8,128)(2,1)S(1)}, bf16[136,256]{1,0:T(8,128)(2,1)S(1)}, u32[]{:S(2)}, u32[]{:S(2)}) collective-permute-start(bf16[136,256]{1,0:T(8,128)(2,1)S(1)} %get-tuple-element.22), channel_id=1, source_target_pairs={{0,10},{1,23},{2,12},{3,25},{4,14},{5,27},{6,16},{7,29},{8,18},{9,... | collective-permute-start | bytes 208904 | tf_op jit(solution)/shard_map/ppermute | solution.py:150
  12.2 11.0 %collective-permute-start.2 = (bf16[136,256]{1,0:T(8,128)(2,1)S(1)}, bf16[136,256]{1,0:T(8,128)(2,1)S(1)}, u32[]{:S(2)}, u32[]{:S(2)}) collective-permute-start(bf16[136,256]{1,0:T(8,128)(2,1)S(1)} %get-tuple-element.22), channel_id=1, source_target_pairs={{0,22},{1,11},{2,24},{3,13},{4,26},{5,15},{6,28},{7,17},{8,30},{9,... | collective-permute-start | bytes 208904 | tf_op jit(solution)/shard_map/ppermute | solution.py:150
  15.0 34.2 %collective-permute-start = (bf16[1024,256]{1,0:T(8,128)(2,1)}, bf16[1024,256]{1,0:T(8,128)(2,1)S(1)}, u32[]{:S(2)}, u32[]{:S(2)}) collective-permute-start(bf16[1024,256]{1,0:T(8,128)(2,1)} %k0_ref.5), channel_id=1, source_target_pairs={{0,1},{1,0},{2,3},{3,2},{4,5},{5,4},{6,7},{7,6},{8,9},{9,8},{10,11... | collective-permute-start | bytes 1572872 | tf_op jit(solution)/shard_map/ppermute | solution.py:159
  18.2 31.1 %collective-permute-start.1 = (bf16[256,1024]{1,0:T(8,128)(2,1)S(1)}, bf16[256,1024]{1,0:T(8,128)(2,1)S(1)}, u32[]{:S(2)}, u32[]{:S(2)}) collective-permute-start(bf16[256,1024]{1,0:T(8,128)(2,1)S(1)} %bitcast.11), channel_id=1, source_target_pairs={{0,1},{1,0},{2,3},{3,2},{4,5},{5,4},{6,7},{7,6},{8,9},{9,8},{10,11... | collective-permute-start | bytes 1572872 | tf_op jit(solution)/shard_map/ppermute | solution.py:160
  23.2 13.3 %collective-permute-start.5 = (bf16[3,136,256]{2,1,0:T(8,128)(2,1)S(1)}, bf16[3,136,256]{2,1,0:T(8,128)(2,1)S(1)}, u32[]{:S(2)}, u32[]{:S(2)}) collective-permute-start(bf16[3,136,256]{2,1,0:T(8,128)(2,1)S(1)} %pad_maximum_fusion.refs_0_), channel_id=1, source_target_pairs={{0,28},{1,5},{2,30},{3,7},{4,0},{5,9},{6,2},{7,11},{8,4},{9,13},{1... | collective-permute-start | bytes 626696 | tf_op jit(solution)/shard_map/ppermute | solution.py:150
  25.3 19.5 %collective-permute-start.6 = (bf16[3,136,256]{2,1,0:T(8,128)(2,1)S(1)}, bf16[3,136,256]{2,1,0:T(8,128)(2,1)S(1)}, u32[]{:S(2)}, u32[]{:S(2)}) collective-permute-start(bf16[3,136,256]{2,1,0:T(8,128)(2,1)S(1)} %pad_maximum_fusion.refs_0_), channel_id=1, source_target_pairs={{0,4},{1,29},{2,6},{3,31},{4,8},{5,1},{6,10},{7,3},{8,12},{9,5},{1... | collective-permute-start | bytes 626696 | tf_op jit(solution)/shard_map/ppermute | solution.py:150
  32.4 32.1 %collective-permute-start.9 = (bf16[3,136,256]{2,1,0:T(8,128)(2,1)S(1)}, bf16[3,136,256]{2,1,0:T(8,128)(2,1)S(1)}, u32[]{:S(2)}, u32[]{:S(2)}) collective-permute-start(bf16[3,136,256]{2,1,0:T(8,128)(2,1)S(1)} %pad_maximum_fusion.refs_0_), channel_id=1, source_target_pairs={{0,30},{1,3},{2,0},{3,5},{4,2},{5,7},{6,4},{7,9},{8,6},{9,11},{10,... | collective-permute-start | bytes 626696 | tf_op jit(solution)/shard_map/ppermute | solution.py:150
  36.5 28.0 %collective-permute-start.10 = (bf16[3,136,256]{2,1,0:T(8,128)(2,1)S(1)}, bf16[3,136,256]{2,1,0:T(8,128)(2,1)S(1)}, u32[]{:S(2)}, u32[]{:S(2)}) collective-permute-start(bf16[3,136,256]{2,1,0:T(8,128)(2,1)S(1)} %pad_maximum_fusion.refs_0_), channel_id=1, source_target_pairs={{0,2},{1,31},{2,4},{3,1},{4,6},{5,3},{6,8},{7,5},{8,10},{9,7},{10,... | collective-permute-start | bytes 626696 | tf_op jit(solution)/shard_map/ppermute | solution.py:150
  44.8 16.9 %collective-permute-start.4 = (bf16[1,136,256]{2,1,0:T(8,128)(2,1)S(1)}, bf16[1,136,256]{2,1,0:T(8,128)(2,1)S(1)}, u32[]{:S(2)}, u32[]{:S(2)}) collective-permute-start(bf16[1,136,256]{2,1,0:T(8,128)(2,1)S(1)} %get-tuple-element.21), channel_id=1, source_target_pairs={{0,16},{1,17},{2,18},{3,19},{4,20},{5,21},{6,22},{7,23},{8,24},{9,... | collective-permute-start | bytes 208904 | tf_op jit(solution)/shard_map/ppermute | solution.py:150
  52.6 28.8 %collective-permute-start.7 = (bf16[3,272,128]{2,1,0:T(8,128)(2,1)S(1)}, bf16[3,272,128]{2,1,0:T(8,128)(2,1)S(1)}, u32[]{:S(2)}, u32[]{:S(2)}) collective-permute-start(bf16[3,272,128]{2,1,0:T(8,128)(2,1)S(1)} %get-tuple-element.13.refs_2_), channel_id=1, source_target_pairs={{0,4},{1,29},{2,6},{3,31},{4,8},{5,1},{6,10},{7,3},{8,12},{9,5},{1... | collective-permute-start | bytes 626696 | tf_op jit(solution)/shard_map/ppermute | solution.py:150
  57.1 24.3 %collective-permute-start.8 = (bf16[3,272,128]{2,1,0:T(8,128)(2,1)S(1)}, bf16[3,272,128]{2,1,0:T(8,128)(2,1)S(1)}, u32[]{:S(2)}, u32[]{:S(2)}) collective-permute-start(bf16[3,272,128]{2,1,0:T(8,128)(2,1)S(1)} %get-tuple-element.15), channel_id=1, source_target_pairs={{0,28},{1,5},{2,30},{3,7},{4,0},{5,9},{6,2},{7,11},{8,4},{9,13},{1... | collective-permute-start | bytes 626696 | tf_op jit(solution)/shard_map/ppermute | solution.py:150
  67.8 13.6 %collective-permute-start.11 = (bf16[3,272,128]{2,1,0:T(8,128)(2,1)S(1)}, bf16[3,272,128]{2,1,0:T(8,128)(2,1)S(1)}, u32[]{:S(2)}, u32[]{:S(2)}) collective-permute-start(bf16[3,272,128]{2,1,0:T(8,128)(2,1)S(1)} %get-tuple-element.17), channel_id=1, source_target_pairs={{0,2},{1,31},{2,4},{3,1},{4,6},{5,3},{6,8},{7,5},{8,10},{9,7},{10,... | collective-permute-start | bytes 626696 | tf_op jit(solution)/shard_map/ppermute | solution.py:150
  70.2 11.2 %collective-permute-start.12 = (bf16[3,272,128]{2,1,0:T(8,128)(2,1)S(1)}, bf16[3,272,128]{2,1,0:T(8,128)(2,1)S(1)}, u32[]{:S(2)}, u32[]{:S(2)}) collective-permute-start(bf16[3,272,128]{2,1,0:T(8,128)(2,1)S(1)} %get-tuple-element.18), channel_id=1, source_target_pairs={{0,30},{1,3},{2,0},{3,5},{4,2},{5,7},{6,4},{7,9},{8,6},{9,11},{10,... | collective-permute-start | bytes 626696 | tf_op jit(solution)/shard_map/ppermute | solution.py:150
  74.8 23.5 %collective-permute-start.15 = (bf16[1,272,128]{2,1,0:T(8,128)(2,1)S(1)}, bf16[1,272,128]{2,1,0:T(8,128)(2,1)S(1)}, u32[]{:S(2)}, u32[]{:S(2)}) collective-permute-start(bf16[1,272,128]{2,1,0:T(8,128)(2,1)S(1)} %get-tuple-element.16.refs_2_), channel_id=1, source_target_pairs={{0,16},{1,17},{2,18},{3,19},{4,20},{5,21},{6,22},{7,23},{8,24},{9,... | collective-permute-start | bytes 208904 | tf_op jit(solution)/shard_map/ppermute | solution.py:150
  81.6 17.5 %collective-permute-start.13 = (bf16[272,128]{1,0:T(8,128)(2,1)S(1)}, bf16[272,128]{1,0:T(8,128)(2,1)S(1)}, u32[]{:S(2)}, u32[]{:S(2)}) collective-permute-start(bf16[272,128]{1,0:T(8,128)(2,1)S(1)} %get-tuple-element.19), channel_id=1, source_target_pairs={{0,10},{1,23},{2,12},{3,25},{4,14},{5,27},{6,16},{7,29},{8,18},{9,... | collective-permute-start | bytes 208904 | tf_op jit(solution)/shard_map/ppermute | solution.py:150
  96.3 11.8 %collective-permute-start.14 = (bf16[272,128]{1,0:T(8,128)(2,1)S(1)}, bf16[272,128]{1,0:T(8,128)(2,1)S(1)}, u32[]{:S(2)}, u32[]{:S(2)}) collective-permute-start(bf16[272,128]{1,0:T(8,128)(2,1)S(1)} %get-tuple-element.20), channel_id=1, source_target_pairs={{0,22},{1,11},{2,24},{3,13},{4,26},{5,15},{6,28},{7,17},{8,30},{9,... | collective-permute-start | bytes 208904 | tf_op jit(solution)/shard_map/ppermute | solution.py:150

commit v11 on v8

--- a/solution.py
+++ b/solution.py
@@ -100,25 +100,22 @@
     return total, top + jnp.log(mixed)
 
 
-def near_kernel(*refs):
-    *parts, extra, out1_ref, out2_ref = refs
-    width = out1_ref.shape[0] - TAIL
-    for slot, out_ref in ((1, out1_ref), (2, out2_ref)):
-        blocks = [ref[slot] for ref in parts] + ([extra[0]] if slot == 1 else [])
-        total, lse = mix(blocks)
-        out_ref[:width, :] = total.astype(jnp.bfloat16)
-        out_ref[width:, :] = tail_rows(lse)
+def near_kernel(slot, count, *refs):
+    *parts, out_ref = refs
+    width = out_ref.shape[0] - TAIL
+    total, lse = mix([ref[slot if i < count else 0] for i, ref in enumerate(parts)])
+    out_ref[:width, :] = total.astype(jnp.bfloat16)
+    out_ref[width:, :] = tail_rows(lse)
 
 
-def near_merge(parts, extra):
-    shape = jax.ShapeDtypeStruct(extra.shape[1:], extra.dtype)
+def near_merge(slot, parts, *extra):
     return pl.pallas_call(
-        near_kernel,
-        in_specs=[VMEM] * (len(parts) + 1),
-        out_specs=[VMEM] * 2,
-        out_shape=[shape] * 2,
+        functools.partial(near_kernel, slot, len(parts)),
+        in_specs=[VMEM] * (len(parts) + len(extra)),
+        out_specs=VMEM,
+        out_shape=jax.ShapeDtypeStruct(parts[0].shape[1:], parts[0].dtype),
         compiler_params=PARAMS,
-    )(*parts, extra)
+    )(*parts, *extra)
 
 
 def far_kernel(*refs):
@@ -174,8 +171,9 @@
     part_up1, part_down1 = attend(first, (up1, down1), keys, vts, cand, (part_eight,))
     back += [shift(part_up1, 1), shift(part_down1, -1)]
     parts = [part_own] + back
-    slot1, slot2 = near_merge(parts, extra)
-    return far_merge(parts, shift(slot1, 5), shift(slot2, -5))
+    two = shift(near_merge(2, parts), -5)
+    one = shift(near_merge(1, parts, extra), 5)
+    return far_merge(parts, one, two)
 
 
 def solution(mesh):

time: 105 us -> 105 us (level)
  waiting for transfers between devices: 14.4 us -> 25 us
  starting transfers between devices: 75.6 us -> 65.8 us
    ppermute x14, waiting for transfers between devices: 14.4 us -> 25 us  [shift(): return lax.ppermute(x, ('z', 'core'), pairs)]
    ppermute x14, starting transfers between devices: 71.3 us -> 61.5 us  [shift(): return lax.ppermute(x, ('z', 'core'), pairs)]
  transfers between devices with their start and end apart: 16 -> 16, of which waited for: 4 -> 6; matrix products, arithmetic and copies ran while one was open for 1% -> 1% of each run, Pallas kernels for 9% -> 6%
where the time goes in v11:
time: 105 us; the launch traced here: 104 us
  starting transfers between devices  65.8 us (63%)
  waiting for transfers between devices  25 us (24%)
  Pallas kernels  10.3 us (10%)
  other arithmetic  1.66 us (2%)
  local copies, waits for them, and re-layouts  1.25 us (1%)
    ppermute x14, starting transfers between devices, shift(): return lax.ppermute(x, ('z', 'core'), pairs)  61.5 us
    ppermute x14, waiting for transfers between devices, shift(): return lax.ppermute(x, ('z', 'core'), pairs)  25 us
    pallas_call x3, Pallas kernels, attend(): pl.pallas_call(functools.partial(attend_kernel, counts), in_specs=[SMEM]...  9.27 us
    ppermute x1, starting transfers between devices, body(): keys = (hist_keys, lax.ppermute(hist_keys, 'core', swap))  2.41 us
  transfers between devices with their start and end apart: 16, of which 6 were waited for; matrix products, arithmetic and copies ran while one was open for 1% of the time, Pallas kernels for 6%

profile of v11, /device:TPU:6, one launch (start us, length us, event | category | flops | bytes accessed | tf_op | source)
XLA Modules:
  0.0 104.4 jit_solution(7377963768039628400)
XLA Ops:
  1.6 14.5 %collective-permute-start.2 = (bf16[136,256]{1,0:T(8,128)(2,1)S(1)}, bf16[136,256]{1,0:T(8,128)(2,1)S(1)}, u32[]{:S(2)}, u32[]{:S(2)}) collective-permute-start(bf16[136,256]{1,0:T(8,128)(2,1)S(1)} %get-tuple-element.18), channel_id=1, source_target_pairs={{0,22},{1,11},{2,24},{3,13},{4,26},{5,15},{6,28},{7,17},{8,30},{9,... | collective-permute-start | bytes 208904 | tf_op jit(solution)/shard_map/ppermute | solution.py:148
  16.1 1.9 %collective-permute-start.3 = (bf16[136,256]{1,0:T(8,128)(2,1)S(1)}, bf16[136,256]{1,0:T(8,128)(2,1)S(1)}, u32[]{:S(2)}, u32[]{:S(2)}) collective-permute-start(bf16[136,256]{1,0:T(8,128)(2,1)S(1)} %get-tuple-element.18), channel_id=1, source_target_pairs={{0,10},{1,23},{2,12},{3,25},{4,14},{5,27},{6,16},{7,29},{8,18},{9,... | collective-permute-start | bytes 208904 | tf_op jit(solution)/shard_map/ppermute | solution.py:148
  19.3 1.9 %collective-permute-start.1 = (bf16[256,1024]{1,0:T(8,128)(2,1)S(1)}, bf16[256,1024]{1,0:T(8,128)(2,1)S(1)}, u32[]{:S(2)}, u32[]{:S(2)}) collective-permute-start(bf16[256,1024]{1,0:T(8,128)(2,1)S(1)} %bitcast.9), channel_id=1, source_target_pairs={{0,1},{1,0},{2,3},{3,2},{4,5},{5,4},{6,7},{7,6},{8,9},{9,8},{10,11... | collective-permute-start | bytes 1572872 | tf_op jit(solution)/shard_map/ppermute | solution.py:157
  21.2 2.4 %collective-permute-start = (bf16[1024,256]{1,0:T(8,128)(2,1)S(1)}, bf16[1024,256]{1,0:T(8,128)(2,1)S(1)}, u32[]{:S(2)}, u32[]{:S(2)}) collective-permute-start(bf16[1024,256]{1,0:T(8,128)(2,1)S(1)} %copy-done), channel_id=1, source_target_pairs={{0,1},{1,0},{2,3},{3,2},{4,5},{5,4},{6,7},{7,6},{8,9},{9,8},{10,11... | collective-permute-start | bytes 1572872 | tf_op jit(solution)/shard_map/ppermute | solution.py:156
  23.6 5.5 %collective-permute-done.3 = bf16[136,256]{1,0:T(8,128)(2,1)S(1)} collective-permute-done((bf16[136,256]{1,0:T(8,128)(2,1)S(1)}, bf16[136,256]{1,0:T(8,128)(2,1)S(1)}, u32[]{:S(2)}, u32[]{:S(2)}) %collective-permute-start.3) | collective-permute-done | bytes 69664 | tf_op jit(solution)/shard_map/ppermute | solution.py:148
  29.2 1.9 %collective-permute-start.6 = (bf16[3,136,256]{2,1,0:T(8,128)(2,1)S(1)}, bf16[3,136,256]{2,1,0:T(8,128)(2,1)S(1)}, u32[]{:S(2)}, u32[]{:S(2)}) collective-permute-start(bf16[3,136,256]{2,1,0:T(8,128)(2,1)S(1)} %pad_maximum_fusion.refs_0_), channel_id=1, source_target_pairs={{0,4},{1,29},{2,6},{3,31},{4,8},{5,1},{6,10},{7,3},{8,12},{9,5},{1... | collective-permute-start | bytes 626696 | tf_op jit(solution)/shard_map/ppermute | solution.py:148
  31.1 6.0 %collective-permute-start.5 = (bf16[3,136,256]{2,1,0:T(8,128)(2,1)S(1)}, bf16[3,136,256]{2,1,0:T(8,128)(2,1)S(1)}, u32[]{:S(2)}, u32[]{:S(2)}) collective-permute-start(bf16[3,136,256]{2,1,0:T(8,128)(2,1)S(1)} %pad_maximum_fusion.refs_0_), channel_id=1, source_target_pairs={{0,28},{1,5},{2,30},{3,7},{4,0},{5,9},{6,2},{7,11},{8,4},{9,13},{1... | collective-permute-start | bytes 626696 | tf_op jit(solution)/shard_map/ppermute | solution.py:148
  37.2 1.9 %collective-permute-start.10 = (bf16[3,136,256]{2,1,0:T(8,128)(2,1)S(1)}, bf16[3,136,256]{2,1,0:T(8,128)(2,1)S(1)}, u32[]{:S(2)}, u32[]{:S(2)}) collective-permute-start(bf16[3,136,256]{2,1,0:T(8,128)(2,1)S(1)} %pad_maximum_fusion.refs_0_), channel_id=1, source_target_pairs={{0,2},{1,31},{2,4},{3,1},{4,6},{5,3},{6,8},{7,5},{8,10},{9,7},{10,... | collective-permute-start | bytes 626696 | tf_op jit(solution)/shard_map/ppermute | solution.py:148
  39.1 6.6 %collective-permute-done.6.refs_1_ = bf16[3,136,256]{2,1,0:T(8,128)(2,1)S(1)} collective-permute-done((bf16[3,136,256]{2,1,0:T(8,128)(2,1)S(1)}, bf16[3,136,256]{2,1,0:T(8,128)(2,1)S(1)}, u32[]{:S(2)}, u32[]{:S(2)}) %collective-permute-start.6) | collective-permute-done | bytes 208928 | tf_op jit(solution)/shard_map/ppermute | solution.py:148
  45.7 2.0 %collective-permute-start.9 = (bf16[3,136,256]{2,1,0:T(8,128)(2,1)S(1)}, bf16[3,136,256]{2,1,0:T(8,128)(2,1)S(1)}, u32[]{:S(2)}, u32[]{:S(2)}) collective-permute-start(bf16[3,136,256]{2,1,0:T(8,128)(2,1)S(1)} %pad_maximum_fusion.refs_0_), channel_id=1, source_target_pairs={{0,30},{1,3},{2,0},{3,5},{4,2},{5,7},{6,4},{7,9},{8,6},{9,11},{10,... | collective-permute-start | bytes 626696 | tf_op jit(solution)/shard_map/ppermute | solution.py:148
  47.7 4.8 %collective-permute-start.4 = (bf16[1,136,256]{2,1,0:T(8,128)(2,1)S(1)}, bf16[1,136,256]{2,1,0:T(8,128)(2,1)S(1)}, u32[]{:S(2)}, u32[]{:S(2)}) collective-permute-start(bf16[1,136,256]{2,1,0:T(8,128)(2,1)S(1)} %bitcast.14), channel_id=1, source_target_pairs={{0,26},{1,7},{2,28},{3,9},{4,30},{5,11},{6,0},{7,13},{8,2},{9,15},... | collective-permute-start | bytes 208904 | tf_op jit(solution)/shard_map/ppermute | solution.py:148
  52.5 3.3 %shard_map.55 = (bf16[3,272,128]{2,1,0:T(8,128)(2,1)S(1)}, bf16[3,272,128]{2,1,0:T(8,128)(2,1)S(1)}) custom-call(s32[2]{0:T(128)S(1)} %add_multiply_fusion.first_ref, bf16[1024,256]{1,0:T(8,128)(2,1)S(1)} %copy-done, bf16[1024,256]{1,0:T(8,128)(2,1)S(1)} %collective-permute-done.k1_ref, bf16[256,1024]{1,0:T(8,128)(2,1)S(1)} %bitcast.10, ...), custom_call_target="tpu_custom_call" | custom-call | tf_op jit(solution)/shard_map/pallas_call | solution.py:81
  55.8 2.7 %shard_map.56 = (bf16[3,272,128]{2,1,0:T(8,128)(2,1)S(1)}, bf16[1,272,128]{2,1,0:T(8,128)(2,1)S(1)}) custom-call(s32[2]{0:T(128)S(1)} %add_multiply_fusion.first_ref, bf16[1024,256]{1,0:T(8,128)(2,1)S(1)} %copy-done, bf16[1024,256]{1,0:T(8,128)(2,1)S(1)} %collective-permute-done.k1_ref, bf16[256,1024]{1,0:T(8,128)(2,1)S(1)} %bitcast.11, ...), custom_call_target="tpu_custom_call" | custom-call | tf_op jit(solution)/shard_map/pallas_call | solution.py:81
  58.6 3.3 %shard_map.57 = (bf16[3,272,128]{2,1,0:T(8,128)(2,1)S(1)}, bf16[3,272,128]{2,1,0:T(8,128)(2,1)S(1)}) custom-call(s32[2]{0:T(128)S(1)} %add_multiply_fusion.first_ref, bf16[1024,256]{1,0:T(8,128)(2,1)S(1)} %copy-done, bf16[1024,256]{1,0:T(8,128)(2,1)S(1)} %collective-permute-done.k1_ref, bf16[256,1024]{1,0:T(8,128)(2,1)S(1)} %bitcast.12, ...), custom_call_target="tpu_custom_call" | custom-call | tf_op jit(solution)/shard_map/pallas_call | solution.py:81
  61.8 5.3 %collective-permute-start.11 = (bf16[3,272,128]{2,1,0:T(8,128)(2,1)S(1)}, bf16[3,272,128]{2,1,0:T(8,128)(2,1)S(1)}, u32[]{:S(2)}, u32[]{:S(2)}) collective-permute-start(bf16[3,272,128]{2,1,0:T(8,128)(2,1)S(1)} %get-tuple-element.15), channel_id=1, source_target_pairs={{0,2},{1,31},{2,4},{3,1},{4,6},{5,3},{6,8},{7,5},{8,10},{9,7},{10,... | collective-permute-start | bytes 626696 | tf_op jit(solution)/shard_map/ppermute | solution.py:148
  67.1 1.9 %collective-permute-start.12 = (bf16[3,272,128]{2,1,0:T(8,128)(2,1)S(1)}, bf16[3,272,128]{2,1,0:T(8,128)(2,1)S(1)}, u32[]{:S(2)}, u32[]{:S(2)}) collective-permute-start(bf16[3,272,128]{2,1,0:T(8,128)(2,1)S(1)} %get-tuple-element.16), channel_id=1, source_target_pairs={{0,30},{1,3},{2,0},{3,5},{4,2},{5,7},{6,4},{7,9},{8,6},{9,11},{10,... | collective-permute-start | bytes 626696 | tf_op jit(solution)/shard_map/ppermute | solution.py:148
  69.0 3.5 %collective-permute-start.8 = (bf16[3,272,128]{2,1,0:T(8,128)(2,1)S(1)}, bf16[3,272,128]{2,1,0:T(8,128)(2,1)S(1)}, u32[]{:S(2)}, u32[]{:S(2)}) collective-permute-start(bf16[3,272,128]{2,1,0:T(8,128)(2,1)S(1)} %get-tuple-element.13), channel_id=1, source_target_pairs={{0,28},{1,5},{2,30},{3,7},{4,0},{5,9},{6,2},{7,11},{8,4},{9,13},{1... | collective-permute-start | bytes 626696 | tf_op jit(solution)/shard_map/ppermute | solution.py:148
  72.5 3.3 %collective-permute-start.7 = (bf16[3,272,128]{2,1,0:T(8,128)(2,1)S(1)}, bf16[3,272,128]{2,1,0:T(8,128)(2,1)S(1)}, u32[]{:S(2)}, u32[]{:S(2)}) collective-permute-start(bf16[3,272,128]{2,1,0:T(8,128)(2,1)S(1)} %get-tuple-element.11.refs_2_), channel_id=1, source_target_pairs={{0,4},{1,29},{2,6},{3,31},{4,8},{5,1},{6,10},{7,3},{8,12},{9,5},{1... | collective-permute-start | bytes 626696 | tf_op jit(solution)/shard_map/ppermute | solution.py:148
  75.8 3.9 %collective-permute-start.13 = (bf16[1,272,128]{2,1,0:T(8,128)(2,1)S(1)}, bf16[1,272,128]{2,1,0:T(8,128)(2,1)S(1)}, u32[]{:S(2)}, u32[]{:S(2)}) collective-permute-start(bf16[1,272,128]{2,1,0:T(8,128)(2,1)S(1)} %get-tuple-element.14.refs_2_), channel_id=1, source_target_pairs={{0,6},{1,27},{2,8},{3,29},{4,10},{5,31},{6,12},{7,1},{8,14},{9,3},... | collective-permute-start | bytes 208904 | tf_op jit(solution)/shard_map/ppermute | solution.py:148
  79.7 5.4 %collective-permute-done.8.refs_2_ = bf16[3,272,128]{2,1,0:T(8,128)(2,1)S(1)} collective-permute-done((bf16[3,272,128]{2,1,0:T(8,128)(2,1)S(1)}, bf16[3,272,128]{2,1,0:T(8,128)(2,1)S(1)}, u32[]{:S(2)}, u32[]{:S(2)}) %collective-permute-start.8) | collective-permute-done | bytes 208928 | tf_op jit(solution)/shard_map/ppermute | solution.py:148
  85.6 5.1 %collective-permute-start.15 = (bf16[272,128]{1,0:T(8,128)(2,1)S(1)}, bf16[272,128]{1,0:T(8,128)(2,1)S(1)}, u32[]{:S(2)}, u32[]{:S(2)}) collective-permute-start(bf16[272,128]{1,0:T(8,128)(2,1)S(1)} %shard_map.59), channel_id=1, source_target_pairs={{0,22},{1,11},{2,24},{3,13},{4,26},{5,15},{6,28},{7,17},{8,30},{9,... | collective-permute-start | bytes 208904 | tf_op jit(solution)/shard_map/ppermute | solution.py:148
  90.9 5.5 %collective-permute-start.14 = (bf16[272,128]{1,0:T(8,128)(2,1)S(1)}, bf16[272,128]{1,0:T(8,128)(2,1)S(1)}, u32[]{:S(2)}, u32[]{:S(2)}) collective-permute-start(bf16[272,128]{1,0:T(8,128)(2,1)S(1)} %shard_map.58), channel_id=1, source_target_pairs={{0,10},{1,23},{2,12},{3,25},{4,14},{5,27},{6,16},{7,29},{8,18},{9,... | collective-permute-start | bytes 208904 | tf_op jit(solution)/shard_map/ppermute | solution.py:148
  96.4 1.5 %collective-permute-done.15.refs_6_ = bf16[272,128]{1,0:T(8,128)(2,1)S(1)} collective-permute-done((bf16[272,128]{1,0:T(8,128)(2,1)S(1)}, bf16[272,128]{1,0:T(8,128)(2,1)S(1)}, u32[]{:S(2)}, u32[]{:S(2)}) %collective-permute-start.15) | collective-permute-done | bytes 69664 | tf_op jit(solution)/shard_map/ppermute | solution.py:148
  97.9 5.6 %collective-permute-done.14.refs_5_ = bf16[272,128]{1,0:T(8,128)(2,1)S(1)} collective-permute-done((bf16[272,128]{1,0:T(8,128)(2,1)S(1)}, bf16[272,128]{1,0:T(8,128)(2,1)S(1)}, u32[]{:S(2)}, u32[]{:S(2)}) %collective-permute-start.14) | collective-permute-done | bytes 69664 | tf_op jit(solution)/shard_map/ppermute | solution.py:148
  (21 shorter events, 4.4 us)
Async XLA Ops:
  1.6 19.7 %copy-start = (bf16[1024,256]{1,0:T(8,128)(2,1)S(1)}, bf16[1024,256]{1,0:T(8,128)(2,1)}, u32[]{:S(2)}) copy-start(bf16[1024,256]{1,0:T(8,128)(2,1)} %k0_ref.5) | copy-start | bytes 1572868
  1.6 22.1 %collective-permute-start.2 = (bf16[136,256]{1,0:T(8,128)(2,1)S(1)}, bf16[136,256]{1,0:T(8,128)(2,1)S(1)}, u32[]{:S(2)}, u32[]{:S(2)}) collective-permute-start(bf16[136,256]{1,0:T(8,128)(2,1)S(1)} %get-tuple-element.18), channel_id=1, source_target_pairs={{0,22},{1,11},{2,24},{3,13},{4,26},{5,15},{6,28},{7,17},{8,30},{9,... | collective-permute-start | bytes 208904 | tf_op jit(solution)/shard_map/ppermute | solution.py:148
  16.1 13.1 %collective-permute-start.3 = (bf16[136,256]{1,0:T(8,128)(2,1)S(1)}, bf16[136,256]{1,0:T(8,128)(2,1)S(1)}, u32[]{:S(2)}, u32[]{:S(2)}) collective-permute-start(bf16[136,256]{1,0:T(8,128)(2,1)S(1)} %get-tuple-element.18), channel_id=1, source_target_pairs={{0,10},{1,23},{2,12},{3,25},{4,14},{5,27},{6,16},{7,29},{8,18},{9,... | collective-permute-start | bytes 208904 | tf_op jit(solution)/shard_map/ppermute | solution.py:148
  19.3 33.2 %collective-permute-start.1 = (bf16[256,1024]{1,0:T(8,128)(2,1)S(1)}, bf16[256,1024]{1,0:T(8,128)(2,1)S(1)}, u32[]{:S(2)}, u32[]{:S(2)}) collective-permute-start(bf16[256,1024]{1,0:T(8,128)(2,1)S(1)} %bitcast.9), channel_id=1, source_target_pairs={{0,1},{1,0},{2,3},{3,2},{4,5},{5,4},{6,7},{7,6},{8,9},{9,8},{10,11... | collective-permute-start | bytes 1572872 | tf_op jit(solution)/shard_map/ppermute | solution.py:157
  21.2 31.3 %collective-permute-start = (bf16[1024,256]{1,0:T(8,128)(2,1)S(1)}, bf16[1024,256]{1,0:T(8,128)(2,1)S(1)}, u32[]{:S(2)}, u32[]{:S(2)}) collective-permute-start(bf16[1024,256]{1,0:T(8,128)(2,1)S(1)} %copy-done), channel_id=1, source_target_pairs={{0,1},{1,0},{2,3},{3,2},{4,5},{5,4},{6,7},{7,6},{8,9},{9,8},{10,11... | collective-permute-start | bytes 1572872 | tf_op jit(solution)/shard_map/ppermute | solution.py:156
  29.2 16.5 %collective-permute-start.6 = (bf16[3,136,256]{2,1,0:T(8,128)(2,1)S(1)}, bf16[3,136,256]{2,1,0:T(8,128)(2,1)S(1)}, u32[]{:S(2)}, u32[]{:S(2)}) collective-permute-start(bf16[3,136,256]{2,1,0:T(8,128)(2,1)S(1)} %pad_maximum_fusion.refs_0_), channel_id=1, source_target_pairs={{0,4},{1,29},{2,6},{3,31},{4,8},{5,1},{6,10},{7,3},{8,12},{9,5},{1... | collective-permute-start | bytes 626696 | tf_op jit(solution)/shard_map/ppermute | solution.py:148
  31.1 16.5 %collective-permute-start.5 = (bf16[3,136,256]{2,1,0:T(8,128)(2,1)S(1)}, bf16[3,136,256]{2,1,0:T(8,128)(2,1)S(1)}, u32[]{:S(2)}, u32[]{:S(2)}) collective-permute-start(bf16[3,136,256]{2,1,0:T(8,128)(2,1)S(1)} %pad_maximum_fusion.refs_0_), channel_id=1, source_target_pairs={{0,28},{1,5},{2,30},{3,7},{4,0},{5,9},{6,2},{7,11},{8,4},{9,13},{1... | collective-permute-start | bytes 626696 | tf_op jit(solution)/shard_map/ppermute | solution.py:148
  37.2 21.4 %collective-permute-start.10 = (bf16[3,136,256]{2,1,0:T(8,128)(2,1)S(1)}, bf16[3,136,256]{2,1,0:T(8,128)(2,1)S(1)}, u32[]{:S(2)}, u32[]{:S(2)}) collective-permute-start(bf16[3,136,256]{2,1,0:T(8,128)(2,1)S(1)} %pad_maximum_fusion.refs_0_), channel_id=1, source_target_pairs={{0,2},{1,31},{2,4},{3,1},{4,6},{5,3},{6,8},{7,5},{8,10},{9,7},{10,... | collective-permute-start | bytes 626696 | tf_op jit(solution)/shard_map/ppermute | solution.py:148
  45.7 12.9 %collective-permute-start.9 = (bf16[3,136,256]{2,1,0:T(8,128)(2,1)S(1)}, bf16[3,136,256]{2,1,0:T(8,128)(2,1)S(1)}, u32[]{:S(2)}, u32[]{:S(2)}) collective-permute-start(bf16[3,136,256]{2,1,0:T(8,128)(2,1)S(1)} %pad_maximum_fusion.refs_0_), channel_id=1, source_target_pairs={{0,30},{1,3},{2,0},{3,5},{4,2},{5,7},{6,4},{7,9},{8,6},{9,11},{10,... | collective-permute-start | bytes 626696 | tf_op jit(solution)/shard_map/ppermute | solution.py:148
  47.7 8.1 %collective-permute-start.4 = (bf16[1,136,256]{2,1,0:T(8,128)(2,1)S(1)}, bf16[1,136,256]{2,1,0:T(8,128)(2,1)S(1)}, u32[]{:S(2)}, u32[]{:S(2)}) collective-permute-start(bf16[1,136,256]{2,1,0:T(8,128)(2,1)S(1)} %bitcast.14), channel_id=1, source_target_pairs={{0,26},{1,7},{2,28},{3,9},{4,30},{5,11},{6,0},{7,13},{8,2},{9,15},... | collective-permute-start | bytes 208904 | tf_op jit(solution)/shard_map/ppermute | solution.py:148
  61.8 17.9 %collective-permute-start.11 = (bf16[3,272,128]{2,1,0:T(8,128)(2,1)S(1)}, bf16[3,272,128]{2,1,0:T(8,128)(2,1)S(1)}, u32[]{:S(2)}, u32[]{:S(2)}) collective-permute-start(bf16[3,272,128]{2,1,0:T(8,128)(2,1)S(1)} %get-tuple-element.15), channel_id=1, source_target_pairs={{0,2},{1,31},{2,4},{3,1},{4,6},{5,3},{6,8},{7,5},{8,10},{9,7},{10,... | collective-permute-start | bytes 626696 | tf_op jit(solution)/shard_map/ppermute | solution.py:148
  67.1 12.6 %collective-permute-start.12 = (bf16[3,272,128]{2,1,0:T(8,128)(2,1)S(1)}, bf16[3,272,128]{2,1,0:T(8,128)(2,1)S(1)}, u32[]{:S(2)}, u32[]{:S(2)}) collective-permute-start(bf16[3,272,128]{2,1,0:T(8,128)(2,1)S(1)} %get-tuple-element.16), channel_id=1, source_target_pairs={{0,30},{1,3},{2,0},{3,5},{4,2},{5,7},{6,4},{7,9},{8,6},{9,11},{10,... | collective-permute-start | bytes 626696 | tf_op jit(solution)/shard_map/ppermute | solution.py:148
  69.0 16.1 %collective-permute-start.8 = (bf16[3,272,128]{2,1,0:T(8,128)(2,1)S(1)}, bf16[3,272,128]{2,1,0:T(8,128)(2,1)S(1)}, u32[]{:S(2)}, u32[]{:S(2)}) collective-permute-start(bf16[3,272,128]{2,1,0:T(8,128)(2,1)S(1)} %get-tuple-element.13), channel_id=1, source_target_pairs={{0,28},{1,5},{2,30},{3,7},{4,0},{5,9},{6,2},{7,11},{8,4},{9,13},{1... | collective-permute-start | bytes 626696 | tf_op jit(solution)/shard_map/ppermute | solution.py:148
  72.5 13.0 %collective-permute-start.7 = (bf16[3,272,128]{2,1,0:T(8,128)(2,1)S(1)}, bf16[3,272,128]{2,1,0:T(8,128)(2,1)S(1)}, u32[]{:S(2)}, u32[]{:S(2)}) collective-permute-start(bf16[3,272,128]{2,1,0:T(8,128)(2,1)S(1)} %get-tuple-element.11.refs_2_), channel_id=1, source_target_pairs={{0,4},{1,29},{2,6},{3,31},{4,8},{5,1},{6,10},{7,3},{8,12},{9,5},{1... | collective-permute-start | bytes 626696 | tf_op jit(solution)/shard_map/ppermute | solution.py:148
  75.8 15.0 %collective-permute-start.13 = (bf16[1,272,128]{2,1,0:T(8,128)(2,1)S(1)}, bf16[1,272,128]{2,1,0:T(8,128)(2,1)S(1)}, u32[]{:S(2)}, u32[]{:S(2)}) collective-permute-start(bf16[1,272,128]{2,1,0:T(8,128)(2,1)S(1)} %get-tuple-element.14.refs_2_), channel_id=1, source_target_pairs={{0,6},{1,27},{2,8},{3,29},{4,10},{5,31},{6,12},{7,1},{8,14},{9,3},... | collective-permute-start | bytes 208904 | tf_op jit(solution)/shard_map/ppermute | solution.py:148
  85.6 12.3 %collective-permute-start.15 = (bf16[272,128]{1,0:T(8,128)(2,1)S(1)}, bf16[272,128]{1,0:T(8,128)(2,1)S(1)}, u32[]{:S(2)}, u32[]{:S(2)}) collective-permute-start(bf16[272,128]{1,0:T(8,128)(2,1)S(1)} %shard_map.59), channel_id=1, source_target_pairs={{0,22},{1,11},{2,24},{3,13},{4,26},{5,15},{6,28},{7,17},{8,30},{9,... | collective-permute-start | bytes 208904 | tf_op jit(solution)/shard_map/ppermute | solution.py:148
  90.9 12.6 %collective-permute-start.14 = (bf16[272,128]{1,0:T(8,128)(2,1)S(1)}, bf16[272,128]{1,0:T(8,128)(2,1)S(1)}, u32[]{:S(2)}, u32[]{:S(2)}) collective-permute-start(bf16[272,128]{1,0:T(8,128)(2,1)S(1)} %shard_map.58), channel_id=1, source_target_pairs={{0,10},{1,23},{2,12},{3,25},{4,14},{5,27},{6,16},{7,29},{8,18},{9,... | collective-permute-start | bytes 208904 | tf_op jit(solution)/shard_map/ppermute | solution.py:148

commit v12 on v11

--- a/solution.py
+++ b/solution.py
@@ -164,12 +164,11 @@
     eight = shift(up5[None], -3)
     up1, down1 = shift(own, -1), shift(own, 1)
 
-    part_up2, part_down2 = attend(first, (up2, down2), keys, vts, cand)
-    back = [shift(part_up2, 2), shift(part_down2, -2)]
-    part_own, part_eight = attend(first, (own, eight), keys, vts, cand, (part_up2,))
+    part_up2, part_down2, part_eight, part_up1, part_down1, part_own = attend(
+        first, (up2, down2, eight, up1, down1, own), keys, vts, cand
+    )
+    back = [shift(part_up2, 2), shift(part_down2, -2), shift(part_up1, 1), shift(part_down1, -1)]
     extra = shift(part_eight, 3)
-    part_up1, part_down1 = attend(first, (up1, down1), keys, vts, cand, (part_eight,))
-    back += [shift(part_up1, 1), shift(part_down1, -1)]
     parts = [part_own] + back
     two = shift(near_merge(2, parts), -5)
     one = shift(near_merge(1, parts, extra), 5)

time: 105 us -> 104 us (level)
  Pallas kernels: 10.3 us -> 7.17 us
  waiting for transfers between devices: 25 us -> 27.3 us
    pallas_call x3 -> x1, Pallas kernels: 9.27 us -> 6.1 us  [attend(): pl.pallas_call(functools.partial(attend_kernel, counts), in_specs=[SMEM]...]
    ppermute x14, waiting for transfers between devices: 25 us -> 27.3 us  [shift(): return lax.ppermute(x, ('z', 'core'), pairs)]
  transfers between devices with their start and end apart: 16 -> 16, of which waited for: 6 -> 7; matrix products, arithmetic and copies ran while one was open for 1% -> 1% of each run, Pallas kernels for 6% -> 0%
where the time goes in v12:
time: 104 us; the launch traced here: 103 us
  starting transfers between devices  65.3 us (63%)
  waiting for transfers between devices  27.3 us (26%)
  Pallas kernels  7.17 us (7%)
  other arithmetic  1.66 us (2%)
  local copies, waits for them, and re-layouts  1.25 us (1%)
    ppermute x14, starting transfers between devices, shift(): return lax.ppermute(x, ('z', 'core'), pairs)  60.9 us
    ppermute x14, waiting for transfers between devices, shift(): return lax.ppermute(x, ('z', 'core'), pairs)  27.3 us
    pallas_call x1, Pallas kernels, attend(): pl.pallas_call(functools.partial(attend_kernel, counts), in_specs=[SMEM]...  6.1 us
    ppermute x1, starting transfers between devices, body(): keys = (hist_keys, lax.ppermute(hist_keys, 'core', swap))  2.41 us
  transfers between devices with their start and end apart: 16, of which 7 were waited for; matrix products, arithmetic and copies ran while one was open for 1% of the time, Pallas kernels for 0%

profile of v12, /device:TPU:6, one launch (start us, length us, event | category | flops | bytes accessed | tf_op | source)
XLA Modules:
  0.0 102.9 jit_solution(5424614467339660177)
XLA Ops:
  1.6 14.5 %collective-permute-start.2 = (bf16[136,256]{1,0:T(8,128)(2,1)S(1)}, bf16[136,256]{1,0:T(8,128)(2,1)S(1)}, u32[]{:S(2)}, u32[]{:S(2)}) collective-permute-start(bf16[136,256]{1,0:T(8,128)(2,1)S(1)} %get-tuple-element.18), channel_id=1, source_target_pairs={{0,22},{1,11},{2,24},{3,13},{4,26},{5,15},{6,28},{7,17},{8,30},{9,... | collective-permute-start | bytes 208904 | tf_op jit(solution)/shard_map/ppermute | solution.py:148
  16.1 1.9 %collective-permute-start.3 = (bf16[136,256]{1,0:T(8,128)(2,1)S(1)}, bf16[136,256]{1,0:T(8,128)(2,1)S(1)}, u32[]{:S(2)}, u32[]{:S(2)}) collective-permute-start(bf16[136,256]{1,0:T(8,128)(2,1)S(1)} %get-tuple-element.18), channel_id=1, source_target_pairs={{0,10},{1,23},{2,12},{3,25},{4,14},{5,27},{6,16},{7,29},{8,18},{9,... | collective-permute-start | bytes 208904 | tf_op jit(solution)/shard_map/ppermute | solution.py:148
  18.0 1.2 %copy.6 = bf16[1024,256]{0,1:T(8,128)(2,1)S(1)} copy(bf16[1024,256]{1,0:T(8,128)(2,1)} %param.7) | data formatting | bytes 1048576 | tf_op args[2]
  19.3 1.9 %collective-permute-start.1 = (bf16[256,1024]{1,0:T(8,128)(2,1)S(1)}, bf16[256,1024]{1,0:T(8,128)(2,1)S(1)}, u32[]{:S(2)}, u32[]{:S(2)}) collective-permute-start(bf16[256,1024]{1,0:T(8,128)(2,1)S(1)} %bitcast.9), channel_id=1, source_target_pairs={{0,1},{1,0},{2,3},{3,2},{4,5},{5,4},{6,7},{7,6},{8,9},{9,8},{10,11... | collective-permute-start | bytes 1572872 | tf_op jit(solution)/shard_map/ppermute | solution.py:157
  21.2 2.4 %collective-permute-start = (bf16[1024,256]{1,0:T(8,128)(2,1)S(1)}, bf16[1024,256]{1,0:T(8,128)(2,1)S(1)}, u32[]{:S(2)}, u32[]{:S(2)}) collective-permute-start(bf16[1024,256]{1,0:T(8,128)(2,1)S(1)} %copy-done), channel_id=1, source_target_pairs={{0,1},{1,0},{2,3},{3,2},{4,5},{5,4},{6,7},{7,6},{8,9},{9,8},{10,11... | collective-permute-start | bytes 1572872 | tf_op jit(solution)/shard_map/ppermute | solution.py:156
  23.6 5.5 %collective-permute-done.3 = bf16[136,256]{1,0:T(8,128)(2,1)S(1)} collective-permute-done((bf16[136,256]{1,0:T(8,128)(2,1)S(1)}, bf16[136,256]{1,0:T(8,128)(2,1)S(1)}, u32[]{:S(2)}, u32[]{:S(2)}) %collective-permute-start.3) | collective-permute-done | bytes 69664 | tf_op jit(solution)/shard_map/ppermute | solution.py:148
  29.2 1.9 %collective-permute-start.8 = (bf16[3,136,256]{2,1,0:T(8,128)(2,1)S(1)}, bf16[3,136,256]{2,1,0:T(8,128)(2,1)S(1)}, u32[]{:S(2)}, u32[]{:S(2)}) collective-permute-start(bf16[3,136,256]{2,1,0:T(8,128)(2,1)S(1)} %pad_maximum_fusion.refs_5_), channel_id=1, source_target_pairs={{0,2},{1,31},{2,4},{3,1},{4,6},{5,3},{6,8},{7,5},{8,10},{9,7},{10,... | collective-permute-start | bytes 626696 | tf_op jit(solution)/shard_map/ppermute | solution.py:148
  31.1 4.6 %collective-permute-start.6 = (bf16[1,136,256]{2,1,0:T(8,128)(2,1)S(1)}, bf16[1,136,256]{2,1,0:T(8,128)(2,1)S(1)}, u32[]{:S(2)}, u32[]{:S(2)}) collective-permute-start(bf16[1,136,256]{2,1,0:T(8,128)(2,1)S(1)} %bitcast.12), channel_id=1, source_target_pairs={{0,26},{1,7},{2,28},{3,9},{4,30},{5,11},{6,0},{7,13},{8,2},{9,15},... | collective-permute-start | bytes 208904 | tf_op jit(solution)/shard_map/ppermute | solution.py:148
  35.7 2.5 %collective-permute-start.7 = (bf16[3,136,256]{2,1,0:T(8,128)(2,1)S(1)}, bf16[3,136,256]{2,1,0:T(8,128)(2,1)S(1)}, u32[]{:S(2)}, u32[]{:S(2)}) collective-permute-start(bf16[3,136,256]{2,1,0:T(8,128)(2,1)S(1)} %pad_maximum_fusion.refs_5_), channel_id=1, source_target_pairs={{0,30},{1,3},{2,0},{3,5},{4,2},{5,7},{6,4},{7,9},{8,6},{9,11},{10,... | collective-permute-start | bytes 626696 | tf_op jit(solution)/shard_map/ppermute | solution.py:148
  38.2 2.5 %collective-permute-done.6.refs_2_ = bf16[1,136,256]{2,1,0:T(8,128)(2,1)S(1)} collective-permute-done((bf16[1,136,256]{2,1,0:T(8,128)(2,1)S(1)}, bf16[1,136,256]{2,1,0:T(8,128)(2,1)S(1)}, u32[]{:S(2)}, u32[]{:S(2)}) %collective-permute-start.6) | collective-permute-done | bytes 69664 | tf_op jit(solution)/shard_map/ppermute | solution.py:148
  40.7 2.3 %collective-permute-start.5 = (bf16[3,136,256]{2,1,0:T(8,128)(2,1)S(1)}, bf16[3,136,256]{2,1,0:T(8,128)(2,1)S(1)}, u32[]{:S(2)}, u32[]{:S(2)}) collective-permute-start(bf16[3,136,256]{2,1,0:T(8,128)(2,1)S(1)} %pad_maximum_fusion.refs_5_), channel_id=1, source_target_pairs={{0,4},{1,29},{2,6},{3,31},{4,8},{5,1},{6,10},{7,3},{8,12},{9,5},{1... | collective-permute-start | bytes 626696 | tf_op jit(solution)/shard_map/ppermute | solution.py:148
  43.1 5.6 %collective-permute-start.4 = (bf16[3,136,256]{2,1,0:T(8,128)(2,1)S(1)}, bf16[3,136,256]{2,1,0:T(8,128)(2,1)S(1)}, u32[]{:S(2)}, u32[]{:S(2)}) collective-permute-start(bf16[3,136,256]{2,1,0:T(8,128)(2,1)S(1)} %pad_maximum_fusion.refs_5_), channel_id=1, source_target_pairs={{0,28},{1,5},{2,30},{3,7},{4,0},{5,9},{6,2},{7,11},{8,4},{9,13},{1... | collective-permute-start | bytes 626696 | tf_op jit(solution)/shard_map/ppermute | solution.py:148
  48.8 7.6 %collective-permute-done.5.refs_1_ = bf16[3,136,256]{2,1,0:T(8,128)(2,1)S(1)} collective-permute-done((bf16[3,136,256]{2,1,0:T(8,128)(2,1)S(1)}, bf16[3,136,256]{2,1,0:T(8,128)(2,1)S(1)}, u32[]{:S(2)}, u32[]{:S(2)}) %collective-permute-start.5) | collective-permute-done | bytes 208928 | tf_op jit(solution)/shard_map/ppermute | solution.py:148
  56.4 6.1 %shard_map.55 = (bf16[3,272,128]{2,1,0:T(8,128)(2,1)S(1)}, bf16[3,272,128]{2,1,0:T(8,128)(2,1)S(1)}, bf16[1,272,128]{2,1,0:T(8,128)(2,1)S(1)}, bf16[3,272,128]{2...) custom-call(s32[2]{0:T(128)S(1)} %add_multiply_fusion.first_ref, ...), custom_call_target="tpu_custom_call" | custom-call | tf_op jit(solution)/shard_map/pallas_call | solution.py:81
  62.5 2.9 %collective-permute-start.9 = (bf16[3,272,128]{2,1,0:T(8,128)(2,1)S(1)}, bf16[3,272,128]{2,1,0:T(8,128)(2,1)S(1)}, u32[]{:S(2)}, u32[]{:S(2)}) collective-permute-start(bf16[3,272,128]{2,1,0:T(8,128)(2,1)S(1)} %get-tuple-element.12), channel_id=1, source_target_pairs={{0,4},{1,29},{2,6},{3,31},{4,8},{5,1},{6,10},{7,3},{8,12},{9,5},{1... | collective-permute-start | bytes 626696 | tf_op jit(solution)/shard_map/ppermute | solution.py:148
  65.5 5.0 %collective-permute-start.10 = (bf16[3,272,128]{2,1,0:T(8,128)(2,1)S(1)}, bf16[3,272,128]{2,1,0:T(8,128)(2,1)S(1)}, u32[]{:S(2)}, u32[]{:S(2)}) collective-permute-start(bf16[3,272,128]{2,1,0:T(8,128)(2,1)S(1)} %get-tuple-element.13), channel_id=1, source_target_pairs={{0,28},{1,5},{2,30},{3,7},{4,0},{5,9},{6,2},{7,11},{8,4},{9,13},{1... | collective-permute-start | bytes 626696 | tf_op jit(solution)/shard_map/ppermute | solution.py:148
  70.5 2.2 %collective-permute-start.11 = (bf16[3,272,128]{2,1,0:T(8,128)(2,1)S(1)}, bf16[3,272,128]{2,1,0:T(8,128)(2,1)S(1)}, u32[]{:S(2)}, u32[]{:S(2)}) collective-permute-start(bf16[3,272,128]{2,1,0:T(8,128)(2,1)S(1)} %get-tuple-element.14), channel_id=1, source_target_pairs={{0,2},{1,31},{2,4},{3,1},{4,6},{5,3},{6,8},{7,5},{8,10},{9,7},{10,... | collective-permute-start | bytes 626696 | tf_op jit(solution)/shard_map/ppermute | solution.py:148
  72.7 4.9 %collective-permute-start.12 = (bf16[3,272,128]{2,1,0:T(8,128)(2,1)S(1)}, bf16[3,272,128]{2,1,0:T(8,128)(2,1)S(1)}, u32[]{:S(2)}, u32[]{:S(2)}) collective-permute-start(bf16[3,272,128]{2,1,0:T(8,128)(2,1)S(1)} %get-tuple-element.15), channel_id=1, source_target_pairs={{0,30},{1,3},{2,0},{3,5},{4,2},{5,7},{6,4},{7,9},{8,6},{9,11},{10,... | collective-permute-start | bytes 626696 | tf_op jit(solution)/shard_map/ppermute | solution.py:148
  77.6 1.9 %collective-permute-start.13 = (bf16[1,272,128]{2,1,0:T(8,128)(2,1)S(1)}, bf16[1,272,128]{2,1,0:T(8,128)(2,1)S(1)}, u32[]{:S(2)}, u32[]{:S(2)}) collective-permute-start(bf16[1,272,128]{2,1,0:T(8,128)(2,1)S(1)} %get-tuple-element.16), channel_id=1, source_target_pairs={{0,6},{1,27},{2,8},{3,29},{4,10},{5,31},{6,12},{7,1},{8,14},{9,3},... | collective-permute-start | bytes 208904 | tf_op jit(solution)/shard_map/ppermute | solution.py:148
  79.5 3.2 %collective-permute-done.11.refs_3_ = bf16[3,272,128]{2,1,0:T(8,128)(2,1)S(1)} collective-permute-done((bf16[3,272,128]{2,1,0:T(8,128)(2,1)S(1)}, bf16[3,272,128]{2,1,0:T(8,128)(2,1)S(1)}, u32[]{:S(2)}, u32[]{:S(2)}) %collective-permute-start.11) | collective-permute-done | bytes 208928 | tf_op jit(solution)/shard_map/ppermute | solution.py:148
  83.6 5.3 %collective-permute-start.15 = (bf16[272,128]{1,0:T(8,128)(2,1)S(1)}, bf16[272,128]{1,0:T(8,128)(2,1)S(1)}, u32[]{:S(2)}, u32[]{:S(2)}) collective-permute-start(bf16[272,128]{1,0:T(8,128)(2,1)S(1)} %shard_map.57), channel_id=1, source_target_pairs={{0,22},{1,11},{2,24},{3,13},{4,26},{5,15},{6,28},{7,17},{8,30},{9,... | collective-permute-start | bytes 208904 | tf_op jit(solution)/shard_map/ppermute | solution.py:148
  89.0 5.4 %collective-permute-start.14 = (bf16[272,128]{1,0:T(8,128)(2,1)S(1)}, bf16[272,128]{1,0:T(8,128)(2,1)S(1)}, u32[]{:S(2)}, u32[]{:S(2)}) collective-permute-start(bf16[272,128]{1,0:T(8,128)(2,1)S(1)} %shard_map.56), channel_id=1, source_target_pairs={{0,10},{1,23},{2,12},{3,25},{4,14},{5,27},{6,16},{7,29},{8,18},{9,... | collective-permute-start | bytes 208904 | tf_op jit(solution)/shard_map/ppermute | solution.py:148
  94.4 1.3 %collective-permute-done.15.refs_6_ = bf16[272,128]{1,0:T(8,128)(2,1)S(1)} collective-permute-done((bf16[272,128]{1,0:T(8,128)(2,1)S(1)}, bf16[272,128]{1,0:T(8,128)(2,1)S(1)}, u32[]{:S(2)}, u32[]{:S(2)}) %collective-permute-start.15) | collective-permute-done | bytes 69664 | tf_op jit(solution)/shard_map/ppermute | solution.py:148
  95.6 6.4 %collective-permute-done.14.refs_5_ = bf16[272,128]{1,0:T(8,128)(2,1)S(1)} collective-permute-done((bf16[272,128]{1,0:T(8,128)(2,1)S(1)}, bf16[272,128]{1,0:T(8,128)(2,1)S(1)}, u32[]{:S(2)}, u32[]{:S(2)}) %collective-permute-start.14) | collective-permute-done | bytes 69664 | tf_op jit(solution)/shard_map/ppermute | solution.py:148
  (19 shorter events, 3.5 us)
Async XLA Ops:
  1.6 19.7 %copy-start = (bf16[1024,256]{1,0:T(8,128)(2,1)S(1)}, bf16[1024,256]{1,0:T(8,128)(2,1)}, u32[]{:S(2)}) copy-start(bf16[1024,256]{1,0:T(8,128)(2,1)} %k0_ref.1) | copy-start | bytes 1572868
  1.6 22.1 %collective-permute-start.2 = (bf16[136,256]{1,0:T(8,128)(2,1)S(1)}, bf16[136,256]{1,0:T(8,128)(2,1)S(1)}, u32[]{:S(2)}, u32[]{:S(2)}) collective-permute-start(bf16[136,256]{1,0:T(8,128)(2,1)S(1)} %get-tuple-element.18), channel_id=1, source_target_pairs={{0,22},{1,11},{2,24},{3,13},{4,26},{5,15},{6,28},{7,17},{8,30},{9,... | collective-permute-start | bytes 208904 | tf_op jit(solution)/shard_map/ppermute | solution.py:148
  16.1 13.1 %collective-permute-start.3 = (bf16[136,256]{1,0:T(8,128)(2,1)S(1)}, bf16[136,256]{1,0:T(8,128)(2,1)S(1)}, u32[]{:S(2)}, u32[]{:S(2)}) collective-permute-start(bf16[136,256]{1,0:T(8,128)(2,1)S(1)} %get-tuple-element.18), channel_id=1, source_target_pairs={{0,10},{1,23},{2,12},{3,25},{4,14},{5,27},{6,16},{7,29},{8,18},{9,... | collective-permute-start | bytes 208904 | tf_op jit(solution)/shard_map/ppermute | solution.py:148
  19.3 37.1 %collective-permute-start.1 = (bf16[256,1024]{1,0:T(8,128)(2,1)S(1)}, bf16[256,1024]{1,0:T(8,128)(2,1)S(1)}, u32[]{:S(2)}, u32[]{:S(2)}) collective-permute-start(bf16[256,1024]{1,0:T(8,128)(2,1)S(1)} %bitcast.9), channel_id=1, source_target_pairs={{0,1},{1,0},{2,3},{3,2},{4,5},{5,4},{6,7},{7,6},{8,9},{9,8},{10,11... | collective-permute-start | bytes 1572872 | tf_op jit(solution)/shard_map/ppermute | solution.py:157
  21.2 35.2 %collective-permute-start = (bf16[1024,256]{1,0:T(8,128)(2,1)S(1)}, bf16[1024,256]{1,0:T(8,128)(2,1)S(1)}, u32[]{:S(2)}, u32[]{:S(2)}) collective-permute-start(bf16[1024,256]{1,0:T(8,128)(2,1)S(1)} %copy-done), channel_id=1, source_target_pairs={{0,1},{1,0},{2,3},{3,2},{4,5},{5,4},{6,7},{7,6},{8,9},{9,8},{10,11... | collective-permute-start | bytes 1572872 | tf_op jit(solution)/shard_map/ppermute | solution.py:156
  29.2 13.9 %collective-permute-start.8 = (bf16[3,136,256]{2,1,0:T(8,128)(2,1)S(1)}, bf16[3,136,256]{2,1,0:T(8,128)(2,1)S(1)}, u32[]{:S(2)}, u32[]{:S(2)}) collective-permute-start(bf16[3,136,256]{2,1,0:T(8,128)(2,1)S(1)} %pad_maximum_fusion.refs_5_), channel_id=1, source_target_pairs={{0,2},{1,31},{2,4},{3,1},{4,6},{5,3},{6,8},{7,5},{8,10},{9,7},{10,... | collective-permute-start | bytes 626696 | tf_op jit(solution)/shard_map/ppermute | solution.py:148
  31.1 9.6 %collective-permute-start.6 = (bf16[1,136,256]{2,1,0:T(8,128)(2,1)S(1)}, bf16[1,136,256]{2,1,0:T(8,128)(2,1)S(1)}, u32[]{:S(2)}, u32[]{:S(2)}) collective-permute-start(bf16[1,136,256]{2,1,0:T(8,128)(2,1)S(1)} %bitcast.12), channel_id=1, source_target_pairs={{0,26},{1,7},{2,28},{3,9},{4,30},{5,11},{6,0},{7,13},{8,2},{9,15},... | collective-permute-start | bytes 208904 | tf_op jit(solution)/shard_map/ppermute | solution.py:148
  35.7 13.1 %collective-permute-start.7 = (bf16[3,136,256]{2,1,0:T(8,128)(2,1)S(1)}, bf16[3,136,256]{2,1,0:T(8,128)(2,1)S(1)}, u32[]{:S(2)}, u32[]{:S(2)}) collective-permute-start(bf16[3,136,256]{2,1,0:T(8,128)(2,1)S(1)} %pad_maximum_fusion.refs_5_), channel_id=1, source_target_pairs={{0,30},{1,3},{2,0},{3,5},{4,2},{5,7},{6,4},{7,9},{8,6},{9,11},{10,... | collective-permute-start | bytes 626696 | tf_op jit(solution)/shard_map/ppermute | solution.py:148
  40.7 15.7 %collective-permute-start.5 = (bf16[3,136,256]{2,1,0:T(8,128)(2,1)S(1)}, bf16[3,136,256]{2,1,0:T(8,128)(2,1)S(1)}, u32[]{:S(2)}, u32[]{:S(2)}) collective-permute-start(bf16[3,136,256]{2,1,0:T(8,128)(2,1)S(1)} %pad_maximum_fusion.refs_5_), channel_id=1, source_target_pairs={{0,4},{1,29},{2,6},{3,31},{4,8},{5,1},{6,10},{7,3},{8,12},{9,5},{1... | collective-permute-start | bytes 626696 | tf_op jit(solution)/shard_map/ppermute | solution.py:148
  43.1 13.3 %collective-permute-start.4 = (bf16[3,136,256]{2,1,0:T(8,128)(2,1)S(1)}, bf16[3,136,256]{2,1,0:T(8,128)(2,1)S(1)}, u32[]{:S(2)}, u32[]{:S(2)}) collective-permute-start(bf16[3,136,256]{2,1,0:T(8,128)(2,1)S(1)} %pad_maximum_fusion.refs_5_), channel_id=1, source_target_pairs={{0,28},{1,5},{2,30},{3,7},{4,0},{5,9},{6,2},{7,11},{8,4},{9,13},{1... | collective-permute-start | bytes 626696 | tf_op jit(solution)/shard_map/ppermute | solution.py:148
  62.5 17.0 %collective-permute-start.9 = (bf16[3,272,128]{2,1,0:T(8,128)(2,1)S(1)}, bf16[3,272,128]{2,1,0:T(8,128)(2,1)S(1)}, u32[]{:S(2)}, u32[]{:S(2)}) collective-permute-start(bf16[3,272,128]{2,1,0:T(8,128)(2,1)S(1)} %get-tuple-element.12), channel_id=1, source_target_pairs={{0,4},{1,29},{2,6},{3,31},{4,8},{5,1},{6,10},{7,3},{8,12},{9,5},{1... | collective-permute-start | bytes 626696 | tf_op jit(solution)/shard_map/ppermute | solution.py:148
  65.5 14.0 %collective-permute-start.10 = (bf16[3,272,128]{2,1,0:T(8,128)(2,1)S(1)}, bf16[3,272,128]{2,1,0:T(8,128)(2,1)S(1)}, u32[]{:S(2)}, u32[]{:S(2)}) collective-permute-start(bf16[3,272,128]{2,1,0:T(8,128)(2,1)S(1)} %get-tuple-element.13), channel_id=1, source_target_pairs={{0,28},{1,5},{2,30},{3,7},{4,0},{5,9},{6,2},{7,11},{8,4},{9,13},{1... | collective-permute-start | bytes 626696 | tf_op jit(solution)/shard_map/ppermute | solution.py:148
  70.5 12.2 %collective-permute-start.11 = (bf16[3,272,128]{2,1,0:T(8,128)(2,1)S(1)}, bf16[3,272,128]{2,1,0:T(8,128)(2,1)S(1)}, u32[]{:S(2)}, u32[]{:S(2)}) collective-permute-start(bf16[3,272,128]{2,1,0:T(8,128)(2,1)S(1)} %get-tuple-element.14), channel_id=1, source_target_pairs={{0,2},{1,31},{2,4},{3,1},{4,6},{5,3},{6,8},{7,5},{8,10},{9,7},{10,... | collective-permute-start | bytes 626696 | tf_op jit(solution)/shard_map/ppermute | solution.py:148
  72.7 10.7 %collective-permute-start.12 = (bf16[3,272,128]{2,1,0:T(8,128)(2,1)S(1)}, bf16[3,272,128]{2,1,0:T(8,128)(2,1)S(1)}, u32[]{:S(2)}, u32[]{:S(2)}) collective-permute-start(bf16[3,272,128]{2,1,0:T(8,128)(2,1)S(1)} %get-tuple-element.15), channel_id=1, source_target_pairs={{0,30},{1,3},{2,0},{3,5},{4,2},{5,7},{6,4},{7,9},{8,6},{9,11},{10,... | collective-permute-start | bytes 626696 | tf_op jit(solution)/shard_map/ppermute | solution.py:148
  77.6 11.3 %collective-permute-start.13 = (bf16[1,272,128]{2,1,0:T(8,128)(2,1)S(1)}, bf16[1,272,128]{2,1,0:T(8,128)(2,1)S(1)}, u32[]{:S(2)}, u32[]{:S(2)}) collective-permute-start(bf16[1,272,128]{2,1,0:T(8,128)(2,1)S(1)} %get-tuple-element.16), channel_id=1, source_target_pairs={{0,6},{1,27},{2,8},{3,29},{4,10},{5,31},{6,12},{7,1},{8,14},{9,3},... | collective-permute-start | bytes 208904 | tf_op jit(solution)/shard_map/ppermute | solution.py:148
  83.6 12.1 %collective-permute-start.15 = (bf16[272,128]{1,0:T(8,128)(2,1)S(1)}, bf16[272,128]{1,0:T(8,128)(2,1)S(1)}, u32[]{:S(2)}, u32[]{:S(2)}) collective-permute-start(bf16[272,128]{1,0:T(8,128)(2,1)S(1)} %shard_map.57), channel_id=1, source_target_pairs={{0,22},{1,11},{2,24},{3,13},{4,26},{5,15},{6,28},{7,17},{8,30},{9,... | collective-permute-start | bytes 208904 | tf_op jit(solution)/shard_map/ppermute | solution.py:148
  89.0 13.1 %collective-permute-start.14 = (bf16[272,128]{1,0:T(8,128)(2,1)S(1)}, bf16[272,128]{1,0:T(8,128)(2,1)S(1)}, u32[]{:S(2)}, u32[]{:S(2)}) collective-permute-start(bf16[272,128]{1,0:T(8,128)(2,1)S(1)} %shard_map.56), channel_id=1, source_target_pairs={{0,10},{1,23},{2,12},{3,25},{4,14},{5,27},{6,16},{7,29},{8,18},{9,... | collective-permute-start | bytes 208904 | tf_op jit(solution)/shard_map/ppermute | solution.py:148

commit v13 on v12

--- a/solution.py
+++ b/solution.py
@@ -164,9 +164,10 @@
     eight = shift(up5[None], -3)
     up1, down1 = shift(own, -1), shift(own, 1)
 
-    part_up2, part_down2, part_eight, part_up1, part_down1, part_own = attend(
-        first, (up2, down2, eight, up1, down1, own), keys, vts, cand
+    part_up2, part_down2, part_eight, part_up1, part_down1 = attend(
+        first, (up2, down2, eight, up1, down1), keys, vts, cand
     )
+    (part_own,) = attend(first, (own,), keys, vts, cand)
     back = [shift(part_up2, 2), shift(part_down2, -2), shift(part_up1, 1), shift(part_down1, -1)]
     extra = shift(part_eight, 3)
     parts = [part_own] + back

time: 104 us -> 103 us (level)
  waiting for transfers between devices: 27.3 us -> 25.2 us
  Pallas kernels: 7.17 us -> 9.26 us
    ppermute x14, waiting for transfers between devices: 27.3 us -> 25.1 us  [shift(): return lax.ppermute(x, ('z', 'core'), pairs)]
    pallas_call x1 -> x2, Pallas kernels: 6.1 us -> 8.2 us  [attend(): pl.pallas_call(functools.partial(attend_kernel, counts), in_specs=[SMEM]...]
  transfers between devices with their start and end apart: 16 -> 16, of which waited for: 7 -> 7; matrix products, arithmetic and copies ran while one was open for 1% -> 1% of each run, Pallas kernels for 0% -> 3%
where the time goes in v13:
time: 103 us
  starting transfers between devices  65.3 us (63%)
  waiting for transfers between devices  25.2 us (24%)
  Pallas kernels  9.26 us (9%)
  other arithmetic  1.66 us (2%)
  local copies, waits for them, and re-layouts  1.25 us (1%)
    ppermute x14, starting transfers between devices, shift(): return lax.ppermute(x, ('z', 'core'), pairs)  60.9 us
    ppermute x14, waiting for transfers between devices, shift(): return lax.ppermute(x, ('z', 'core'), pairs)  25.1 us
    pallas_call x2, Pallas kernels, attend(): pl.pallas_call(functools.partial(attend_kernel, counts), in_specs=[SMEM]...  8.2 us
    ppermute x1, starting transfers between devices, body(): keys = (hist_keys, lax.ppermute(hist_keys, 'core', swap))  2.41 us
  transfers between devices with their start and end apart: 16, of which 7 were waited for; matrix products, arithmetic and copies ran while one was open for 1% of the time, Pallas kernels for 3%

profile of v13, /device:TPU:6, one launch (start us, length us, event | category | flops | bytes accessed | tf_op | source)
XLA Modules:
  0.0 102.8 jit_solution(908768198117244952)
XLA Ops:
  1.6 14.5 %collective-permute-start.2 = (bf16[136,256]{1,0:T(8,128)(2,1)S(1)}, bf16[136,256]{1,0:T(8,128)(2,1)S(1)}, u32[]{:S(2)}, u32[]{:S(2)}) collective-permute-start(bf16[136,256]{1,0:T(8,128)(2,1)S(1)} %get-tuple-element.16), channel_id=1, source_target_pairs={{0,22},{1,11},{2,24},{3,13},{4,26},{5,15},{6,28},{7,17},{8,30},{9,... | collective-permute-start | bytes 208904 | tf_op jit(solution)/shard_map/ppermute | solution.py:148
  16.1 1.9 %collective-permute-start.3 = (bf16[136,256]{1,0:T(8,128)(2,1)S(1)}, bf16[136,256]{1,0:T(8,128)(2,1)S(1)}, u32[]{:S(2)}, u32[]{:S(2)}) collective-permute-start(bf16[136,256]{1,0:T(8,128)(2,1)S(1)} %get-tuple-element.16), channel_id=1, source_target_pairs={{0,10},{1,23},{2,12},{3,25},{4,14},{5,27},{6,16},{7,29},{8,18},{9,... | collective-permute-start | bytes 208904 | tf_op jit(solution)/shard_map/ppermute | solution.py:148
  18.0 1.2 %copy.6 = bf16[1024,256]{0,1:T(8,128)(2,1)S(1)} copy(bf16[1024,256]{1,0:T(8,128)(2,1)} %param.7) | data formatting | bytes 1048576 | tf_op args[2]
  19.3 1.9 %collective-permute-start.1 = (bf16[256,1024]{1,0:T(8,128)(2,1)S(1)}, bf16[256,1024]{1,0:T(8,128)(2,1)S(1)}, u32[]{:S(2)}, u32[]{:S(2)}) collective-permute-start(bf16[256,1024]{1,0:T(8,128)(2,1)S(1)} %bitcast.9), channel_id=1, source_target_pairs={{0,1},{1,0},{2,3},{3,2},{4,5},{5,4},{6,7},{7,6},{8,9},{9,8},{10,11... | collective-permute-start | bytes 1572872 | tf_op jit(solution)/shard_map/ppermute | solution.py:157
  21.2 2.4 %collective-permute-start = (bf16[1024,256]{1,0:T(8,128)(2,1)S(1)}, bf16[1024,256]{1,0:T(8,128)(2,1)S(1)}, u32[]{:S(2)}, u32[]{:S(2)}) collective-permute-start(bf16[1024,256]{1,0:T(8,128)(2,1)S(1)} %copy-done), channel_id=1, source_target_pairs={{0,1},{1,0},{2,3},{3,2},{4,5},{5,4},{6,7},{7,6},{8,9},{9,8},{10,11... | collective-permute-start | bytes 1572872 | tf_op jit(solution)/shard_map/ppermute | solution.py:156
  23.6 5.5 %collective-permute-done.3 = bf16[136,256]{1,0:T(8,128)(2,1)S(1)} collective-permute-done((bf16[136,256]{1,0:T(8,128)(2,1)S(1)}, bf16[136,256]{1,0:T(8,128)(2,1)S(1)}, u32[]{:S(2)}, u32[]{:S(2)}) %collective-permute-start.3) | collective-permute-done | bytes 69664 | tf_op jit(solution)/shard_map/ppermute | solution.py:148
  29.2 1.9 %collective-permute-start.8 = (bf16[3,136,256]{2,1,0:T(8,128)(2,1)S(1)}, bf16[3,136,256]{2,1,0:T(8,128)(2,1)S(1)}, u32[]{:S(2)}, u32[]{:S(2)}) collective-permute-start(bf16[3,136,256]{2,1,0:T(8,128)(2,1)S(1)} %pad_maximum_fusion.refs_0_), channel_id=1, source_target_pairs={{0,2},{1,31},{2,4},{3,1},{4,6},{5,3},{6,8},{7,5},{8,10},{9,7},{10,... | collective-permute-start | bytes 626696 | tf_op jit(solution)/shard_map/ppermute | solution.py:148
  31.1 4.6 %collective-permute-start.6 = (bf16[1,136,256]{2,1,0:T(8,128)(2,1)S(1)}, bf16[1,136,256]{2,1,0:T(8,128)(2,1)S(1)}, u32[]{:S(2)}, u32[]{:S(2)}) collective-permute-start(bf16[1,136,256]{2,1,0:T(8,128)(2,1)S(1)} %bitcast.13), channel_id=1, source_target_pairs={{0,26},{1,7},{2,28},{3,9},{4,30},{5,11},{6,0},{7,13},{8,2},{9,15},... | collective-permute-start | bytes 208904 | tf_op jit(solution)/shard_map/ppermute | solution.py:148
  35.7 2.5 %collective-permute-start.7 = (bf16[3,136,256]{2,1,0:T(8,128)(2,1)S(1)}, bf16[3,136,256]{2,1,0:T(8,128)(2,1)S(1)}, u32[]{:S(2)}, u32[]{:S(2)}) collective-permute-start(bf16[3,136,256]{2,1,0:T(8,128)(2,1)S(1)} %pad_maximum_fusion.refs_0_), channel_id=1, source_target_pairs={{0,30},{1,3},{2,0},{3,5},{4,2},{5,7},{6,4},{7,9},{8,6},{9,11},{10,... | collective-permute-start | bytes 626696 | tf_op jit(solution)/shard_map/ppermute | solution.py:148
  38.2 2.5 %collective-permute-done.6.refs_2_ = bf16[1,136,256]{2,1,0:T(8,128)(2,1)S(1)} collective-permute-done((bf16[1,136,256]{2,1,0:T(8,128)(2,1)S(1)}, bf16[1,136,256]{2,1,0:T(8,128)(2,1)S(1)}, u32[]{:S(2)}, u32[]{:S(2)}) %collective-permute-start.6) | collective-permute-done | bytes 69664 | tf_op jit(solution)/shard_map/ppermute | solution.py:148
  40.7 2.3 %collective-permute-start.5 = (bf16[3,136,256]{2,1,0:T(8,128)(2,1)S(1)}, bf16[3,136,256]{2,1,0:T(8,128)(2,1)S(1)}, u32[]{:S(2)}, u32[]{:S(2)}) collective-permute-start(bf16[3,136,256]{2,1,0:T(8,128)(2,1)S(1)} %pad_maximum_fusion.refs_0_), channel_id=1, source_target_pairs={{0,4},{1,29},{2,6},{3,31},{4,8},{5,1},{6,10},{7,3},{8,12},{9,5},{1... | collective-permute-start | bytes 626696 | tf_op jit(solution)/shard_map/ppermute | solution.py:148
  43.1 5.6 %collective-permute-start.4 = (bf16[3,136,256]{2,1,0:T(8,128)(2,1)S(1)}, bf16[3,136,256]{2,1,0:T(8,128)(2,1)S(1)}, u32[]{:S(2)}, u32[]{:S(2)}) collective-permute-start(bf16[3,136,256]{2,1,0:T(8,128)(2,1)S(1)} %pad_maximum_fusion.refs_0_), channel_id=1, source_target_pairs={{0,28},{1,5},{2,30},{3,7},{4,0},{5,9},{6,2},{7,11},{8,4},{9,13},{1... | collective-permute-start | bytes 626696 | tf_op jit(solution)/shard_map/ppermute | solution.py:148
  48.8 7.6 %collective-permute-done.5.refs_1_ = bf16[3,136,256]{2,1,0:T(8,128)(2,1)S(1)} collective-permute-done((bf16[3,136,256]{2,1,0:T(8,128)(2,1)S(1)}, bf16[3,136,256]{2,1,0:T(8,128)(2,1)S(1)}, u32[]{:S(2)}, u32[]{:S(2)}) %collective-permute-start.5) | collective-permute-done | bytes 208928 | tf_op jit(solution)/shard_map/ppermute | solution.py:148
  56.4 5.5 %shard_map.56 = (bf16[3,272,128]{2,1,0:T(8,128)(2,1)S(1)}, bf16[3,272,128]{2,1,0:T(8,128)(2,1)S(1)}, bf16[1,272,128]{2,1,0:T(8,128)(2,1)S(1)}, bf16[3,272,128]{2,1,0:T(8,128)(2,1)S(1)}, bf16[3,272,128]{2,1,0:T(8,128)(2,1)S(1)}) custom-call(s32[2]{0:T(128)S(1)} %add_multiply_fusion.first_ref, bf16[1024,256]{1,0:T(8,128)(2,1)S(1)} %copy-done, ...), custom_call_target="tpu_custom_call" | custom-call | tf_op jit(solution)/shard_map/pallas_call | solution.py:81
  61.9 2.9 %collective-permute-start.9 = (bf16[3,272,128]{2,1,0:T(8,128)(2,1)S(1)}, bf16[3,272,128]{2,1,0:T(8,128)(2,1)S(1)}, u32[]{:S(2)}, u32[]{:S(2)}) collective-permute-start(bf16[3,272,128]{2,1,0:T(8,128)(2,1)S(1)} %get-tuple-element.10), channel_id=1, source_target_pairs={{0,4},{1,29},{2,6},{3,31},{4,8},{5,1},{6,10},{7,3},{8,12},{9,5},{1... | collective-permute-start | bytes 626696 | tf_op jit(solution)/shard_map/ppermute | solution.py:148
  64.8 5.0 %collective-permute-start.10 = (bf16[3,272,128]{2,1,0:T(8,128)(2,1)S(1)}, bf16[3,272,128]{2,1,0:T(8,128)(2,1)S(1)}, u32[]{:S(2)}, u32[]{:S(2)}) collective-permute-start(bf16[3,272,128]{2,1,0:T(8,128)(2,1)S(1)} %get-tuple-element.11), channel_id=1, source_target_pairs={{0,28},{1,5},{2,30},{3,7},{4,0},{5,9},{6,2},{7,11},{8,4},{9,13},{1... | collective-permute-start | bytes 626696 | tf_op jit(solution)/shard_map/ppermute | solution.py:148
  69.9 2.2 %collective-permute-start.11 = (bf16[3,272,128]{2,1,0:T(8,128)(2,1)S(1)}, bf16[3,272,128]{2,1,0:T(8,128)(2,1)S(1)}, u32[]{:S(2)}, u32[]{:S(2)}) collective-permute-start(bf16[3,272,128]{2,1,0:T(8,128)(2,1)S(1)} %get-tuple-element.12), channel_id=1, source_target_pairs={{0,2},{1,31},{2,4},{3,1},{4,6},{5,3},{6,8},{7,5},{8,10},{9,7},{10,... | collective-permute-start | bytes 626696 | tf_op jit(solution)/shard_map/ppermute | solution.py:148
  72.1 4.8 %collective-permute-start.12 = (bf16[3,272,128]{2,1,0:T(8,128)(2,1)S(1)}, bf16[3,272,128]{2,1,0:T(8,128)(2,1)S(1)}, u32[]{:S(2)}, u32[]{:S(2)}) collective-permute-start(bf16[3,272,128]{2,1,0:T(8,128)(2,1)S(1)} %get-tuple-element.13), channel_id=1, source_target_pairs={{0,30},{1,3},{2,0},{3,5},{4,2},{5,7},{6,4},{7,9},{8,6},{9,11},{10,... | collective-permute-start | bytes 626696 | tf_op jit(solution)/shard_map/ppermute | solution.py:148
  76.9 1.9 %collective-permute-start.13 = (bf16[1,272,128]{2,1,0:T(8,128)(2,1)S(1)}, bf16[1,272,128]{2,1,0:T(8,128)(2,1)S(1)}, u32[]{:S(2)}, u32[]{:S(2)}) collective-permute-start(bf16[1,272,128]{2,1,0:T(8,128)(2,1)S(1)} %get-tuple-element.14), channel_id=1, source_target_pairs={{0,6},{1,27},{2,8},{3,29},{4,10},{5,31},{6,12},{7,1},{8,14},{9,3},... | collective-permute-start | bytes 208904 | tf_op jit(solution)/shard_map/ppermute | solution.py:148
  78.9 2.7 %shard_map.55.refs_0_ = bf16[3,272,128]{2,1,0:T(8,128)(2,1)S(1)} custom-call(s32[2]{0:T(128)S(1)} %add_multiply_fusion.first_ref, bf16[1024,256]{1,0:T(8,128)(2,1)S(1)} %copy-done, bf16[1024,256]{1,0:T(8,128)(2,1)S(1)} %collective-permute-done.k1_ref, bf16[256,1024]{1,0:T(8,128)(2,1)S(1)} %bitcast.11, bf16[256,1024]{1,0:T(8,128)(2,1)S(1)} %collective-permute-done.1.v1_ref, ...), custom_call_target="tpu_custom_call" | custom-call | tf_op jit(solution)/shard_map/pallas_call | solution.py:81
  82.9 5.3 %collective-permute-start.15 = (bf16[272,128]{1,0:T(8,128)(2,1)S(1)}, bf16[272,128]{1,0:T(8,128)(2,1)S(1)}, u32[]{:S(2)}, u32[]{:S(2)}) collective-permute-start(bf16[272,128]{1,0:T(8,128)(2,1)S(1)} %shard_map.58), channel_id=1, source_target_pairs={{0,22},{1,11},{2,24},{3,13},{4,26},{5,15},{6,28},{7,17},{8,30},{9,... | collective-permute-start | bytes 208904 | tf_op jit(solution)/shard_map/ppermute | solution.py:148
  88.3 5.4 %collective-permute-start.14 = (bf16[272,128]{1,0:T(8,128)(2,1)S(1)}, bf16[272,128]{1,0:T(8,128)(2,1)S(1)}, u32[]{:S(2)}, u32[]{:S(2)}) collective-permute-start(bf16[272,128]{1,0:T(8,128)(2,1)S(1)} %shard_map.57), channel_id=1, source_target_pairs={{0,10},{1,23},{2,12},{3,25},{4,14},{5,27},{6,16},{7,29},{8,18},{9,... | collective-permute-start | bytes 208904 | tf_op jit(solution)/shard_map/ppermute | solution.py:148
  93.8 0.9 collective-permute-done.15.refs_6_
  94.6 7.4 %collective-permute-done.14.refs_5_ = bf16[272,128]{1,0:T(8,128)(2,1)S(1)} collective-permute-done((bf16[272,128]{1,0:T(8,128)(2,1)S(1)}, bf16[272,128]{1,0:T(8,128)(2,1)S(1)}, u32[]{:S(2)}, u32[]{:S(2)}) %collective-permute-start.14) | collective-permute-done | bytes 69664 | tf_op jit(solution)/shard_map/ppermute | solution.py:148
  (20 shorter events, 4.0 us)
Async XLA Ops:
  1.6 19.7 %copy-start = (bf16[1024,256]{1,0:T(8,128)(2,1)S(1)}, bf16[1024,256]{1,0:T(8,128)(2,1)}, u32[]{:S(2)}) copy-start(bf16[1024,256]{1,0:T(8,128)(2,1)} %k0_ref.3) | copy-start | bytes 1572868
  1.6 22.1 %collective-permute-start.2 = (bf16[136,256]{1,0:T(8,128)(2,1)S(1)}, bf16[136,256]{1,0:T(8,128)(2,1)S(1)}, u32[]{:S(2)}, u32[]{:S(2)}) collective-permute-start(bf16[136,256]{1,0:T(8,128)(2,1)S(1)} %get-tuple-element.16), channel_id=1, source_target_pairs={{0,22},{1,11},{2,24},{3,13},{4,26},{5,15},{6,28},{7,17},{8,30},{9,... | collective-permute-start | bytes 208904 | tf_op jit(solution)/shard_map/ppermute | solution.py:148
  16.1 13.1 %collective-permute-start.3 = (bf16[136,256]{1,0:T(8,128)(2,1)S(1)}, bf16[136,256]{1,0:T(8,128)(2,1)S(1)}, u32[]{:S(2)}, u32[]{:S(2)}) collective-permute-start(bf16[136,256]{1,0:T(8,128)(2,1)S(1)} %get-tuple-element.16), channel_id=1, source_target_pairs={{0,10},{1,23},{2,12},{3,25},{4,14},{5,27},{6,16},{7,29},{8,18},{9,... | collective-permute-start | bytes 208904 | tf_op jit(solution)/shard_map/ppermute | solution.py:148
  19.3 37.1 %collective-permute-start.1 = (bf16[256,1024]{1,0:T(8,128)(2,1)S(1)}, bf16[256,1024]{1,0:T(8,128)(2,1)S(1)}, u32[]{:S(2)}, u32[]{:S(2)}) collective-permute-start(bf16[256,1024]{1,0:T(8,128)(2,1)S(1)} %bitcast.9), channel_id=1, source_target_pairs={{0,1},{1,0},{2,3},{3,2},{4,5},{5,4},{6,7},{7,6},{8,9},{9,8},{10,11... | collective-permute-start | bytes 1572872 | tf_op jit(solution)/shard_map/ppermute | solution.py:157
  21.2 35.2 %collective-permute-start = (bf16[1024,256]{1,0:T(8,128)(2,1)S(1)}, bf16[1024,256]{1,0:T(8,128)(2,1)S(1)}, u32[]{:S(2)}, u32[]{:S(2)}) collective-permute-start(bf16[1024,256]{1,0:T(8,128)(2,1)S(1)} %copy-done), channel_id=1, source_target_pairs={{0,1},{1,0},{2,3},{3,2},{4,5},{5,4},{6,7},{7,6},{8,9},{9,8},{10,11... | collective-permute-start | bytes 1572872 | tf_op jit(solution)/shard_map/ppermute | solution.py:156
  29.2 13.9 %collective-permute-start.8 = (bf16[3,136,256]{2,1,0:T(8,128)(2,1)S(1)}, bf16[3,136,256]{2,1,0:T(8,128)(2,1)S(1)}, u32[]{:S(2)}, u32[]{:S(2)}) collective-permute-start(bf16[3,136,256]{2,1,0:T(8,128)(2,1)S(1)} %pad_maximum_fusion.refs_0_), channel_id=1, source_target_pairs={{0,2},{1,31},{2,4},{3,1},{4,6},{5,3},{6,8},{7,5},{8,10},{9,7},{10,... | collective-permute-start | bytes 626696 | tf_op jit(solution)/shard_map/ppermute | solution.py:148
  31.1 9.6 %collective-permute-start.6 = (bf16[1,136,256]{2,1,0:T(8,128)(2,1)S(1)}, bf16[1,136,256]{2,1,0:T(8,128)(2,1)S(1)}, u32[]{:S(2)}, u32[]{:S(2)}) collective-permute-start(bf16[1,136,256]{2,1,0:T(8,128)(2,1)S(1)} %bitcast.13), channel_id=1, source_target_pairs={{0,26},{1,7},{2,28},{3,9},{4,30},{5,11},{6,0},{7,13},{8,2},{9,15},... | collective-permute-start | bytes 208904 | tf_op jit(solution)/shard_map/ppermute | solution.py:148
  35.7 13.1 %collective-permute-start.7 = (bf16[3,136,256]{2,1,0:T(8,128)(2,1)S(1)}, bf16[3,136,256]{2,1,0:T(8,128)(2,1)S(1)}, u32[]{:S(2)}, u32[]{:S(2)}) collective-permute-start(bf16[3,136,256]{2,1,0:T(8,128)(2,1)S(1)} %pad_maximum_fusion.refs_0_), channel_id=1, source_target_pairs={{0,30},{1,3},{2,0},{3,5},{4,2},{5,7},{6,4},{7,9},{8,6},{9,11},{10,... | collective-permute-start | bytes 626696 | tf_op jit(solution)/shard_map/ppermute | solution.py:148
  40.7 15.7 %collective-permute-start.5 = (bf16[3,136,256]{2,1,0:T(8,128)(2,1)S(1)}, bf16[3,136,256]{2,1,0:T(8,128)(2,1)S(1)}, u32[]{:S(2)}, u32[]{:S(2)}) collective-permute-start(bf16[3,136,256]{2,1,0:T(8,128)(2,1)S(1)} %pad_maximum_fusion.refs_0_), channel_id=1, source_target_pairs={{0,4},{1,29},{2,6},{3,31},{4,8},{5,1},{6,10},{7,3},{8,12},{9,5},{1... | collective-permute-start | bytes 626696 | tf_op jit(solution)/shard_map/ppermute | solution.py:148
  43.1 13.3 %collective-permute-start.4 = (bf16[3,136,256]{2,1,0:T(8,128)(2,1)S(1)}, bf16[3,136,256]{2,1,0:T(8,128)(2,1)S(1)}, u32[]{:S(2)}, u32[]{:S(2)}) collective-permute-start(bf16[3,136,256]{2,1,0:T(8,128)(2,1)S(1)} %pad_maximum_fusion.refs_0_), channel_id=1, source_target_pairs={{0,28},{1,5},{2,30},{3,7},{4,0},{5,9},{6,2},{7,11},{8,4},{9,13},{1... | collective-permute-start | bytes 626696 | tf_op jit(solution)/shard_map/ppermute | solution.py:148
  61.9 19.7 %collective-permute-start.9 = (bf16[3,272,128]{2,1,0:T(8,128)(2,1)S(1)}, bf16[3,272,128]{2,1,0:T(8,128)(2,1)S(1)}, u32[]{:S(2)}, u32[]{:S(2)}) collective-permute-start(bf16[3,272,128]{2,1,0:T(8,128)(2,1)S(1)} %get-tuple-element.10), channel_id=1, source_target_pairs={{0,4},{1,29},{2,6},{3,31},{4,8},{5,1},{6,10},{7,3},{8,12},{9,5},{1... | collective-permute-start | bytes 626696 | tf_op jit(solution)/shard_map/ppermute | solution.py:148
  64.8 16.8 %collective-permute-start.10 = (bf16[3,272,128]{2,1,0:T(8,128)(2,1)S(1)}, bf16[3,272,128]{2,1,0:T(8,128)(2,1)S(1)}, u32[]{:S(2)}, u32[]{:S(2)}) collective-permute-start(bf16[3,272,128]{2,1,0:T(8,128)(2,1)S(1)} %get-tuple-element.11), channel_id=1, source_target_pairs={{0,28},{1,5},{2,30},{3,7},{4,0},{5,9},{6,2},{7,11},{8,4},{9,13},{1... | collective-permute-start | bytes 626696 | tf_op jit(solution)/shard_map/ppermute | solution.py:148
  69.9 12.2 %collective-permute-start.11 = (bf16[3,272,128]{2,1,0:T(8,128)(2,1)S(1)}, bf16[3,272,128]{2,1,0:T(8,128)(2,1)S(1)}, u32[]{:S(2)}, u32[]{:S(2)}) collective-permute-start(bf16[3,272,128]{2,1,0:T(8,128)(2,1)S(1)} %get-tuple-element.12), channel_id=1, source_target_pairs={{0,2},{1,31},{2,4},{3,1},{4,6},{5,3},{6,8},{7,5},{8,10},{9,7},{10,... | collective-permute-start | bytes 626696 | tf_op jit(solution)/shard_map/ppermute | solution.py:148
  72.1 10.7 %collective-permute-start.12 = (bf16[3,272,128]{2,1,0:T(8,128)(2,1)S(1)}, bf16[3,272,128]{2,1,0:T(8,128)(2,1)S(1)}, u32[]{:S(2)}, u32[]{:S(2)}) collective-permute-start(bf16[3,272,128]{2,1,0:T(8,128)(2,1)S(1)} %get-tuple-element.13), channel_id=1, source_target_pairs={{0,30},{1,3},{2,0},{3,5},{4,2},{5,7},{6,4},{7,9},{8,6},{9,11},{10,... | collective-permute-start | bytes 626696 | tf_op jit(solution)/shard_map/ppermute | solution.py:148
  76.9 11.3 %collective-permute-start.13 = (bf16[1,272,128]{2,1,0:T(8,128)(2,1)S(1)}, bf16[1,272,128]{2,1,0:T(8,128)(2,1)S(1)}, u32[]{:S(2)}, u32[]{:S(2)}) collective-permute-start(bf16[1,272,128]{2,1,0:T(8,128)(2,1)S(1)} %get-tuple-element.14), channel_id=1, source_target_pairs={{0,6},{1,27},{2,8},{3,29},{4,10},{5,31},{6,12},{7,1},{8,14},{9,3},... | collective-permute-start | bytes 208904 | tf_op jit(solution)/shard_map/ppermute | solution.py:148
  82.9 11.7 %collective-permute-start.15 = (bf16[272,128]{1,0:T(8,128)(2,1)S(1)}, bf16[272,128]{1,0:T(8,128)(2,1)S(1)}, u32[]{:S(2)}, u32[]{:S(2)}) collective-permute-start(bf16[272,128]{1,0:T(8,128)(2,1)S(1)} %shard_map.58), channel_id=1, source_target_pairs={{0,22},{1,11},{2,24},{3,13},{4,26},{5,15},{6,28},{7,17},{8,30},{9,... | collective-permute-start | bytes 208904 | tf_op jit(solution)/shard_map/ppermute | solution.py:148
  88.3 13.6 %collective-permute-start.14 = (bf16[272,128]{1,0:T(8,128)(2,1)S(1)}, bf16[272,128]{1,0:T(8,128)(2,1)S(1)}, u32[]{:S(2)}, u32[]{:S(2)}) collective-permute-start(bf16[272,128]{1,0:T(8,128)(2,1)S(1)} %shard_map.57), channel_id=1, source_target_pairs={{0,10},{1,23},{2,12},{3,25},{4,14},{5,27},{6,16},{7,29},{8,18},{9,... | collective-permute-start | bytes 208904 | tf_op jit(solution)/shard_map/ppermute | solution.py:148
